TPU v7x, 512 devices: a whole 4x8x8 slice. The times are simulated.
512 devices in a mesh: dp: 4 (over x), seq: 32 (over z_hi, y, core), tensor: 4 (over z_lo).
Axes of the slice: x: 4, y: 8, z: 8 (z_hi: 2, z_lo: 4; z = z_hi * 4 + z_lo), core: 2. Of those that a mesh axis runs over, the one named last changes fastest.
Arguments:
- query_rows: bfloat16 [16384, 3072], P(('dp', 'seq'), 'tensor'), parts along dimension 0, may hold values from -17 to 17
- key_rows: bfloat16 [16384, 3072], P(('dp', 'seq'), 'tensor'), parts along dimension 0, may hold values from -17 to 17
- value_rows: bfloat16 [16384, 3072], P(('dp', 'seq'), 'tensor'), parts along dimension 0, may hold values from -6 to 6
- deal_owner: int32 [16384], P(('dp', 'seq')), parts along dimension 0, may hold values from 0 to 31, as said below
- deal_slot: int32 [16384], P(('dp', 'seq')), parts along dimension 0, may hold values from 0 to 127
- clip_lengths: int32 [32], P('dp'), parts along dimension 0, may hold values from 1 to 1536, 4096 in all
- clip_steps: int32 [32], P('dp'), parts along dimension 0, may hold values from 0 to 999
- gate_table: bfloat16 [1000, 3072], P(None, 'tensor'), may hold values from -4 to 4
Outputs:
- attention_out: bfloat16 [16384, 3072], P(('dp', 'seq'), 'tensor'), parts along dimension 0
There are 4 independent parts, one for each index of `dp`. A program takes and returns all parts, laid end to end along the dimension named above; an argument that names none is the same for every part. Nothing has to cross between parts.
Inputs may be any that keep to these rules, and one draw needn't show every extreme that they name: The pairs (deal_owner, deal_slot) are all distinct, so every owner receives exactly 128 rows; the rows of one device bound for one owner number at most 6, and that bound is reached in every draw.
All inputs are finite; a program needn't handle non-finite values.
Results may differ from a plain program's by a relative error of at most 0.0085.
Values may be sent and summed in bfloat16 or wider, within the bound.
No kernel may reach another device: no remote copies, remote signals or barrier semaphores. Data moves between devices by JAX's collectives and lax.ppermute only.
A program may use at most 64 MiB of HBM per device.

v0:
```python
import math

import jax
import jax.numpy as jnp
from jax import lax
from jax.sharding import PartitionSpec as P

HEAD_DIM = 128


masked_score = -1e30


def shifted(value, axis, by):
    devices = lax.axis_size(axis)
    return lax.ppermute(value, axis, [(i, (i + by) % devices) for i in range(devices)])


def attend(carry_state, query_heads, own_clip, key_block, key_clip):
    same_clip = own_clip[:, None] == key_clip[None, :]
    old_max, old_sum, old_numerator = carry_state
    block_rows = key_block.shape[1]
    key_heads = key_block[0].reshape(block_rows, old_max.shape[0], HEAD_DIM)
    value_heads = key_block[1].reshape(block_rows, old_max.shape[0], HEAD_DIM)
    scores = jnp.einsum(
        "qhd,khd->hqk", query_heads, key_heads, preferred_element_type=jnp.float32
    ) * (1.0 / math.sqrt(HEAD_DIM))
    allowed = same_clip[None, :, :]
    new_max = jnp.maximum(old_max, jnp.max(jnp.where(allowed, scores, masked_score), axis=2))
    rescale = jnp.exp(old_max - new_max)
    weights = jnp.where(allowed, jnp.exp(scores - new_max[:, :, None]), 0.0)
    new_sum = old_sum * rescale + jnp.sum(weights, axis=2)
    added = jnp.einsum(
        "hqk,khd->qhd",
        weights.astype(jnp.bfloat16),
        value_heads,
        preferred_element_type=jnp.float32,
    )
    new_numerator = old_numerator * rescale.T[:, :, None] + added
    return (new_max, new_sum, new_numerator)


def shards(
    query_rows, key_rows, value_rows, deal_owner, deal_slot, clip_lengths, clip_steps, gate_table
):
    devices = lax.axis_size("seq")
    row_count = query_rows.shape[0]
    row_width = query_rows.shape[1]
    head_count = row_width // HEAD_DIM
    capacity = 3 * row_count // (2 * devices)
    my_index = lax.axis_index("seq")
    owner_ids = jnp.arange(devices, dtype=jnp.int32)
    chosen = (deal_owner[:, None] == owner_ids[None, :]).astype(jnp.int32)
    earlier = jnp.cumsum(chosen, axis=0) - chosen
    target = deal_owner * capacity + jnp.sum(earlier * chosen, axis=1)

    def pack_rows(source):
        buffer = jnp.zeros((devices * capacity, row_width), source.dtype).at[target].set(source)
        return buffer.reshape(devices, capacity, row_width)

    slot_buffer = (
        jnp.full((devices * capacity,), -1, jnp.int32)
        .at[target]
        .set(deal_slot)
        .reshape(devices, capacity)
    )
    slot_arrived = lax.all_to_all(
        slot_buffer, "seq", split_axis=0, concat_axis=0, tiled=True
    ).reshape(-1)
    landing = jnp.where(slot_arrived >= 0, slot_arrived, row_count)

    def unpack_rows(buffer):
        flat_rows = buffer.reshape(devices * capacity, row_width)
        return (
            jnp.zeros((row_count, row_width), buffer.dtype).at[landing].set(flat_rows, mode="drop")
        )

    clip_ends = jnp.cumsum(clip_lengths)

    def clip_index(positions):
        return jnp.sum((clip_ends[None, :] <= positions[:, None]).astype(jnp.int32), axis=1)

    local_rows = jnp.arange(row_count, dtype=jnp.int32)
    own_clip = clip_index(my_index * row_count + local_rows)
    start_state = (
        jnp.full((head_count, row_count), masked_score, jnp.float32),
        jnp.zeros((head_count, row_count), jnp.float32),
        jnp.zeros((row_count, head_count, HEAD_DIM), jnp.float32),
    )
    arrived = (
        lax.all_to_all(pack_rows(query_rows), "seq", split_axis=0, concat_axis=0, tiled=True),
        lax.all_to_all(pack_rows(key_rows), "seq", split_axis=0, concat_axis=0, tiled=True),
        lax.all_to_all(pack_rows(value_rows), "seq", split_axis=0, concat_axis=0, tiled=True),
    )
    dealt_query = unpack_rows(arrived[0])
    query_heads = dealt_query.reshape(row_count, head_count, HEAD_DIM)
    key_value = jnp.stack([unpack_rows(arrived[1]), unpack_rows(arrived[2])])
    state = attend(start_state, query_heads, own_clip, key_value, own_clip)

    def loop_step(step_index, carry):
        held_block, inner = carry
        held_block = shifted(held_block, "seq", 1)
        anchor = (my_index - step_index) % devices
        block_clip = clip_index(anchor * row_count + local_rows)
        return (held_block, attend(inner, query_heads, own_clip, held_block, block_clip))

    state = lax.fori_loop(1, devices, loop_step, (key_value, state))[1]
    running_max, running_sum, numerator = state
    attended = (numerator / running_sum.T[:, :, None]).reshape(row_count, row_width)
    clip_slots = jnp.arange(clip_steps.shape[0], dtype=jnp.int32)
    step_of_row = jnp.sum(
        jnp.where(own_clip[:, None] == clip_slots[None, :], clip_steps[None, :], 0), axis=1
    )
    step_onehot = (
        step_of_row[:, None] == jnp.arange(gate_table.shape[0], dtype=jnp.int32)[None, :]
    ).astype(jnp.bfloat16)
    gate_rows = jnp.dot(step_onehot, gate_table, preferred_element_type=jnp.float32)
    return (attended * gate_rows).astype(jnp.bfloat16)


def solution(mesh):
    placed = (
        P(("dp", "seq"), "tensor"),
        P(("dp", "seq"), "tensor"),
        P(("dp", "seq"), "tensor"),
        P(("dp", "seq")),
        P(("dp", "seq")),
        P("dp"),
        P("dp"),
        P(None, "tensor"),
    )
    return jax.shard_map(
        shards, mesh=mesh, in_specs=placed, out_specs=P(("dp", "seq"), "tensor"), check_vma=False
    )
```

profile of v0, /device:TPU:454, one launch (start us, length us, event | category | flops | bytes accessed | tf_op | source)
XLA Modules:
  0.0 708.5 jit_solution(11713875567845068100)
XLA Ops:
  97.3 609.7 %while.22 = (s32[]{:T(128)}, bf16[2,128,768]{1,2,0:T(8,128)(2,1)S(1)}, f32[6,128]{1,0:T(8,128)S(1)}, f32[6,128]{1,0:T(8,128)S(1)}, f32[128,6,128]{2,0,1:T(8,128)...) while((s32[]{:T(128)}, ...), condition=%wide.region_17.18_spmd.clone, body=%wide.region_13.17_spmd.clone.sunk | while | flops 51434768 | bytes 5819222 | solution.py:107
  156.2 17.2 %collective-permute-done = bf16[2,128,768]{1,2,0:T(8,128)(2,1)S(1)} collective-permute-done((bf16[2,128,768]{1,2,0:T(8,128)(2,1)S(1)}, bf16[2,128,768]{1,2,0:T(8,128)(2,1)S(1)}, u32[]{:S(2)}, u32[]{:S(2)}) %collective-permute-start) | collective-permute-done | bytes 393248 | tf_op jit(solution)/shard_map/while/body/eval_jaxpr/ppermute | solution.py:16
  176.4 17.2 %collective-permute-done = bf16[2,128,768]{1,2,0:T(8,128)(2,1)S(1)} collective-permute-done((bf16[2,128,768]{1,2,0:T(8,128)(2,1)S(1)}, bf16[2,128,768]{1,2,0:T(8,128)(2,1)S(1)}, u32[]{:S(2)}, u32[]{:S(2)}) %collective-permute-start) | collective-permute-done | bytes 393248 | tf_op jit(solution)/shard_map/while/body/eval_jaxpr/ppermute | solution.py:16
  196.6 17.2 %collective-permute-done = bf16[2,128,768]{1,2,0:T(8,128)(2,1)S(1)} collective-permute-done((bf16[2,128,768]{1,2,0:T(8,128)(2,1)S(1)}, bf16[2,128,768]{1,2,0:T(8,128)(2,1)S(1)}, u32[]{:S(2)}, u32[]{:S(2)}) %collective-permute-start) | collective-permute-done | bytes 393248 | tf_op jit(solution)/shard_map/while/body/eval_jaxpr/ppermute | solution.py:16
  216.7 16.7 %collective-permute-done = bf16[2,128,768]{1,2,0:T(8,128)(2,1)S(1)} collective-permute-done((bf16[2,128,768]{1,2,0:T(8,128)(2,1)S(1)}, bf16[2,128,768]{1,2,0:T(8,128)(2,1)S(1)}, u32[]{:S(2)}, u32[]{:S(2)}) %collective-permute-start) | collective-permute-done | bytes 393248 | tf_op jit(solution)/shard_map/while/body/eval_jaxpr/ppermute | solution.py:16
  293.6 16.9 %collective-permute-done = bf16[2,128,768]{1,2,0:T(8,128)(2,1)S(1)} collective-permute-done((bf16[2,128,768]{1,2,0:T(8,128)(2,1)S(1)}, bf16[2,128,768]{1,2,0:T(8,128)(2,1)S(1)}, u32[]{:S(2)}, u32[]{:S(2)}) %collective-permute-start) | collective-permute-done | bytes 393248 | tf_op jit(solution)/shard_map/while/body/eval_jaxpr/ppermute | solution.py:16
  313.5 17.2 %collective-permute-done = bf16[2,128,768]{1,2,0:T(8,128)(2,1)S(1)} collective-permute-done((bf16[2,128,768]{1,2,0:T(8,128)(2,1)S(1)}, bf16[2,128,768]{1,2,0:T(8,128)(2,1)S(1)}, u32[]{:S(2)}, u32[]{:S(2)}) %collective-permute-start) | collective-permute-done | bytes 393248 | tf_op jit(solution)/shard_map/while/body/eval_jaxpr/ppermute | solution.py:16
  333.7 16.8 %collective-permute-done = bf16[2,128,768]{1,2,0:T(8,128)(2,1)S(1)} collective-permute-done((bf16[2,128,768]{1,2,0:T(8,128)(2,1)S(1)}, bf16[2,128,768]{1,2,0:T(8,128)(2,1)S(1)}, u32[]{:S(2)}, u32[]{:S(2)}) %collective-permute-start) | collective-permute-done | bytes 393248 | tf_op jit(solution)/shard_map/while/body/eval_jaxpr/ppermute | solution.py:16
  353.5 16.8 %collective-permute-done = bf16[2,128,768]{1,2,0:T(8,128)(2,1)S(1)} collective-permute-done((bf16[2,128,768]{1,2,0:T(8,128)(2,1)S(1)}, bf16[2,128,768]{1,2,0:T(8,128)(2,1)S(1)}, u32[]{:S(2)}, u32[]{:S(2)}) %collective-permute-start) | collective-permute-done | bytes 393248 | tf_op jit(solution)/shard_map/while/body/eval_jaxpr/ppermute | solution.py:16
  373.2 16.6 %collective-permute-done = bf16[2,128,768]{1,2,0:T(8,128)(2,1)S(1)} collective-permute-done((bf16[2,128,768]{1,2,0:T(8,128)(2,1)S(1)}, bf16[2,128,768]{1,2,0:T(8,128)(2,1)S(1)}, u32[]{:S(2)}, u32[]{:S(2)}) %collective-permute-start) | collective-permute-done | bytes 393248 | tf_op jit(solution)/shard_map/while/body/eval_jaxpr/ppermute | solution.py:16
  392.8 16.5 %collective-permute-done = bf16[2,128,768]{1,2,0:T(8,128)(2,1)S(1)} collective-permute-done((bf16[2,128,768]{1,2,0:T(8,128)(2,1)S(1)}, bf16[2,128,768]{1,2,0:T(8,128)(2,1)S(1)}, u32[]{:S(2)}, u32[]{:S(2)}) %collective-permute-start) | collective-permute-done | bytes 393248 | tf_op jit(solution)/shard_map/while/body/eval_jaxpr/ppermute | solution.py:16
  431.7 16.5 %collective-permute-done = bf16[2,128,768]{1,2,0:T(8,128)(2,1)S(1)} collective-permute-done((bf16[2,128,768]{1,2,0:T(8,128)(2,1)S(1)}, bf16[2,128,768]{1,2,0:T(8,128)(2,1)S(1)}, u32[]{:S(2)}, u32[]{:S(2)}) %collective-permute-start) | collective-permute-done | bytes 393248 | tf_op jit(solution)/shard_map/while/body/eval_jaxpr/ppermute | solution.py:16
  451.2 17.0 %collective-permute-done = bf16[2,128,768]{1,2,0:T(8,128)(2,1)S(1)} collective-permute-done((bf16[2,128,768]{1,2,0:T(8,128)(2,1)S(1)}, bf16[2,128,768]{1,2,0:T(8,128)(2,1)S(1)}, u32[]{:S(2)}, u32[]{:S(2)}) %collective-permute-start) | collective-permute-done | bytes 393248 | tf_op jit(solution)/shard_map/while/body/eval_jaxpr/ppermute | solution.py:16
  471.1 17.2 %collective-permute-done = bf16[2,128,768]{1,2,0:T(8,128)(2,1)S(1)} collective-permute-done((bf16[2,128,768]{1,2,0:T(8,128)(2,1)S(1)}, bf16[2,128,768]{1,2,0:T(8,128)(2,1)S(1)}, u32[]{:S(2)}, u32[]{:S(2)}) %collective-permute-start) | collective-permute-done | bytes 393248 | tf_op jit(solution)/shard_map/while/body/eval_jaxpr/ppermute | solution.py:16
  491.3 17.1 %collective-permute-done = bf16[2,128,768]{1,2,0:T(8,128)(2,1)S(1)} collective-permute-done((bf16[2,128,768]{1,2,0:T(8,128)(2,1)S(1)}, bf16[2,128,768]{1,2,0:T(8,128)(2,1)S(1)}, u32[]{:S(2)}, u32[]{:S(2)}) %collective-permute-start) | collective-permute-done | bytes 393248 | tf_op jit(solution)/shard_map/while/body/eval_jaxpr/ppermute | solution.py:16
  511.4 16.4 %collective-permute-done = bf16[2,128,768]{1,2,0:T(8,128)(2,1)S(1)} collective-permute-done((bf16[2,128,768]{1,2,0:T(8,128)(2,1)S(1)}, bf16[2,128,768]{1,2,0:T(8,128)(2,1)S(1)}, u32[]{:S(2)}, u32[]{:S(2)}) %collective-permute-start) | collective-permute-done | bytes 393248 | tf_op jit(solution)/shard_map/while/body/eval_jaxpr/ppermute | solution.py:16
  530.8 16.8 %collective-permute-done = bf16[2,128,768]{1,2,0:T(8,128)(2,1)S(1)} collective-permute-done((bf16[2,128,768]{1,2,0:T(8,128)(2,1)S(1)}, bf16[2,128,768]{1,2,0:T(8,128)(2,1)S(1)}, u32[]{:S(2)}, u32[]{:S(2)}) %collective-permute-start) | collective-permute-done | bytes 393248 | tf_op jit(solution)/shard_map/while/body/eval_jaxpr/ppermute | solution.py:16
  550.6 16.8 %collective-permute-done = bf16[2,128,768]{1,2,0:T(8,128)(2,1)S(1)} collective-permute-done((bf16[2,128,768]{1,2,0:T(8,128)(2,1)S(1)}, bf16[2,128,768]{1,2,0:T(8,128)(2,1)S(1)}, u32[]{:S(2)}, u32[]{:S(2)}) %collective-permute-start) | collective-permute-done | bytes 393248 | tf_op jit(solution)/shard_map/while/body/eval_jaxpr/ppermute | solution.py:16
  570.4 17.4 %collective-permute-done = bf16[2,128,768]{1,2,0:T(8,128)(2,1)S(1)} collective-permute-done((bf16[2,128,768]{1,2,0:T(8,128)(2,1)S(1)}, bf16[2,128,768]{1,2,0:T(8,128)(2,1)S(1)}, u32[]{:S(2)}, u32[]{:S(2)}) %collective-permute-start) | collective-permute-done | bytes 393248 | tf_op jit(solution)/shard_map/while/body/eval_jaxpr/ppermute | solution.py:16
  590.8 17.9 %collective-permute-done = bf16[2,128,768]{1,2,0:T(8,128)(2,1)S(1)} collective-permute-done((bf16[2,128,768]{1,2,0:T(8,128)(2,1)S(1)}, bf16[2,128,768]{1,2,0:T(8,128)(2,1)S(1)}, u32[]{:S(2)}, u32[]{:S(2)}) %collective-permute-start) | collective-permute-done | bytes 393248 | tf_op jit(solution)/shard_map/while/body/eval_jaxpr/ppermute | solution.py:16
  611.7 17.7 %collective-permute-done = bf16[2,128,768]{1,2,0:T(8,128)(2,1)S(1)} collective-permute-done((bf16[2,128,768]{1,2,0:T(8,128)(2,1)S(1)}, bf16[2,128,768]{1,2,0:T(8,128)(2,1)S(1)}, u32[]{:S(2)}, u32[]{:S(2)}) %collective-permute-start) | collective-permute-done | bytes 393248 | tf_op jit(solution)/shard_map/while/body/eval_jaxpr/ppermute | solution.py:16
  632.4 17.7 %collective-permute-done = bf16[2,128,768]{1,2,0:T(8,128)(2,1)S(1)} collective-permute-done((bf16[2,128,768]{1,2,0:T(8,128)(2,1)S(1)}, bf16[2,128,768]{1,2,0:T(8,128)(2,1)S(1)}, u32[]{:S(2)}, u32[]{:S(2)}) %collective-permute-start) | collective-permute-done | bytes 393248 | tf_op jit(solution)/shard_map/while/body/eval_jaxpr/ppermute | solution.py:16
  653.0 17.3 %collective-permute-done = bf16[2,128,768]{1,2,0:T(8,128)(2,1)S(1)} collective-permute-done((bf16[2,128,768]{1,2,0:T(8,128)(2,1)S(1)}, bf16[2,128,768]{1,2,0:T(8,128)(2,1)S(1)}, u32[]{:S(2)}, u32[]{:S(2)}) %collective-permute-start) | collective-permute-done | bytes 393248 | tf_op jit(solution)/shard_map/while/body/eval_jaxpr/ppermute | solution.py:16
  673.3 16.9 %collective-permute-done = bf16[2,128,768]{1,2,0:T(8,128)(2,1)S(1)} collective-permute-done((bf16[2,128,768]{1,2,0:T(8,128)(2,1)S(1)}, bf16[2,128,768]{1,2,0:T(8,128)(2,1)S(1)}, u32[]{:S(2)}, u32[]{:S(2)}) %collective-permute-start) | collective-permute-done | bytes 393248 | tf_op jit(solution)/shard_map/while/body/eval_jaxpr/ppermute | solution.py:16
  (437 shorter events, 313.1 us)
Async XLA Ops:
  4.4 19.7 %all-to-all-start = ((s32[32,1,6]{2,1,0:T(1,128)}), s32[32,1,6]{2,1,0:T(1,128)S(1)}, u32[]{:S(2)}, u32[]{:S(2)}) async-start(s32[32,1,6]{2,1,0:T(1,128)} %bitcast), calls=%async_computation | async-start | bytes 32768 | tf_op jit(solution)/shard_map/all_to_all | solution.py:67
  24.1 23.5 %all-to-all-start.3 = ((bf16[32,6,768]{2,1,0:T(8,128)(2,1)}), bf16[32,6,768]{2,1,0:T(8,128)(2,1)S(1)}, u32[]{:S(2)}, u32[]{:S(2)}) async-start(bf16[32,6,768]{2,1,0:T(8,128)(2,1)} %reshape.165), calls=%async_computation.3 | async-start | bytes 786432 | tf_op jit(solution)/shard_map/all_to_all | solution.py:91
  47.6 23.7 %all-to-all-start.1 = ((bf16[32,6,768]{2,1,0:T(8,128)(2,1)}), bf16[32,6,768]{2,1,0:T(8,128)(2,1)S(1)}, u32[]{:S(2)}, u32[]{:S(2)}) async-start(bf16[32,6,768]{2,1,0:T(8,128)(2,1)} %reshape.159), calls=%async_computation.1 | async-start | bytes 786432 | tf_op jit(solution)/shard_map/all_to_all | solution.py:92
  71.3 23.7 %all-to-all-start.2 = ((bf16[32,6,768]{2,1,0:T(8,128)(2,1)}), bf16[32,6,768]{2,1,0:T(8,128)(2,1)S(1)}, u32[]{:S(2)}, u32[]{:S(2)}) async-start(bf16[32,6,768]{2,1,0:T(8,128)(2,1)} %reshape.161), calls=%async_computation.2 | async-start | bytes 786432 | tf_op jit(solution)/shard_map/all_to_all | solution.py:93
  154.1 19.3 %collective-permute-start = (bf16[2,128,768]{1,2,0:T(8,128)(2,1)S(1)}, bf16[2,128,768]{1,2,0:T(8,128)(2,1)S(1)}, u32[]{:S(2)}, u32[]{:S(2)}) collective-permute-start(bf16[2,128,768]{1,2,0:T(8,128)(2,1)S(1)} %get-tuple-element.426), channel_id=1, source_target_pairs={{0,4},{4,8},{8,12},{12,16},{16,20},{20,24},{24,28},{28,32},{32,36}... | collective-permute-start | bytes 1179656 | tf_op jit(solution)/shard_map/while/body/eval_jaxpr/ppermute | solution.py:16
  174.2 19.4 %collective-permute-start = (bf16[2,128,768]{1,2,0:T(8,128)(2,1)S(1)}, bf16[2,128,768]{1,2,0:T(8,128)(2,1)S(1)}, u32[]{:S(2)}, u32[]{:S(2)}) collective-permute-start(bf16[2,128,768]{1,2,0:T(8,128)(2,1)S(1)} %get-tuple-element.426), channel_id=1, source_target_pairs={{0,4},{4,8},{8,12},{12,16},{16,20},{20,24},{24,28},{28,32},{32,36}... | collective-permute-start | bytes 1179656 | tf_op jit(solution)/shard_map/while/body/eval_jaxpr/ppermute | solution.py:16
  194.4 19.3 %collective-permute-start = (bf16[2,128,768]{1,2,0:T(8,128)(2,1)S(1)}, bf16[2,128,768]{1,2,0:T(8,128)(2,1)S(1)}, u32[]{:S(2)}, u32[]{:S(2)}) collective-permute-start(bf16[2,128,768]{1,2,0:T(8,128)(2,1)S(1)} %get-tuple-element.426), channel_id=1, source_target_pairs={{0,4},{4,8},{8,12},{12,16},{16,20},{20,24},{24,28},{28,32},{32,36}... | collective-permute-start | bytes 1179656 | tf_op jit(solution)/shard_map/while/body/eval_jaxpr/ppermute | solution.py:16
  214.6 18.8 %collective-permute-start = (bf16[2,128,768]{1,2,0:T(8,128)(2,1)S(1)}, bf16[2,128,768]{1,2,0:T(8,128)(2,1)S(1)}, u32[]{:S(2)}, u32[]{:S(2)}) collective-permute-start(bf16[2,128,768]{1,2,0:T(8,128)(2,1)S(1)} %get-tuple-element.426), channel_id=1, source_target_pairs={{0,4},{4,8},{8,12},{12,16},{16,20},{20,24},{24,28},{28,32},{32,36}... | collective-permute-start | bytes 1179656 | tf_op jit(solution)/shard_map/while/body/eval_jaxpr/ppermute | solution.py:16
  291.4 19.1 %collective-permute-start = (bf16[2,128,768]{1,2,0:T(8,128)(2,1)S(1)}, bf16[2,128,768]{1,2,0:T(8,128)(2,1)S(1)}, u32[]{:S(2)}, u32[]{:S(2)}) collective-permute-start(bf16[2,128,768]{1,2,0:T(8,128)(2,1)S(1)} %get-tuple-element.426), channel_id=1, source_target_pairs={{0,4},{4,8},{8,12},{12,16},{16,20},{20,24},{24,28},{28,32},{32,36}... | collective-permute-start | bytes 1179656 | tf_op jit(solution)/shard_map/while/body/eval_jaxpr/ppermute | solution.py:16
  311.4 19.3 %collective-permute-start = (bf16[2,128,768]{1,2,0:T(8,128)(2,1)S(1)}, bf16[2,128,768]{1,2,0:T(8,128)(2,1)S(1)}, u32[]{:S(2)}, u32[]{:S(2)}) collective-permute-start(bf16[2,128,768]{1,2,0:T(8,128)(2,1)S(1)} %get-tuple-element.426), channel_id=1, source_target_pairs={{0,4},{4,8},{8,12},{12,16},{16,20},{20,24},{24,28},{28,32},{32,36}... | collective-permute-start | bytes 1179656 | tf_op jit(solution)/shard_map/while/body/eval_jaxpr/ppermute | solution.py:16
  331.5 19.0 %collective-permute-start = (bf16[2,128,768]{1,2,0:T(8,128)(2,1)S(1)}, bf16[2,128,768]{1,2,0:T(8,128)(2,1)S(1)}, u32[]{:S(2)}, u32[]{:S(2)}) collective-permute-start(bf16[2,128,768]{1,2,0:T(8,128)(2,1)S(1)} %get-tuple-element.426), channel_id=1, source_target_pairs={{0,4},{4,8},{8,12},{12,16},{16,20},{20,24},{24,28},{28,32},{32,36}... | collective-permute-start | bytes 1179656 | tf_op jit(solution)/shard_map/while/body/eval_jaxpr/ppermute | solution.py:16
  351.4 18.9 %collective-permute-start = (bf16[2,128,768]{1,2,0:T(8,128)(2,1)S(1)}, bf16[2,128,768]{1,2,0:T(8,128)(2,1)S(1)}, u32[]{:S(2)}, u32[]{:S(2)}) collective-permute-start(bf16[2,128,768]{1,2,0:T(8,128)(2,1)S(1)} %get-tuple-element.426), channel_id=1, source_target_pairs={{0,4},{4,8},{8,12},{12,16},{16,20},{20,24},{24,28},{28,32},{32,36}... | collective-permute-start | bytes 1179656 | tf_op jit(solution)/shard_map/while/body/eval_jaxpr/ppermute | solution.py:16
  371.1 18.8 %collective-permute-start = (bf16[2,128,768]{1,2,0:T(8,128)(2,1)S(1)}, bf16[2,128,768]{1,2,0:T(8,128)(2,1)S(1)}, u32[]{:S(2)}, u32[]{:S(2)}) collective-permute-start(bf16[2,128,768]{1,2,0:T(8,128)(2,1)S(1)} %get-tuple-element.426), channel_id=1, source_target_pairs={{0,4},{4,8},{8,12},{12,16},{16,20},{20,24},{24,28},{28,32},{32,36}... | collective-permute-start | bytes 1179656 | tf_op jit(solution)/shard_map/while/body/eval_jaxpr/ppermute | solution.py:16
  449.0 19.1 %collective-permute-start = (bf16[2,128,768]{1,2,0:T(8,128)(2,1)S(1)}, bf16[2,128,768]{1,2,0:T(8,128)(2,1)S(1)}, u32[]{:S(2)}, u32[]{:S(2)}) collective-permute-start(bf16[2,128,768]{1,2,0:T(8,128)(2,1)S(1)} %get-tuple-element.426), channel_id=1, source_target_pairs={{0,4},{4,8},{8,12},{12,16},{16,20},{20,24},{24,28},{28,32},{32,36}... | collective-permute-start | bytes 1179656 | tf_op jit(solution)/shard_map/while/body/eval_jaxpr/ppermute | solution.py:16
  469.0 19.3 %collective-permute-start = (bf16[2,128,768]{1,2,0:T(8,128)(2,1)S(1)}, bf16[2,128,768]{1,2,0:T(8,128)(2,1)S(1)}, u32[]{:S(2)}, u32[]{:S(2)}) collective-permute-start(bf16[2,128,768]{1,2,0:T(8,128)(2,1)S(1)} %get-tuple-element.426), channel_id=1, source_target_pairs={{0,4},{4,8},{8,12},{12,16},{16,20},{20,24},{24,28},{28,32},{32,36}... | collective-permute-start | bytes 1179656 | tf_op jit(solution)/shard_map/while/body/eval_jaxpr/ppermute | solution.py:16
  489.2 19.3 %collective-permute-start = (bf16[2,128,768]{1,2,0:T(8,128)(2,1)S(1)}, bf16[2,128,768]{1,2,0:T(8,128)(2,1)S(1)}, u32[]{:S(2)}, u32[]{:S(2)}) collective-permute-start(bf16[2,128,768]{1,2,0:T(8,128)(2,1)S(1)} %get-tuple-element.426), channel_id=1, source_target_pairs={{0,4},{4,8},{8,12},{12,16},{16,20},{20,24},{24,28},{28,32},{32,36}... | collective-permute-start | bytes 1179656 | tf_op jit(solution)/shard_map/while/body/eval_jaxpr/ppermute | solution.py:16
  528.7 18.9 %collective-permute-start = (bf16[2,128,768]{1,2,0:T(8,128)(2,1)S(1)}, bf16[2,128,768]{1,2,0:T(8,128)(2,1)S(1)}, u32[]{:S(2)}, u32[]{:S(2)}) collective-permute-start(bf16[2,128,768]{1,2,0:T(8,128)(2,1)S(1)} %get-tuple-element.426), channel_id=1, source_target_pairs={{0,4},{4,8},{8,12},{12,16},{16,20},{20,24},{24,28},{28,32},{32,36}... | collective-permute-start | bytes 1179656 | tf_op jit(solution)/shard_map/while/body/eval_jaxpr/ppermute | solution.py:16
  548.5 18.9 %collective-permute-start = (bf16[2,128,768]{1,2,0:T(8,128)(2,1)S(1)}, bf16[2,128,768]{1,2,0:T(8,128)(2,1)S(1)}, u32[]{:S(2)}, u32[]{:S(2)}) collective-permute-start(bf16[2,128,768]{1,2,0:T(8,128)(2,1)S(1)} %get-tuple-element.426), channel_id=1, source_target_pairs={{0,4},{4,8},{8,12},{12,16},{16,20},{20,24},{24,28},{28,32},{32,36}... | collective-permute-start | bytes 1179656 | tf_op jit(solution)/shard_map/while/body/eval_jaxpr/ppermute | solution.py:16
  568.3 19.6 %collective-permute-start = (bf16[2,128,768]{1,2,0:T(8,128)(2,1)S(1)}, bf16[2,128,768]{1,2,0:T(8,128)(2,1)S(1)}, u32[]{:S(2)}, u32[]{:S(2)}) collective-permute-start(bf16[2,128,768]{1,2,0:T(8,128)(2,1)S(1)} %get-tuple-element.426), channel_id=1, source_target_pairs={{0,4},{4,8},{8,12},{12,16},{16,20},{20,24},{24,28},{28,32},{32,36}... | collective-permute-start | bytes 1179656 | tf_op jit(solution)/shard_map/while/body/eval_jaxpr/ppermute | solution.py:16
  588.7 20.0 %collective-permute-start = (bf16[2,128,768]{1,2,0:T(8,128)(2,1)S(1)}, bf16[2,128,768]{1,2,0:T(8,128)(2,1)S(1)}, u32[]{:S(2)}, u32[]{:S(2)}) collective-permute-start(bf16[2,128,768]{1,2,0:T(8,128)(2,1)S(1)} %get-tuple-element.426), channel_id=1, source_target_pairs={{0,4},{4,8},{8,12},{12,16},{16,20},{20,24},{24,28},{28,32},{32,36}... | collective-permute-start | bytes 1179656 | tf_op jit(solution)/shard_map/while/body/eval_jaxpr/ppermute | solution.py:16
  609.5 19.9 %collective-permute-start = (bf16[2,128,768]{1,2,0:T(8,128)(2,1)S(1)}, bf16[2,128,768]{1,2,0:T(8,128)(2,1)S(1)}, u32[]{:S(2)}, u32[]{:S(2)}) collective-permute-start(bf16[2,128,768]{1,2,0:T(8,128)(2,1)S(1)} %get-tuple-element.426), channel_id=1, source_target_pairs={{0,4},{4,8},{8,12},{12,16},{16,20},{20,24},{24,28},{28,32},{32,36}... | collective-permute-start | bytes 1179656 | tf_op jit(solution)/shard_map/while/body/eval_jaxpr/ppermute | solution.py:16
  630.2 19.8 %collective-permute-start = (bf16[2,128,768]{1,2,0:T(8,128)(2,1)S(1)}, bf16[2,128,768]{1,2,0:T(8,128)(2,1)S(1)}, u32[]{:S(2)}, u32[]{:S(2)}) collective-permute-start(bf16[2,128,768]{1,2,0:T(8,128)(2,1)S(1)} %get-tuple-element.426), channel_id=1, source_target_pairs={{0,4},{4,8},{8,12},{12,16},{16,20},{20,24},{24,28},{28,32},{32,36}... | collective-permute-start | bytes 1179656 | tf_op jit(solution)/shard_map/while/body/eval_jaxpr/ppermute | solution.py:16
  650.9 19.5 %collective-permute-start = (bf16[2,128,768]{1,2,0:T(8,128)(2,1)S(1)}, bf16[2,128,768]{1,2,0:T(8,128)(2,1)S(1)}, u32[]{:S(2)}, u32[]{:S(2)}) collective-permute-start(bf16[2,128,768]{1,2,0:T(8,128)(2,1)S(1)} %get-tuple-element.426), channel_id=1, source_target_pairs={{0,4},{4,8},{8,12},{12,16},{16,20},{20,24},{24,28},{28,32},{32,36}... | collective-permute-start | bytes 1179656 | tf_op jit(solution)/shard_map/while/body/eval_jaxpr/ppermute | solution.py:16
  671.2 19.0 %collective-permute-start = (bf16[2,128,768]{1,2,0:T(8,128)(2,1)S(1)}, bf16[2,128,768]{1,2,0:T(8,128)(2,1)S(1)}, u32[]{:S(2)}, u32[]{:S(2)}) collective-permute-start(bf16[2,128,768]{1,2,0:T(8,128)(2,1)S(1)} %get-tuple-element.426), channel_id=1, source_target_pairs={{0,4},{4,8},{8,12},{12,16},{16,20},{20,24},{24,28},{28,32},{32,36}... | collective-permute-start | bytes 1179656 | tf_op jit(solution)/shard_map/while/body/eval_jaxpr/ppermute | solution.py:16
  (14 other events, 967.6 us)
where the time goes:
time: 710 us; the launch traced here: 709 us
  waiting for transfers between devices  555 us (78%)
  starting transfers between devices  99.7 us (14%)
  matrix products  20.9 us (3%)
  local copies, waits for them, and re-layouts  17.4 us (2%)
  other arithmetic  12.3 us (2%)
    ppermute x31, waiting for transfers between devices, shifted(): lax.ppermute(value, axis, [(i, (i + by) % devices) for i in range(devices)])  517 us
    ppermute x31, starting transfers between devices, shifted(): lax.ppermute(value, axis, [(i, (i + by) % devices) for i in range(devices)])  59.5 us
  transfers between devices with their start and end apart: 35, of which 35 were waited for; matrix products, arithmetic and copies ran while one was open for 3% of the time, Pallas kernels for 0%

commit v1 on v0

v1 whole, which is shorter than its diff:
```python
import functools
import math

import jax
import jax.numpy as jnp
from jax import lax
from jax.experimental import pallas as pl
from jax.experimental.pallas import tpu as pltpu
from jax.sharding import PartitionSpec as P

HEAD_DIM = 128
MASKED = -1e30
SCALE = 1.0 / math.sqrt(HEAD_DIM)
LOG2E = math.log2(math.e)
ROWS_BOUND = 6
MSG = 8
CHUNK = 256

NT = (((1,), (1,)), ((), ()))
TN = (((0,), (0,)), ((), ()))


def iota(shape, axis):
    return lax.broadcasted_iota(jnp.int32, shape, axis)


def dot(a, b, dims=(((1,), (0,)), ((), ()))):
    return lax.dot_general(a, b, dims, preferred_element_type=jnp.float32)


def clip_bounds(lengths_ref):
    bounds = []
    end = jnp.int32(0)
    for c in range(lengths_ref.shape[0]):
        start = end
        end = end + lengths_ref[c]
        bounds.append((start, end))
    return bounds


def pack_kernel(owners, lengths_ref, owner_ref, slot_ref, query_ref, out_ref):
    rows = query_ref.shape[0]
    owner = owner_ref[...]
    slot = slot_ref[...]
    place = owner * rows + slot
    clip = jnp.zeros_like(place)
    for _, end in clip_bounds(lengths_ref):
        clip = clip + (place >= end).astype(jnp.int32)
    along = jnp.broadcast_to(owner.astype(jnp.float32), (rows, rows))
    down = along.T
    earlier = (along == down) & (iota((rows, rows), 0) < iota((rows, rows), 1))
    rank = jnp.sum(earlier.astype(jnp.float32), axis=0, keepdims=True)
    rank_down = jnp.broadcast_to(rank, (rows, rows)).T
    target = owner * MSG + rank.astype(jnp.int32)
    spread = (owners * MSG, rows)
    line = iota(spread, 0)
    kind = lax.rem(line, MSG)
    pick = (line == target).astype(jnp.bfloat16)
    main = dot(pick, query_ref[...])
    slot_part = jnp.where(
        (kind == ROWS_BOUND) & (lax.div(line, MSG) == owner), (slot + 1).astype(jnp.float32), 0.0
    ).astype(jnp.bfloat16)
    rank_at = (rank_down == iota((rows, rows), 1).astype(jnp.float32)).astype(jnp.bfloat16)
    clip_part = jnp.where(kind == ROWS_BOUND + 1, clip.astype(jnp.float32), 0.0).astype(jnp.bfloat16)
    unit = (iota((rows, rows), 0) == iota((rows, rows), 1)).astype(jnp.bfloat16)
    extra = dot(slot_part, rank_at) + dot(clip_part, unit)
    out_ref[...] = main.astype(jnp.bfloat16)
    out_ref[:, :rows] = (main[:, :rows] + extra).astype(jnp.bfloat16)


def unpack_kernel(owners, plane, plane_ref, got_ref, query_ref, key_clip_ref):
    lines = owners * MSG
    rows = query_ref.shape[0]
    got = got_ref[...]
    head = got[:, :rows]
    square = (lines, lines)
    to_slot = (lax.div(iota(square, 0), MSG) * MSG + ROWS_BOUND == iota(square, 1)).astype(
        jnp.bfloat16
    )
    spread = dot(to_slot, head)
    kind = lax.rem(iota((lines, rows), 0), MSG)
    lane = iota((lines, rows), 1)
    place = jnp.sum(
        jnp.where((lane == kind) & (kind < ROWS_BOUND), spread, 0.0), axis=1, keepdims=True
    )
    put = (place == (lane + 1).astype(jnp.float32)).astype(jnp.bfloat16)
    query_ref[...] = dot(put, got, TN).astype(jnp.bfloat16)
    first = plane_ref[0] * plane
    block = (plane, lines)
    to_clip = (
        (iota(block, 0) + first) * MSG + ROWS_BOUND + 1 == iota(block, 1)
    ).astype(jnp.bfloat16)
    clips = dot(to_clip, head)
    unit = (iota((rows, rows), 0) == iota((rows, rows), 1)).astype(jnp.bfloat16)
    down = iota((rows, rows), 0).astype(jnp.float32)
    for j in range(plane):
        member = (clips[j : j + 1, :] == down).astype(jnp.bfloat16)
        key_clip_ref[j * rows : (j + 1) * rows, :] = dot(unit, member, NT).astype(jnp.bfloat16)


def attend_kernel(
    base_ref, lengths_ref, query_ref, key_ref, value_ref, key_clip_ref, out_ref, stat_ref, scores
):
    h = pl.program_id(0)
    rows = query_ref.shape[0]
    keys = key_ref.shape[0]
    position = iota((rows, HEAD_DIM), 0) + base_ref[0]
    lane = iota((rows, HEAD_DIM), 1)
    dead = jnp.zeros((rows, HEAD_DIM), jnp.float32)
    for c, (start, end) in enumerate(clip_bounds(lengths_ref)):
        outside = (position < start) | (position >= end)
        dead = jnp.where((lane == c) & outside, MASKED, dead)
    query = jnp.concatenate([query_ref[...], dead.astype(jnp.bfloat16)], axis=1)
    top = jnp.full((rows, HEAD_DIM), -3e38, jnp.float32)
    for k in range(0, keys, CHUNK):
        key = jnp.concatenate(
            [key_ref[k : k + CHUNK, :], key_clip_ref[k : k + CHUNK, :]], axis=1
        )
        s = dot(query, key, NT)
        scores[:, k : k + CHUNK] = s
        for j in range(0, CHUNK, HEAD_DIM):
            top = jnp.maximum(top, s[:, j : j + HEAD_DIM])
    top = jnp.max(top, axis=1, keepdims=True)
    shift = top * (SCALE * LOG2E)
    ones = jnp.ones((CHUNK, HEAD_DIM), jnp.bfloat16)
    total = jnp.zeros((rows, 2 * HEAD_DIM), jnp.float32)
    for k in range(0, keys, CHUNK):
        w = jnp.exp2(scores[:, k : k + CHUNK] * (SCALE * LOG2E) - shift).astype(jnp.bfloat16)
        value = jnp.concatenate([value_ref[k : k + CHUNK, :], ones], axis=1)
        total = total + dot(w, value)
    weight = total[:, HEAD_DIM:]
    out_ref[...] = (total[:, :HEAD_DIM] / weight).astype(out_ref.dtype)
    level = shift + jnp.log2(weight)

    high = level.astype(jnp.bfloat16)
    rest = level - high.astype(jnp.float32)
    mid = rest.astype(jnp.bfloat16)
    low = (rest - mid.astype(jnp.float32)).astype(jnp.bfloat16)
    held = jnp.where(h == 0, jnp.zeros((rows, HEAD_DIM), jnp.bfloat16), stat_ref[...])
    held = jnp.where(lane == h, high, held)
    held = jnp.where(lane == h + 8, mid, held)
    stat_ref[...] = jnp.where(lane == h + 16, low, held)


def combine_kernel(
    base_ref, lengths_ref, own_ref, own_stat_ref, far_ref, gates_ref, out_ref
):
    rows, width = own_ref.shape
    position = iota((rows, HEAD_DIM), 0) + base_ref[0]
    lane = iota((rows, HEAD_DIM), 1)
    member = jnp.zeros((rows, HEAD_DIM), jnp.float32)
    for c, (start, end) in enumerate(clip_bounds(lengths_ref)):
        inside = (position >= start) & (position < end)
        member = jnp.where((lane == c) & inside, 1.0, member)
    gate = dot(member[:, : gates_ref.shape[0]].astype(jnp.bfloat16), gates_ref[...])

    own_stat = own_stat_ref[...].astype(jnp.float32)
    far_stat = far_ref[:, width:].astype(jnp.float32)
    for h in range(width // HEAD_DIM):

        def level(stat):
            return (stat[:, h : h + 1] + stat[:, h + 8 : h + 9]) + stat[:, h + 16 : h + 17]

        gap = level(own_stat) - level(far_stat)
        own_share = 1.0 / (1.0 + jnp.exp2(-gap))
        far_share = 1.0 / (1.0 + jnp.exp2(gap))
        at = slice(h * HEAD_DIM, (h + 1) * HEAD_DIM)
        mixed = own_ref[:, at] * own_share + far_ref[:, at].astype(jnp.float32) * far_share
        out_ref[:, at] = (mixed * gate[:, at]).astype(jnp.bfloat16)


SMEM = pl.BlockSpec(memory_space=pltpu.SMEM)
VMEM = pl.BlockSpec(memory_space=pltpu.VMEM)


def attend(base, lengths, query, key_value, key_clip, out_type):
    rows, width = query.shape
    heads = width // HEAD_DIM
    keys = key_value.shape[0]
    return pl.pallas_call(
        attend_kernel,
        grid=(heads,),
        in_specs=[
            SMEM,
            SMEM,
            pl.BlockSpec((rows, HEAD_DIM), lambda h: (0, h)),
            pl.BlockSpec((keys, HEAD_DIM), lambda h: (0, h)),
            pl.BlockSpec((keys, HEAD_DIM), lambda h: (0, heads + h)),
            pl.BlockSpec((keys, HEAD_DIM), lambda h: (0, 0)),
        ],
        out_specs=[
            pl.BlockSpec((rows, HEAD_DIM), lambda h: (0, h)),
            pl.BlockSpec((rows, HEAD_DIM), lambda h: (0, 0)),
        ],
        out_shape=[
            jax.ShapeDtypeStruct((rows, width), out_type),
            jax.ShapeDtypeStruct((rows, HEAD_DIM), jnp.bfloat16),
        ],
        scratch_shapes=[pltpu.VMEM((rows, keys), jnp.float32)],
        compiler_params=pltpu.CompilerParams(vmem_limit_bytes=32 * 1024 * 1024),
        cost_estimate=pl.CostEstimate(
            flops=4 * rows * keys * width,
            bytes_accessed=4 * keys * width,
            transcendentals=rows * keys * heads,
        ),
    )(base, lengths, query, key_value, key_value, key_clip)


def shards(
    query_rows, key_rows, value_rows, deal_owner, deal_slot, clip_lengths, clip_steps, gate_table
):
    devices = lax.axis_size("seq")
    plane = devices // 2
    rows, width = query_rows.shape
    me = lax.axis_index("seq")
    far = (me + plane) % devices
    across = [(i, (i + plane) % devices) for i in range(devices)]
    planes = [list(range(plane)), list(range(plane, devices))]

    key_value = lax.all_gather(
        jnp.concatenate([key_rows, value_rows], axis=1),
        "seq",
        axis_index_groups=planes,
        tiled=True,
    )

    message = pl.pallas_call(
        functools.partial(pack_kernel, devices),
        in_specs=[SMEM, VMEM, VMEM, VMEM],
        out_specs=VMEM,
        out_shape=jax.ShapeDtypeStruct((devices * MSG, width), jnp.bfloat16),
    )(clip_lengths, deal_owner[None, :], deal_slot[None, :], query_rows)
    got = lax.all_to_all(
        message.reshape(devices, MSG, width), "seq", split_axis=0, concat_axis=0, tiled=True
    ).reshape(devices * MSG, width)
    query, key_clip = pl.pallas_call(
        functools.partial(unpack_kernel, devices, plane),
        in_specs=[SMEM, VMEM],
        out_specs=[VMEM, VMEM],
        out_shape=[
            jax.ShapeDtypeStruct((rows, width), jnp.bfloat16),
            jax.ShapeDtypeStruct((plane * rows, HEAD_DIM), jnp.bfloat16),
        ],
    )((me // plane)[None], got)
    far_query = lax.ppermute(query, "seq", across)
    gates = jnp.take(gate_table, clip_steps, axis=0)

    base = (me * rows)[None]
    far_base = (far * rows)[None]
    far_out, far_stat = attend(
        far_base, clip_lengths, far_query, key_value, key_clip, jnp.bfloat16
    )
    sent = lax.ppermute(jnp.concatenate([far_out, far_stat], axis=1), "seq", across)
    own_out, own_stat = attend(base, clip_lengths, query, key_value, key_clip, jnp.float32)
    return pl.pallas_call(
        combine_kernel,
        in_specs=[SMEM, SMEM, VMEM, VMEM, VMEM, VMEM],
        out_specs=VMEM,
        out_shape=jax.ShapeDtypeStruct((rows, width), jnp.bfloat16),
    )(base, clip_lengths, own_out, own_stat, sent, gates)


def solution(mesh):
    placed = (
        P(("dp", "seq"), "tensor"),
        P(("dp", "seq"), "tensor"),
        P(("dp", "seq"), "tensor"),
        P(("dp", "seq")),
        P(("dp", "seq")),
        P("dp"),
        P("dp"),
        P(None, "tensor"),
    )
    return jax.shard_map(
        shards, mesh=mesh, in_specs=placed, out_specs=P(("dp", "seq"), "tensor"), check_vma=False
    )
```

time: 710 us -> 111 us (0.16)
  the two profiles are of different devices: /device:TPU:454 before, /device:TPU:1 now
where the time goes in v1:
time: 111 us; the launch traced here: 110 us
  waiting for transfers between devices  37 us (33%)
  starting transfers between devices  26.8 us (24%)
  Pallas kernels  23.2 us (21%)
  between operations  13.5 us (12%)
  local copies, waits for them, and re-layouts  7.19 us (6%)
  other arithmetic  2.62 us (2%)
    all_to_all x1, waiting for transfers between devices, shards(): lax.all_to_all(message.reshape(devices, MSG, width), 'seq', split_axis=0,...  20.5 us
    all_to_all x1, starting transfers between devices, shards(): lax.all_to_all(message.reshape(devices, MSG, width), 'seq', split_axis=0,...  17.2 us
    pallas_call x2, Pallas kernels, attend(): pl.pallas_call(attend_kernel, grid=(heads,), in_specs=[SMEM, SMEM, pl.Blo...  16 us
    all_gather x1, waiting for transfers between devices, shards(): lax.all_gather(jnp.concatenate([key_rows, value_rows], axis=1), 'seq', ax...  8.31 us
    ppermute x1, waiting for transfers between devices, shards(): far_query = lax.ppermute(query, 'seq', across)  8.1 us
    ppermute x1, starting transfers between devices, shards(): lax.ppermute(jnp.concatenate([far_out, far_stat], axis=1), 'seq', across)  7.08 us
    unnamed x24, local copies, waits for them, and re-layouts  6.62 us
    pallas_call x1, Pallas kernels, shards(): pl.pallas_call(functools.partial(unpack_kernel, devices, plane), in_specs...  2.8 us
  transfers between devices with their start and end apart: 4, of which 3 were waited for; matrix products, arithmetic and copies ran while one was open for 1% of the time, Pallas kernels for 12%

profile of v1, /device:TPU:1, one launch (start us, length us, event | category | flops | bytes accessed | tf_op | source)
XLA Modules:
  0.0 110.3 jit_solution(17591256841881195060)
XLA Ops:
  6.5 1.9 %pad_maximum_fusion = bf16[128,1536]{1,0:T(8,128)(2,1)} fusion(bf16[128,768]{1,0:T(8,128)(2,1)} %param.10, bf16[128,768]{1,0:T(8,128)(2,1)} %param.9), kind=kLoop, calls=%fused_computation.1 | loop fusion | flops 786432 | bytes 786432 | tf_op jit(solution)/shard_map/concatenate | solution.py:221
  8.5 0.0 all-gather.2.cloned.1.call-update
  8.5 2.1 %shard_map.82 = bf16[256,768]{1,0:T(8,128)(2,1)} custom-call(s32[8]{0:T(128)} %lengths_ref.7, s32[1,128]{1,0:T(1,128)} %bitcast.9, s32[1,128]{1,0:T(1,128)} %bitcast.10, bf16[128,768]{1,0:T(8,128)(2,1)} %query_ref.1), custom_call_target="tpu_custom_call" | custom-call | tf_op jit(solution)/shard_map/pallas_call | solution.py:227
  10.6 17.2 %all-to-all-start = ((bf16[32,8,768]{2,1,0:T(8,128)(2,1)}), bf16[32,8,768]{2,1,0:T(8,128)(2,1)S(1)}, u32[]{:S(2)}, u32[]{:S(2)}) async-start(bf16[32,8,768]{2,1,0:T(8,128)(2,1)} %bitcast.8), calls=%async_computation | async-start | bytes 786432 | tf_op jit(solution)/shard_map/all_to_all | solution.py:233
  27.9 0.6 gather_fusion
  28.4 20.5 %all-to-all-done = bf16[32,8,768]{2,1,0:T(8,128)(2,1)S(1)} async-done(((bf16[32,8,768]{2,1,0:T(8,128)(2,1)}), bf16[32,8,768]{2,1,0:T(8,128)(2,1)S(1)}, u32[]{:S(2)}, u32[]{:S(2)}) %all-to-all-start) | async-done | bytes 393248 | tf_op jit(solution)/shard_map/all_to_all | solution.py:233
  49.0 0.7 copy-done.9
  49.7 2.8 %shard_map.83 = (bf16[128,768]{1,0:T(8,128)(2,1)}, bf16[2048,128]{1,0:T(8,128)(2,1)}) custom-call(s32[1]{0:T(128)} %bitcast.1.plane_ref, bf16[256,768]{1,0:T(8,128)(2,1)} %bitcast.7), custom_call_target="tpu_custom_call" | custom-call | tf_op jit(solution)/shard_map/pallas_call | solution.py:236
  52.5 2.5 %collective-permute-start = (bf16[128,768]{1,0:T(8,128)(2,1)}, bf16[128,768]{1,0:T(8,128)(2,1)S(1)}, u32[]{:S(2)}, u32[]{:S(2)}) collective-permute-start(bf16[128,768]{1,0:T(8,128)(2,1)} %get-tuple-element.11.query_ref), channel_id=1, source_target_pairs={{0,64},{4,68},{8,72},{12,76},{16,80},{20,84},{24,88},{28,92},{32,9... | collective-permute-start | bytes 589832 | tf_op jit(solution)/shard_map/ppermute | solution.py:245
  55.1 8.1 %collective-permute-done.query_ref = bf16[128,768]{1,0:T(8,128)(2,1)S(1)} collective-permute-done((bf16[128,768]{1,0:T(8,128)(2,1)}, bf16[128,768]{1,0:T(8,128)(2,1)S(1)}, u32[]{:S(2)}, u32[]{:S(2)}) %collective-permute-start) | collective-permute-done | bytes 196640 | tf_op jit(solution)/shard_map/ppermute | solution.py:245
  63.2 8.3 %all-gather.2.cloned.1.call-done.key_ref.value_ref = bf16[2048,1536]{1,0:T(8,128)(2,1)} async-done(((bf16[128,1536]{1,0:T(8,128)(2,1)}), bf16[2048,1536]{1,0:T(8,128)(2,1)}) %all-gather.2.cloned.1.call-update) | async-done | bytes 6291472 | tf_op jit(solution)/shard_map/all_gather | solution.py:220
  71.5 0.0 copy-done.8
  71.5 2.8 %copy-done.1 = bf16[2048,1536]{1,0:T(8,128)(2,1)S(1)} copy-done((bf16[2048,1536]{1,0:T(8,128)(2,1)S(1)}, bf16[2048,1536]{1,0:T(8,128)(2,1)}, u32[]{:S(2)}) %copy-start.1) | copy-done | bytes 6291480
  74.3 1.0 copy-done.3
  75.3 8.0 %shard_map.85 = (bf16[128,768]{1,0:T(8,128)(2,1)S(1)}, bf16[128,128]{1,0:T(8,128)(2,1)S(1)}) custom-call(s32[1]{0:T(128)} %bitcast.6.base_ref, s32[8]{0:T(128)S(1)} %copy-done.8, bf16[128,768]{1,0:T(8,128)(2,1)S(1)} %collective-permute-done.query_ref, bf16[2048,1536]{1,0:T(8,128)(2,1)S(1)} %copy-done.1, bf16[2048,1536]{1,0:T(8,128)(2,1)S(1)} %copy-done.1, ...), custom_call_target="tpu_custom_call" | custom-call | flops 805306368 | bytes 6291456 | tf_op jit(solution)/shard_map/pallas_call | solution.py:180
  83.4 7.1 %collective-permute-start.1 = (bf16[128,896]{1,0:T(8,128)(2,1)S(1)}, bf16[128,896]{1,0:T(8,128)(2,1)S(1)}, u32[]{:S(2)}, u32[]{:S(2)}) collective-permute-start(bf16[128,896]{1,0:T(8,128)(2,1)S(1)} %pad_maximum_fusion.1), channel_id=1, source_target_pairs={{0,64},{4,68},{8,72},{12,76},{16,80},{20,84},{24,88},{28,92},{32,9... | collective-permute-start | bytes 688136 | tf_op jit(solution)/shard_map/ppermute | solution.py:253
  90.4 0.7 broadcast_select_fusion.gates_ref
  91.1 0.0 copy-done.2
  91.1 8.0 %shard_map.84 = (f32[128,768]{1,0:T(8,128)S(1)}, bf16[128,128]{1,0:T(8,128)(2,1)S(1)}) custom-call(s32[1]{0:T(128)} %bitcast.base_ref, s32[8]{0:T(128)S(1)} %copy-done.8, bf16[128,768]{1,0:T(8,128)(2,1)S(1)} %copy-done.6, bf16[2048,1536]{1,0:T(8,128)(2,1)S(1)} %copy-done.2, bf16[2048,1536]{1,0:T(8,128)(2,1)S(1)} %copy-done.2, bf16[2048,128]{1,0:T(8,128)(2,1)S(1)} %copy-done.4), custom_call_target="tpu_custom_call" | custom-call | flops 805306368 | bytes 6291456 | tf_op jit(solution)/shard_map/pallas_call | solution.py:180
  99.2 0.7 copy-done.5
  99.9 0.6 copy-done.7
  100.5 0.0 collective-permute-done.1.far_ref
  100.5 0.7 copy-done.10
  101.2 2.2 %shard_map.86 = bf16[128,768]{1,0:T(8,128)(2,1)} custom-call(s32[1]{0:T(128)} %bitcast.base_ref, s32[8]{0:T(128)} %lengths_ref.7, f32[128,768]{1,0:T(8,128)} %copy-done.5, bf16[128,128]{1,0:T(8,128)(2,1)} %copy-done.7, bf16[128,896]{1,0:T(8,128)(2,1)} %copy-done.10, bf16[8,768]{1,0:T(8,128)(2,1)} %broadcast_select_fusion.gates_ref), custom_call_target="tpu_custom_call" | custom-call | tf_op jit(solution)/shard_map/pallas_call | solution.py:255
  (21 shorter events, 0.1 us)
Async XLA Ops:
  6.5 21.3 %copy-start = (bf16[1000,768]{1,0:T(8,128)(2,1)S(1)}, bf16[1000,768]{1,0:T(8,128)(2,1)}, u32[]{:S(2)}) copy-start(bf16[1000,768]{1,0:T(8,128)(2,1)} %param.15) | copy-start | bytes 4608004
  6.5 64.9 %copy-start.8 = (s32[8]{0:T(128)S(1)}, s32[8]{0:T(128)}, u32[]{:S(2)}) copy-start(s32[8]{0:T(128)} %lengths_ref.7) | copy-start | bytes 100
  6.5 21.3 %copy-start.11 = (s32[8]{0:T(128)S(1)}, s32[8]{0:T(128)}, u32[]{:S(2)}) copy-start(s32[8]{0:T(128)} %param.14) | copy-start | bytes 100
  6.5 64.9 %all-gather.2.cloned.1.call-start = ((), (), s32[]{:S(2)}) async-start(), calls=%async_computation.1 | async-start | bytes 6684672 | tf_op jit(solution)/shard_map/all_gather | solution.py:220
  10.6 38.4 %all-to-all-start = ((bf16[32,8,768]{2,1,0:T(8,128)(2,1)}), bf16[32,8,768]{2,1,0:T(8,128)(2,1)S(1)}, u32[]{:S(2)}, u32[]{:S(2)}) async-start(bf16[32,8,768]{2,1,0:T(8,128)(2,1)} %bitcast.8), calls=%async_computation | async-start | bytes 786432 | tf_op jit(solution)/shard_map/all_to_all | solution.py:233
  49.0 0.7 copy-start.9
  52.5 10.6 %collective-permute-start = (bf16[128,768]{1,0:T(8,128)(2,1)}, bf16[128,768]{1,0:T(8,128)(2,1)S(1)}, u32[]{:S(2)}, u32[]{:S(2)}) collective-permute-start(bf16[128,768]{1,0:T(8,128)(2,1)} %get-tuple-element.11.query_ref), channel_id=1, source_target_pairs={{0,64},{4,68},{8,72},{12,76},{16,80},{20,84},{24,88},{28,92},{32,9... | collective-permute-start | bytes 589832 | tf_op jit(solution)/shard_map/ppermute | solution.py:245
  71.5 2.8 %copy-start.1 = (bf16[2048,1536]{1,0:T(8,128)(2,1)S(1)}, bf16[2048,1536]{1,0:T(8,128)(2,1)}, u32[]{:S(2)}) copy-start(bf16[2048,1536]{1,0:T(8,128)(2,1)} %all-gather.2.cloned.1.call-done.key_ref.value_ref) | copy-start | bytes 18874372
  74.3 1.0 copy-start.3
  75.3 15.8 %copy-start.2 = (bf16[2048,1536]{1,0:T(8,128)(2,1)S(1)}, bf16[2048,1536]{1,0:T(8,128)(2,1)}, u32[]{:S(2)}) copy-start(bf16[2048,1536]{1,0:T(8,128)(2,1)} %all-gather.2.cloned.1.call-done.key_ref.value_ref) | copy-start | bytes 18874372
  75.3 15.8 %copy-start.4 = (bf16[2048,128]{1,0:T(8,128)(2,1)S(1)}, bf16[2048,128]{1,0:T(8,128)(2,1)}, u32[]{:S(2)}) copy-start(bf16[2048,128]{1,0:T(8,128)(2,1)} %get-tuple-element.12.key_clip_ref) | copy-start | bytes 1572868
  75.3 15.8 %copy-start.6 = (bf16[128,768]{1,0:T(8,128)(2,1)S(1)}, bf16[128,768]{1,0:T(8,128)(2,1)}, u32[]{:S(2)}) copy-start(bf16[128,768]{1,0:T(8,128)(2,1)} %get-tuple-element.11.query_ref) | copy-start | bytes 589828
  83.4 17.2 %collective-permute-start.1 = (bf16[128,896]{1,0:T(8,128)(2,1)S(1)}, bf16[128,896]{1,0:T(8,128)(2,1)S(1)}, u32[]{:S(2)}, u32[]{:S(2)}) collective-permute-start(bf16[128,896]{1,0:T(8,128)(2,1)S(1)} %pad_maximum_fusion.1), channel_id=1, source_target_pairs={{0,64},{4,68},{8,72},{12,76},{16,80},{20,84},{24,88},{28,92},{32,9... | collective-permute-start | bytes 688136 | tf_op jit(solution)/shard_map/ppermute | solution.py:253
  99.2 0.8 copy-start.5
  99.9 0.6 copy-start.7
  100.5 0.7 copy-start.10
Sparse Core Ops, SparseCore 0:
  9.5 61.9 all-gather.1

commit v2 on v0

v2 whole, which is shorter than its diff:
```python
import functools
import math

import jax
import jax.numpy as jnp
from jax import lax
from jax.experimental import pallas as pl
from jax.experimental.pallas import tpu as pltpu
from jax.sharding import PartitionSpec as P

HEAD_DIM = 128
MASKED = -1e30
SCALE2 = math.log2(math.e) / math.sqrt(HEAD_DIM)
BOUND = 6
MSG = 24
CHUNK = 256
ATTEND_VMEM = 24 * 1024 * 1024
SMALL_VMEM = 10 * 1024 * 1024

NN = (((1,), (0,)), ((), ()))
NT = (((1,), (1,)), ((), ()))
TN = (((0,), (0,)), ((), ()))


def iota(shape, axis):
    return lax.broadcasted_iota(jnp.int32, shape, axis)


def dot(a, b, dims=NN):
    return lax.dot_general(a, b, dims, preferred_element_type=jnp.float32)


def unit(size):
    return (iota((size, size), 0) == iota((size, size), 1)).astype(jnp.bfloat16)


def clip_bounds(lengths_ref):
    bounds = []
    end = jnp.int32(0)
    for c in range(lengths_ref.shape[0]):
        start = end
        end = end + lengths_ref[c]
        bounds.append((start, end))
    return bounds


def split_kernel(devices, me_ref, key_ref, value_ref, kept_ref, given_ref):
    half = key_ref.shape[1] // 2
    low, high = slice(0, half), slice(half, 2 * half)
    side = place_of(me_ref[0], devices)[0]

    @pl.when(side == 0)
    def _():
        kept_ref[:, low] = key_ref[:, low]
        kept_ref[:, high] = value_ref[:, low]
        given_ref[:, low] = key_ref[:, high]
        given_ref[:, high] = value_ref[:, high]

    @pl.when(side != 0)
    def _():
        kept_ref[:, low] = key_ref[:, high]
        kept_ref[:, high] = value_ref[:, high]
        given_ref[:, low] = key_ref[:, low]
        given_ref[:, high] = value_ref[:, low]


def pack_kernel(plane, lengths_ref, owner_ref, slot_ref, query_ref, out_ref):
    rows, width = query_ref.shape
    half = width // 2
    ring = plane // 2
    owner = owner_ref[...]
    slot = slot_ref[...]
    place = owner * rows + slot
    clip = jnp.zeros_like(place)
    for _, end in clip_bounds(lengths_ref):
        clip = clip + (place >= end).astype(jnp.int32)
    clip = jnp.broadcast_to(clip.astype(jnp.float32), (8, rows))
    square = (rows, rows)
    along = jnp.broadcast_to(owner.astype(jnp.float32), square)
    earlier = (along == along.T) & (iota(square, 0) < iota(square, 1))
    rank = jnp.sum(earlier.astype(jnp.float32), axis=0, keepdims=True).astype(jnp.int32)
    there = lax.div(lax.rem(owner, plane), 2)
    which = lax.div(owner, plane) * 2 + lax.rem(owner, 2)
    target = there * MSG + which * BOUND + rank
    spread = (ring * MSG, rows)
    line = iota(spread, 0)
    lane = iota(spread, 1)
    kind = lax.rem(line, MSG)
    pick = (line == target).astype(jnp.bfloat16)
    main = dot(pick, query_ref[...])
    slot_down = jnp.broadcast_to((slot + 1).astype(jnp.float32), square).T
    slots = jnp.where(iota(square, 1) == rows - 1, slot_down, 0.0).astype(jnp.bfloat16)
    meta = dot(pick, slots)
    meta = jnp.where((kind == 0) & (lane < rows // 2), clip[:1], meta)
    turned = pltpu.roll(clip, rows // 2, 1)[:1]
    meta = jnp.where((kind == 1) & (lane < rows // 2), turned, meta).astype(jnp.bfloat16)
    for s in range(2):
        at = slice(s * ring * MSG, (s + 1) * ring * MSG)
        out_ref[at, :half] = main[:, s * half : (s + 1) * half].astype(jnp.bfloat16)
        out_ref[at, half:] = meta


def place_of(me, devices):
    plane = devices // 2
    half = lax.div(me, plane)
    return half, lax.div(lax.rem(me, plane), 2), lax.rem(me, 2)


def key_sources(me, devices):
    plane = devices // 2
    ring = plane // 2
    half, y, core = place_of(me, devices)

    def pair(h, distance):
        there = lax.rem(y + (2 * core - 1) * distance + ring, ring)
        at = h * plane + there * 2
        return [at, at + 1]

    near, far = half, 1 - half
    order = [me, lax.rem(me + plane, devices)]
    for h, distance in ((near, 1), (near, 2), (far, 1), (near, 3), (far, 2), (far, 3)):
        order += pair(h, distance)
    return order + [pair(near, 4)[0] + core, pair(far, 4)[0] + core]


def unpack_kernel(
    devices,
    early,
    me_ref,
    lengths_ref,
    got_ref,
    other_ref,
    query_ref,
    other_query_ref,
    clips0_ref,
    clips1_ref,
    dead_ref,
):
    each = got_ref.shape[0]
    lines = 2 * each
    rows = HEAD_DIM
    plane = devices // 2
    me = me_ref[0]
    half, _, core = place_of(me, devices)
    got = jnp.concatenate([got_ref[...], other_ref[...]], axis=0)
    data, meta = got[:, :-rows], got[:, -rows:]
    kind = lax.rem(iota((lines, 1), 0), MSG)
    from_half = lax.div(kind, 2 * BOUND)
    from_core = lax.rem(lax.div(kind, BOUND), 2)
    quarter = (from_core != core).astype(jnp.int32) * 2 + (from_half != half).astype(jnp.int32)
    slot = meta[:, rows - 1 :].astype(jnp.float32)
    target = jnp.where(slot > 0, slot - 1.0 + (quarter * rows).astype(jnp.float32), -1.0)
    target = jnp.broadcast_to(target, (lines, rows))
    target = jnp.concatenate(
        [target[i : i + rows, :].T[:1, :] for i in range(0, lines, rows)], axis=1
    )
    put = (iota((4 * rows, lines), 0).astype(jnp.float32) == target).astype(jnp.bfloat16)
    queries = dot(put, data).astype(jnp.bfloat16)
    query_ref[...] = queries[: 2 * rows]
    other_query_ref[...] = queries[2 * rows :]

    order = key_sources(me, devices)
    slots = len(order)
    block = (slots, lines)
    line = iota(block, 0)
    source = jnp.zeros(block, jnp.int32)
    for j, at in enumerate(order):
        at = lax.div(at, 2) * MSG + (lax.rem(at, 2) != core).astype(jnp.int32) * each
        source = jnp.where(line == j, at, source)
    first = dot((source == iota(block, 1)).astype(jnp.bfloat16), meta)
    second = dot((source + 1 == iota(block, 1)).astype(jnp.bfloat16), meta)
    ids = jnp.where(iota((slots, rows), 1) < rows // 2, first, pltpu.roll(second, rows // 2, 1))
    down = iota((rows, rows), 0).astype(jnp.float32)
    for j in range(slots):
        member = (ids[j : j + 1, :] == down).astype(jnp.bfloat16)
        clips = dot(unit(rows), member, NT).astype(jnp.bfloat16)
        if j < early:
            clips0_ref[j * rows : (j + 1) * rows, :] = clips
        else:
            clips1_ref[(j - early) * rows : (j + 1 - early) * rows, :] = clips

    bounds = clip_bounds(lengths_ref)
    other = lax.rem(me + plane, devices)
    away = 1 - 2 * core
    lane = iota((rows, HEAD_DIM), 1)
    for q, owner in enumerate((me, other, me + away, other + away)):
        position = iota((rows, HEAD_DIM), 0) + owner * rows
        dead = jnp.zeros((rows, HEAD_DIM), jnp.float32)
        for c, (start, end) in enumerate(bounds):
            outside = (position < start) | (position >= end)
            dead = jnp.where((lane == c) & outside, MASKED, dead)
        dead_ref[q * rows : (q + 1) * rows, :] = dead.astype(jnp.bfloat16)


def split3(value):
    high = value.astype(jnp.bfloat16)
    rest = value - high.astype(jnp.float32)
    mid = rest.astype(jnp.bfloat16)
    low = (rest - mid.astype(jnp.float32)).astype(jnp.bfloat16)
    return high, mid, low


def pair_up(sizes):
    chunks = []
    at = 0
    parts = []
    for i, size in enumerate(sizes):
        if size >= CHUNK:
            for start in range(0, size, CHUNK):
                chunks.append((at, [(i, start, CHUNK)]))
                at += CHUNK
            continue
        parts.append((i, 0, size))
        if sum(p[2] for p in parts) == CHUNK:
            chunks.append((at, parts))
            at += CHUNK
            parts = []
    assert not parts
    return chunks


def attend_kernel(sizes, first, last, *refs):
    refs = list(refs)
    dead_ref = refs.pop(0)
    query_refs = [refs.pop(0), refs.pop(0)]
    block_refs = [refs.pop(0) for _ in sizes]
    clip_ref = refs.pop(0)
    if not first:
        sum_ref, stat_ref = refs.pop(0), refs.pop(0)
    if last:
        out_ref, level_ref, sent_ref = refs.pop(0), refs.pop(0), refs.pop(0)
    else:
        new_sum_ref, new_stat_ref = refs.pop(0), refs.pop(0)
    scores = refs.pop(0)
    tile, width = query_refs[0].shape
    heads = width // HEAD_DIM
    lane = iota((tile, HEAD_DIM), 1)
    chunks = pair_up(sizes)
    ones = jnp.ones((CHUNK, HEAD_DIM), jnp.bfloat16)
    for t in range(2):
        rows = slice(t * tile, (t + 1) * tile)
        stat = jnp.zeros((tile, HEAD_DIM), jnp.float32)
        for h in range(heads):
            key_at = slice(h * HEAD_DIM, (h + 1) * HEAD_DIM)
            value_at = slice(width + h * HEAD_DIM, width + (h + 1) * HEAD_DIM)
            query = jnp.concatenate([query_refs[t][:, key_at], dead_ref[rows, :]], axis=1)
            top = jnp.full((tile, HEAD_DIM), -3e38, jnp.float32)
            for at, members in chunks:
                key = jnp.concatenate([block_refs[i][o : o + n, key_at] for i, o, n in members])
                key = jnp.concatenate([key, clip_ref[at : at + CHUNK, :]], axis=1)
                s = dot(query, key, NT)
                scores[t * heads + h, :, at : at + CHUNK] = s
                for j in range(0, CHUNK, HEAD_DIM):
                    top = jnp.maximum(top, s[:, j : j + HEAD_DIM])
            top = jnp.max(top, axis=1, keepdims=True) * SCALE2
            if first:
                total = jnp.zeros((tile, 2 * HEAD_DIM), jnp.float32)
            else:
                old_top = stat_ref[rows, h : h + 1]
                top = jnp.maximum(top, old_top)
                fade = jnp.exp2(old_top - top)
                weight = stat_ref[rows, h + 8 : h + 9] * fade
                weight = jnp.broadcast_to(weight, (tile, HEAD_DIM))
                total = jnp.concatenate([sum_ref[rows, key_at] * fade, weight], axis=1)
            for at, members in chunks:
                w = scores[t * heads + h, :, at : at + CHUNK] * SCALE2 - top
                w = jnp.exp2(w).astype(jnp.bfloat16)
                value = jnp.concatenate([block_refs[i][o : o + n, value_at] for i, o, n in members])
                total = total + dot(w, jnp.concatenate([value, ones], axis=1))
            weight = total[:, HEAD_DIM:]
            if not last:
                new_sum_ref[rows, key_at] = total[:, :HEAD_DIM]
                stat = jnp.where(lane == h, top, stat)
                stat = jnp.where(lane == h + 8, weight, stat)
                continue
            out = total[:, :HEAD_DIM] / weight
            stat = jnp.where(lane == h, top + jnp.log2(weight), stat)
            if t == 0:
                out_ref[:, key_at] = out
            else:
                sent_ref[:, key_at] = out.astype(jnp.bfloat16)
        if not last:
            new_stat_ref[rows, :] = stat
        elif t == 0:
            level_ref[...] = stat
        else:
            high, mid, low = split3(stat)
            mid = pltpu.roll(mid.astype(jnp.float32), 8, 1)
            low = pltpu.roll(low.astype(jnp.float32), 16, 1)
            packed = jnp.where(lane < 8, high.astype(jnp.float32), jnp.where(lane < 16, mid, low))
            sent_ref[:, width:] = packed.astype(jnp.bfloat16)


def combine_kernel(
    devices, mine, me_ref, lengths_ref, own_ref, level_ref, got_ref, gates_ref, out_ref
):
    rows, width = own_ref.shape
    me = me_ref[0]
    half = place_of(me, devices)[0]
    owner = me if mine else lax.rem(me + devices // 2, devices)
    lane = iota((rows, HEAD_DIM), 1)
    position = iota((rows, HEAD_DIM), 0) + owner * rows
    member = jnp.zeros((rows, HEAD_DIM), jnp.float32)
    for c, (start, end) in enumerate(clip_bounds(lengths_ref)):
        inside = (position >= start) & (position < end)
        member = jnp.where((lane == c) & inside, 1.0, member)
    gates = jnp.where(half == 0, gates_ref[:, :width], gates_ref[:, width:])
    gate = dot(member[:, : gates.shape[0]].astype(jnp.bfloat16), gates)
    stat = got_ref[:, width:].astype(jnp.float32)
    for h in range(width // HEAD_DIM):
        got_level = (stat[:, h : h + 1] + stat[:, h + 8 : h + 9]) + stat[:, h + 16 : h + 17]
        gap = level_ref[:, h : h + 1] - got_level
        own_share = 1.0 / (1.0 + jnp.exp2(-gap))
        got_share = 1.0 / (1.0 + jnp.exp2(gap))
        at = slice(h * HEAD_DIM, (h + 1) * HEAD_DIM)
        mixed = own_ref[:, at] * own_share + got_ref[:, at].astype(jnp.float32) * got_share
        out_ref[:, at] = (mixed * gate[:, at]).astype(jnp.bfloat16)


def join_kernel(devices, me_ref, mine_ref, back_ref, out_ref):
    half = mine_ref.shape[1]
    low, high = slice(0, half), slice(half, 2 * half)
    side = place_of(me_ref[0], devices)[0]

    @pl.when(side == 0)
    def _():
        out_ref[:, low] = mine_ref[...]
        out_ref[:, high] = back_ref[...]

    @pl.when(side != 0)
    def _():
        out_ref[:, low] = back_ref[...]
        out_ref[:, high] = mine_ref[...]


SMEM = pl.BlockSpec(memory_space=pltpu.SMEM)


def whole(shape):
    return pl.BlockSpec(shape, lambda i: (0,) * len(shape))


def attend(dead, queries, blocks, clips, state, last):
    tile, width = queries[0].shape
    heads = width // HEAD_DIM
    sizes = [b.shape[0] for b in blocks]
    keys = sum(sizes)
    rows = 2 * tile
    first = state is None
    operands = [dead, *queries, *blocks, clips] + ([] if first else list(state))
    if last:
        out_shape = [
            jax.ShapeDtypeStruct((tile, width), jnp.float32),
            jax.ShapeDtypeStruct((tile, HEAD_DIM), jnp.float32),
            jax.ShapeDtypeStruct((tile, width + HEAD_DIM), jnp.bfloat16),
        ]
    else:
        out_shape = [
            jax.ShapeDtypeStruct((rows, width), jnp.float32),
            jax.ShapeDtypeStruct((rows, HEAD_DIM), jnp.float32),
        ]
    return pl.pallas_call(
        functools.partial(attend_kernel, sizes, first, last),
        grid=(1,),
        in_specs=[whole(o.shape) for o in operands],
        out_specs=[whole(o.shape) for o in out_shape],
        out_shape=out_shape,
        scratch_shapes=[pltpu.VMEM((2 * heads, tile, keys), jnp.float32)],
        compiler_params=pltpu.CompilerParams(vmem_limit_bytes=ATTEND_VMEM),
        cost_estimate=pl.CostEstimate(
            flops=4 * rows * keys * width,
            bytes_accessed=4 * keys * width,
            transcendentals=rows * keys * heads,
        ),
    )(*operands)


def shards(
    query_rows, key_rows, value_rows, deal_owner, deal_slot, clip_lengths, clip_steps, gate_table
):
    devices = lax.axis_size("seq")
    plane = devices // 2
    ring = plane // 2
    rows, width = query_rows.shape
    half_width = width // 2
    me = lax.axis_index("seq")
    core = me % 2

    def index(h, y, c):
        return h * plane + (y % ring) * 2 + c

    everyone = [(h, y, c) for h in range(2) for y in range(ring) for c in range(2)]
    to_half = [(index(h, y, c), index(1 - h, y, c)) for h, y, c in everyone]
    to_core = [(index(h, y, c), index(h, y, 1 - c)) for h, y, c in everyone]
    to_next = [(index(h, y, c), index(h, y + 1 - 2 * c, c)) for h, y, c in everyone]
    chips = [[2 * i, 2 * i + 1] for i in range(plane)]

    def step(block):
        return lax.ppermute(block, "seq", to_next)

    def chip_gather(block):
        return lax.all_gather(block, "seq", axis_index_groups=chips, tiled=True)

    def core_half(block):
        return lax.dynamic_slice_in_dim(block, core * rows, rows, axis=0)

    def small(kernel, in_specs, outs):
        return pl.pallas_call(
            kernel,
            grid=(1,),
            in_specs=in_specs,
            out_specs=[whole(o.shape) for o in outs],
            out_shape=outs,
            compiler_params=pltpu.CompilerParams(vmem_limit_bytes=SMALL_VMEM),
        )

    def bf16(*shape):
        return jax.ShapeDtypeStruct(shape, jnp.bfloat16)

    def after(value, *others):
        return lax.optimization_barrier((value, *others))[0]

    mine = me[None]
    ring_rows = plane * MSG
    message = pl.pallas_call(
        functools.partial(pack_kernel, plane),
        grid=(1,),
        in_specs=[SMEM, whole((1, rows)), whole((1, rows)), whole((rows, width))],
        out_specs=whole((ring_rows, half_width + HEAD_DIM)),
        out_shape=bf16(ring_rows, half_width + HEAD_DIM),
    )(clip_lengths, deal_owner[None, :], deal_slot[None, :], query_rows)
    got = lax.all_to_all(
        message.reshape(plane, MSG, half_width + HEAD_DIM),
        "seq",
        split_axis=0,
        concat_axis=0,
        axis_index_groups=[list(range(c, devices, 2)) for c in range(2)],
        tiled=True,
    ).reshape(ring_rows, half_width + HEAD_DIM)

    kept, given = pl.pallas_call(
        functools.partial(split_kernel, devices),
        grid=(1,),
        in_specs=[SMEM, whole((rows, width)), whole((rows, width))],
        out_specs=[whole((rows, width))] * 2,
        out_shape=[bf16(rows, width)] * 2,
    )(mine, after(key_rows, message), value_rows)
    taken = lax.ppermute(given, "seq", to_half)
    near0 = chip_gather(kept)
    gates = jnp.take(gate_table, clip_steps, axis=0)
    got, gates = lax.optimization_barrier((got, gates))
    near1 = step(near0)
    near2 = step(near1)
    near3 = step(near2)
    far0 = chip_gather(after(taken, got))
    far1 = step(far0)
    far2 = step(far1)
    early = 10
    *queries, clips0, clips1, dead = small(
        functools.partial(unpack_kernel, devices, early),
        [SMEM, SMEM] + [whole((ring_rows, half_width + HEAD_DIM))] * 2,
        [
            bf16(2 * rows, half_width),
            bf16(2 * rows, half_width),
            bf16(early * rows, HEAD_DIM),
            bf16((plane - early) * rows, HEAD_DIM),
            bf16(4 * rows, HEAD_DIM),
        ],
    )(mine, clip_lengths, got, lax.ppermute(got, "seq", to_core))
    near4 = step(core_half(near3))
    far3 = step(far2)
    far4 = step(core_half(far3))

    state = attend(dead, queries, [kept, taken, near1, near2, far1, near3], clips0, None, False)
    own, level, sent = attend(dead, queries, [far2, far3, near4, far4], clips1, state, True)
    received = lax.ppermute(sent, "seq", to_core)

    def combine(which):
        return small(
            functools.partial(combine_kernel, devices, which == 0),
            [
                SMEM,
                SMEM,
                pl.BlockSpec((rows, half_width), lambda i: (which, 0)),
                pl.BlockSpec((rows, HEAD_DIM), lambda i: (which, 0)),
                pl.BlockSpec((rows, half_width + HEAD_DIM), lambda i: (which, 0)),
                whole(gates.shape),
            ],
            [bf16(rows, half_width)],
        )(mine, clip_lengths, own, level, received, gates)[0]

    back = lax.ppermute(combine(1), "seq", to_half)
    (out,) = small(
        functools.partial(join_kernel, devices),
        [SMEM, whole((rows, half_width)), whole((rows, half_width))],
        [bf16(rows, width)],
    )(mine, combine(0), back)
    return out


def solution(mesh):
    placed = (
        P(("dp", "seq"), "tensor"),
        P(("dp", "seq"), "tensor"),
        P(("dp", "seq"), "tensor"),
        P(("dp", "seq")),
        P(("dp", "seq")),
        P("dp"),
        P("dp"),
        P(None, "tensor"),
    )
    return jax.shard_map(
        shards, mesh=mesh, in_specs=placed, out_specs=P(("dp", "seq"), "tensor"), check_vma=False
    )
```

time: 710 us -> 108 us (0.15)
  the two profiles are of different devices: /device:TPU:454 before, /device:TPU:90 now
where the time goes in v2:
time: 108 us; the launch traced here: 107 us
  starting transfers between devices  62.7 us (58%)
  waiting for transfers between devices  20.7 us (19%)
  Pallas kernels  16 us (15%)
  blocking collectives  4.37 us (4%)
  local copies, waits for them, and re-layouts  3.13 us (3%)
    ppermute x8, starting transfers between devices, step(): return lax.ppermute(block, 'seq', to_next)  34.5 us
    all_to_all x1, starting transfers between devices, shards(): lax.all_to_all(message.reshape(plane, MSG, half_width + HEAD_DIM), 'seq',...  15 us
    ppermute x1, waiting for transfers between devices, shards(): back = lax.ppermute(combine(1), 'seq', to_half)  9.98 us
    ppermute x1, starting transfers between devices, shards(): taken = lax.ppermute(given, 'seq', to_half)  7.4 us
    pallas_call x2, Pallas kernels, attend(): pl.pallas_call(functools.partial(attend_kernel, sizes, first, last), grid...  7.17 us
    ppermute x1, waiting for transfers between devices, shards(): taken = lax.ppermute(given, 'seq', to_half)  6.39 us
    all_gather x2, blocking collectives, chip_gather(): return lax.all_gather(block, 'seq', axis_index_groups=chips, tiled=True)  4.37 us
    ppermute x8, waiting for transfers between devices, step(): return lax.ppermute(block, 'seq', to_next)  2.8 us
  transfers between devices with their start and end apart: 13, of which 5 were waited for; matrix products, arithmetic and copies ran while one was open for 2% of the time, Pallas kernels for 9%

profile of v2, /device:TPU:90, one launch (start us, length us, event | category | flops | bytes accessed | tf_op | source)
XLA Modules:
  0.0 107.3 jit_solution(8264757075425160947)
XLA Ops:
  0.0 2.2 %shard_map.82 = bf16[384,512]{1,0:T(8,128)(2,1)} custom-call(s32[8]{0:T(128)} %lengths_ref.7, s32[1,128]{1,0:T(1,128)} %bitcast.8, s32[1,128]{1,0:T(1,128)} %bitcast.9, bf16[128,768]{1,0:T(8,128)(2,1)} %query_ref.1), custom_call_target="tpu_custom_call" | custom-call | tf_op jit(solution)/shard_map/pallas_call | solution.py:425
  2.2 15.0 %all-to-all-start = ((bf16[16,24,512]{2,1,0:T(8,128)(2,1)}), bf16[16,24,512]{2,1,0:T(8,128)(2,1)S(1)}, u32[]{:S(2)}, u32[]{:S(2)}) async-start(bf16[16,24,512]{2,1,0:T(8,128)(2,1)} %bitcast.7), calls=%async_computation | async-start | bytes 786432 | tf_op jit(solution)/shard_map/all_to_all | solution.py:432
  17.2 1.8 %shard_map.84 = (bf16[128,768]{1,0:T(8,128)(2,1)}, bf16[128,768]{1,0:T(8,128)(2,1)}) custom-call(s32[1]{0:T(128)} %bitcast.me_ref, bf16[128,768]{1,0:T(8,128)(2,1)} %key_ref, bf16[128,768]{1,0:T(8,128)(2,1)} %value_ref.1), custom_call_target="tpu_custom_call" | custom-call | tf_op jit(solution)/shard_map/pallas_call | solution.py:441
  19.0 7.4 %collective-permute-start.1 = (bf16[128,768]{1,0:T(8,128)(2,1)}, bf16[128,768]{1,0:T(8,128)(2,1)S(1)}, u32[]{:S(2)}, u32[]{:S(2)}) collective-permute-start(bf16[128,768]{1,0:T(8,128)(2,1)} %get-tuple-element.26), channel_id=1, source_target_pairs={{0,64},{4,68},{8,72},{12,76},{16,80},{20,84},{24,88},{28,92},{32,9... | collective-permute-start | bytes 589832 | tf_op jit(solution)/shard_map/ppermute | solution.py:448
  26.4 2.3 %all_gather.7 = bf16[256,768]{1,0:T(8,128)(2,1)S(1)} all-gather(bf16[128,768]{1,0:T(8,128)(2,1)} %get-tuple-element.28.refs_3_), channel_id=1, replica_groups={{0,4},{8,12},{16,20},{24,28},{32,36},{40,44},{48,52},{56,60},{64,68},{7..., dimensions={0}, use_global_device_ids=true | all-gather | bytes 589824 | tf_op jit(solution)/shard_map/all_gather | solution.py:402
  28.7 4.6 %collective-permute-start.5 = (bf16[256,768]{1,0:T(8,128)(2,1)S(1)}, bf16[256,768]{1,0:T(8,128)(2,1)S(1)}, u32[]{:S(2)}, u32[]{:S(2)}) collective-permute-start(bf16[256,768]{1,0:T(8,128)(2,1)S(1)} %all_gather.7), channel_id=1, source_target_pairs={{0,8},{4,60},{8,16},{12,4},{16,24},{20,12},{24,32},{28,20},{32,40}... | collective-permute-start | bytes 1179656 | tf_op jit(solution)/shard_map/ppermute | solution.py:399
  34.0 6.4 %collective-permute-done.1.refs_4_ = bf16[128,768]{1,0:T(8,128)(2,1)S(1)} collective-permute-done((bf16[128,768]{1,0:T(8,128)(2,1)}, bf16[128,768]{1,0:T(8,128)(2,1)S(1)}, u32[]{:S(2)}, u32[]{:S(2)}) %collective-permute-start.1) | collective-permute-done | bytes 196640 | tf_op jit(solution)/shard_map/ppermute | solution.py:448
  40.4 2.1 %all_gather.6 = bf16[256,768]{1,0:T(8,128)(2,1)S(1)} all-gather(bf16[128,768]{1,0:T(8,128)(2,1)S(1)} %collective-permute-done.1.refs_4_), channel_id=1, replica_groups={{0,4},{8,12},{16,20},{24,28},{32,36},{40,44},{48,52},{56,60},{64,68},{7..., dimensions={0}, use_global_device_ids=true | all-gather | bytes 589824 | tf_op jit(solution)/shard_map/all_gather | solution.py:402
  42.5 4.7 %collective-permute-start.2 = (bf16[256,768]{1,0:T(8,128)(2,1)S(1)}, bf16[256,768]{1,0:T(8,128)(2,1)S(1)}, u32[]{:S(2)}, u32[]{:S(2)}) collective-permute-start(bf16[256,768]{1,0:T(8,128)(2,1)S(1)} %all_gather.6), channel_id=1, source_target_pairs={{0,8},{4,60},{8,16},{12,4},{16,24},{20,12},{24,32},{28,20},{32,40}... | collective-permute-start | bytes 1179656 | tf_op jit(solution)/shard_map/ppermute | solution.py:399
  47.2 2.7 %collective-permute-start.6 = (bf16[256,768]{1,0:T(8,128)(2,1)S(1)}, bf16[256,768]{1,0:T(8,128)(2,1)}, u32[]{:S(2)}, u32[]{:S(2)}) collective-permute-start(bf16[256,768]{1,0:T(8,128)(2,1)S(1)} %collective-permute-done.5.refs_5_), channel_id=1, source_target_pairs={{0,8},{4,60},{8,16},{12,4},{16,24},{20,12},{24,32},{28,20},{32,40}... | collective-permute-start | bytes 1179656 | tf_op jit(solution)/shard_map/ppermute | solution.py:399
  50.6 1.8 %collective-permute-done.2.refs_7_ = bf16[256,768]{1,0:T(8,128)(2,1)S(1)} collective-permute-done((bf16[256,768]{1,0:T(8,128)(2,1)S(1)}, bf16[256,768]{1,0:T(8,128)(2,1)S(1)}, u32[]{:S(2)}, u32[]{:S(2)}) %collective-permute-start.2) | collective-permute-done | bytes 393248 | tf_op jit(solution)/shard_map/ppermute | solution.py:399
  52.4 5.6 %collective-permute-start.3 = (bf16[256,768]{1,0:T(8,128)(2,1)S(1)}, bf16[256,768]{1,0:T(8,128)(2,1)S(1)}, u32[]{:S(2)}, u32[]{:S(2)}) collective-permute-start(bf16[256,768]{1,0:T(8,128)(2,1)S(1)} %collective-permute-done.2.refs_7_), channel_id=1, source_target_pairs={{0,8},{4,60},{8,16},{12,4},{16,24},{20,12},{24,32},{28,20},{32,40}... | collective-permute-start | bytes 1179656 | tf_op jit(solution)/shard_map/ppermute | solution.py:399
  58.8 3.6 %collective-permute-start.7 = (bf16[256,768]{1,0:T(8,128)(2,1)}, bf16[256,768]{1,0:T(8,128)(2,1)}, u32[]{:S(2)}, u32[]{:S(2)}) collective-permute-start(bf16[256,768]{1,0:T(8,128)(2,1)} %collective-permute-done.6.refs_6_), channel_id=1, source_target_pairs={{0,8},{4,60},{8,16},{12,4},{16,24},{20,12},{24,32},{28,20},{32,40}... | collective-permute-start | bytes 1179656 | tf_op jit(solution)/shard_map/ppermute | solution.py:399
  63.3 5.6 %collective-permute-start.4 = (bf16[256,768]{1,0:T(8,128)(2,1)S(1)}, bf16[256,768]{1,0:T(8,128)(2,1)S(1)}, u32[]{:S(2)}, u32[]{:S(2)}) collective-permute-start(bf16[256,768]{1,0:T(8,128)(2,1)S(1)} %collective-permute-done.3.refs_3_), channel_id=1, source_target_pairs={{0,8},{4,60},{8,16},{12,4},{16,24},{20,12},{24,32},{28,20},{32,40}... | collective-permute-start | bytes 1179656 | tf_op jit(solution)/shard_map/ppermute | solution.py:399
  68.9 1.9 %collective-permute-start = (bf16[384,512]{1,0:T(8,128)(2,1)S(1)}, bf16[384,512]{1,0:T(8,128)(2,1)S(1)}, u32[]{:S(2)}, u32[]{:S(2)}) collective-permute-start(bf16[384,512]{1,0:T(8,128)(2,1)S(1)} %bitcast.5), channel_id=1, source_target_pairs={{0,4},{4,0},{8,12},{12,8},{16,20},{20,16},{24,28},{28,24},{32,36},... | collective-permute-start | bytes 1179656 | tf_op jit(solution)/shard_map/ppermute | solution.py:469
  71.9 2.6 %collective-permute-start.8 = (bf16[128,768]{1,0:T(8,128)(2,1)S(1)}, bf16[128,768]{1,0:T(8,128)(2,1)S(1)}, u32[]{:S(2)}, u32[]{:S(2)}) collective-permute-start(bf16[128,768]{1,0:T(8,128)(2,1)S(1)} %constant_dynamic-slice_fusion.1), channel_id=1, source_target_pairs={{0,8},{4,60},{8,16},{12,4},{16,24},{20,12},{24,32},{28,20},{32,40}... | collective-permute-start | bytes 589832 | tf_op jit(solution)/shard_map/ppermute | solution.py:399
  74.5 5.3 %collective-permute-start.9 = (bf16[128,768]{1,0:T(8,128)(2,1)S(1)}, bf16[128,768]{1,0:T(8,128)(2,1)S(1)}, u32[]{:S(2)}, u32[]{:S(2)}) collective-permute-start(bf16[128,768]{1,0:T(8,128)(2,1)S(1)} %constant_dynamic-slice_fusion), channel_id=1, source_target_pairs={{0,8},{4,60},{8,16},{12,4},{16,24},{20,12},{24,32},{28,20},{32,40}... | collective-permute-start | bytes 589832 | tf_op jit(solution)/shard_map/ppermute | solution.py:399
  79.8 2.5 %shard_map.83 = (bf16[256,384]{1,0:T(8,128)(2,1)S(1)}, bf16[256,384]{1,0:T(8,128)(2,1)S(1)}, bf16[1280,128]{1,0:T(8,128)(2,1)S(1)}, bf16[768,128]{1,0:T(8,128)(2,1)S(1)}, bf16[512,128]{1,0:T(8,128)(2,1)S(1)}) custom-call(s32[1]{0:T(128)} %bitcast.me_ref, s32[8]{0:T(128)S(1)} %copy-done.2, bf16[384,512]{1,0:T(8,128)(2,1)S(1)} %bitcast.6, ...), custom_call_target="tpu_custom_call" | custom-call | tf_op jit(solution)/shard_map/pallas_call | solution.py:459
  82.4 4.4 %shard_map.85 = (f32[512,384]{1,0:T(8,128)S(1)}, f32[512,128]{1,0:T(8,128)S(1)}) custom-call(bf16[512,128]{1,0:T(8,128)(2,1)S(1)} %get-tuple-element.22.refs_0_, bf16[256,384]{1,0:T(8,128)(2,1)S(1)} %get-tuple-element.23.refs_1_, bf16[256,384]{1,0:T(8,128)(2,1)S(1)} %get-tuple-element.24.refs_2_, bf16[128,768]{1,0:T(8,128)(2,1)S(1)} %copy-done.1, ...), custom_call_target="tpu_custom_call" | custom-call | flops 1006632960 | bytes 1966080 | tf_op jit(solution)/shard_map/pallas_call | solution.py:362
  86.8 2.8 %shard_map.86 = (f32[256,384]{1,0:T(8,128)S(1)}, f32[256,128]{1,0:T(8,128)S(1)}, bf16[256,512]{1,0:T(8,128)(2,1)S(1)}) custom-call(bf16[512,128]{1,0:T(8,128)(2,1)S(1)} %get-tuple-element.22.refs_0_, bf16[256,384]{1,0:T(8,128)(2,1)S(1)} %get-tuple-element.23.refs_1_, bf16[256,384]{1,0:T(8,128)(2,1)S(1)} %get-tuple-element.24.refs_2_, ...), custom_call_target="tpu_custom_call" | custom-call | flops 603979776 | bytes 1179648 | tf_op jit(solution)/shard_map/pallas_call | solution.py:362
  89.6 1.9 %collective-permute-start.10 = (bf16[256,512]{1,0:T(8,128)(2,1)S(1)}, bf16[256,512]{1,0:T(8,128)(2,1)S(1)}, u32[]{:S(2)}, u32[]{:S(2)}) collective-permute-start(bf16[256,512]{1,0:T(8,128)(2,1)S(1)} %get-tuple-element.35), channel_id=1, source_target_pairs={{0,4},{4,0},{8,12},{12,8},{16,20},{20,16},{24,28},{28,24},{32,36},... | collective-permute-start | bytes 786440 | tf_op jit(solution)/shard_map/ppermute | solution.py:476
  91.5 1.5 %collective-permute-done.10.got_ref = bf16[256,512]{1,0:T(8,128)(2,1)S(1)} collective-permute-done((bf16[256,512]{1,0:T(8,128)(2,1)S(1)}, bf16[256,512]{1,0:T(8,128)(2,1)S(1)}, u32[]{:S(2)}, u32[]{:S(2)}) %collective-permute-start.10) | collective-permute-done | bytes 262176 | tf_op jit(solution)/shard_map/ppermute | solution.py:476
  93.8 1.9 %collective-permute-start.11 = (bf16[128,384]{1,0:T(8,128)(2,1)S(1)}, bf16[128,384]{1,0:T(8,128)(2,1)S(1)}, u32[]{:S(2)}, u32[]{:S(2)}) collective-permute-start(bf16[128,384]{1,0:T(8,128)(2,1)S(1)} %shard_map.88), channel_id=1, source_target_pairs={{0,64},{4,68},{8,72},{12,76},{16,80},{20,84},{24,88},{28,92},{32,9... | collective-permute-start | bytes 294920 | tf_op jit(solution)/shard_map/ppermute | solution.py:492
  96.6 10.0 %collective-permute-done.11.back_ref = bf16[128,384]{1,0:T(8,128)(2,1)S(1)} collective-permute-done((bf16[128,384]{1,0:T(8,128)(2,1)S(1)}, bf16[128,384]{1,0:T(8,128)(2,1)S(1)}, u32[]{:S(2)}, u32[]{:S(2)}) %collective-permute-start.11) | collective-permute-done | bytes 98336 | tf_op jit(solution)/shard_map/ppermute | solution.py:492
  (35 shorter events, 6.5 us)
Async XLA Ops:
  0.0 33.3 %copy-start = (bf16[1000,768]{1,0:T(8,128)(2,1)S(1)}, bf16[1000,768]{1,0:T(8,128)(2,1)}, u32[]{:S(2)}) copy-start(bf16[1000,768]{1,0:T(8,128)(2,1)} %param.15) | copy-start | bytes 4608004
  0.0 33.3 %copy-start.7 = (s32[8]{0:T(128)S(1)}, s32[8]{0:T(128)}, u32[]{:S(2)}) copy-start(s32[8]{0:T(128)} %param.14) | copy-start | bytes 100
  2.2 77.6 %copy-start.2 = (s32[8]{0:T(128)S(1)}, s32[8]{0:T(128)}, u32[]{:S(2)}) copy-start(s32[8]{0:T(128)} %lengths_ref.7) | copy-start | bytes 100
  2.2 31.8 %all-to-all-start = ((bf16[16,24,512]{2,1,0:T(8,128)(2,1)}), bf16[16,24,512]{2,1,0:T(8,128)(2,1)S(1)}, u32[]{:S(2)}, u32[]{:S(2)}) async-start(bf16[16,24,512]{2,1,0:T(8,128)(2,1)} %bitcast.7), calls=%async_computation | async-start | bytes 786432 | tf_op jit(solution)/shard_map/all_to_all | solution.py:432
  19.0 63.3 %copy-start.1 = (bf16[128,768]{1,0:T(8,128)(2,1)S(1)}, bf16[128,768]{1,0:T(8,128)(2,1)}, u32[]{:S(2)}) copy-start(bf16[128,768]{1,0:T(8,128)(2,1)} %get-tuple-element.28.refs_3_) | copy-start | bytes 589828
  19.0 21.4 %collective-permute-start.1 = (bf16[128,768]{1,0:T(8,128)(2,1)}, bf16[128,768]{1,0:T(8,128)(2,1)S(1)}, u32[]{:S(2)}, u32[]{:S(2)}) collective-permute-start(bf16[128,768]{1,0:T(8,128)(2,1)} %get-tuple-element.26), channel_id=1, source_target_pairs={{0,64},{4,68},{8,72},{12,76},{16,80},{20,84},{24,88},{28,92},{32,9... | collective-permute-start | bytes 589832 | tf_op jit(solution)/shard_map/ppermute | solution.py:448
  28.7 18.4 %collective-permute-start.5 = (bf16[256,768]{1,0:T(8,128)(2,1)S(1)}, bf16[256,768]{1,0:T(8,128)(2,1)S(1)}, u32[]{:S(2)}, u32[]{:S(2)}) collective-permute-start(bf16[256,768]{1,0:T(8,128)(2,1)S(1)} %all_gather.7), channel_id=1, source_target_pairs={{0,8},{4,60},{8,16},{12,4},{16,24},{20,12},{24,32},{28,20},{32,40}... | collective-permute-start | bytes 1179656 | tf_op jit(solution)/shard_map/ppermute | solution.py:399
  42.5 10.0 %collective-permute-start.2 = (bf16[256,768]{1,0:T(8,128)(2,1)S(1)}, bf16[256,768]{1,0:T(8,128)(2,1)S(1)}, u32[]{:S(2)}, u32[]{:S(2)}) collective-permute-start(bf16[256,768]{1,0:T(8,128)(2,1)S(1)} %all_gather.6), channel_id=1, source_target_pairs={{0,8},{4,60},{8,16},{12,4},{16,24},{20,12},{24,32},{28,20},{32,40}... | collective-permute-start | bytes 1179656 | tf_op jit(solution)/shard_map/ppermute | solution.py:399
  47.2 11.6 %collective-permute-start.6 = (bf16[256,768]{1,0:T(8,128)(2,1)S(1)}, bf16[256,768]{1,0:T(8,128)(2,1)}, u32[]{:S(2)}, u32[]{:S(2)}) collective-permute-start(bf16[256,768]{1,0:T(8,128)(2,1)S(1)} %collective-permute-done.5.refs_5_), channel_id=1, source_target_pairs={{0,8},{4,60},{8,16},{12,4},{16,24},{20,12},{24,32},{28,20},{32,40}... | collective-permute-start | bytes 1179656 | tf_op jit(solution)/shard_map/ppermute | solution.py:399
  49.8 0.8 copy-start.3
  52.4 10.9 %collective-permute-start.3 = (bf16[256,768]{1,0:T(8,128)(2,1)S(1)}, bf16[256,768]{1,0:T(8,128)(2,1)S(1)}, u32[]{:S(2)}, u32[]{:S(2)}) collective-permute-start(bf16[256,768]{1,0:T(8,128)(2,1)S(1)} %collective-permute-done.2.refs_7_), channel_id=1, source_target_pairs={{0,8},{4,60},{8,16},{12,4},{16,24},{20,12},{24,32},{28,20},{32,40}... | collective-permute-start | bytes 1179656 | tf_op jit(solution)/shard_map/ppermute | solution.py:399
  58.0 0.7 copy-start.5
  58.8 12.1 %collective-permute-start.7 = (bf16[256,768]{1,0:T(8,128)(2,1)}, bf16[256,768]{1,0:T(8,128)(2,1)}, u32[]{:S(2)}, u32[]{:S(2)}) collective-permute-start(bf16[256,768]{1,0:T(8,128)(2,1)} %collective-permute-done.6.refs_6_), channel_id=1, source_target_pairs={{0,8},{4,60},{8,16},{12,4},{16,24},{20,12},{24,32},{28,20},{32,40}... | collective-permute-start | bytes 1179656 | tf_op jit(solution)/shard_map/ppermute | solution.py:399
  63.3 11.2 %collective-permute-start.4 = (bf16[256,768]{1,0:T(8,128)(2,1)S(1)}, bf16[256,768]{1,0:T(8,128)(2,1)S(1)}, u32[]{:S(2)}, u32[]{:S(2)}) collective-permute-start(bf16[256,768]{1,0:T(8,128)(2,1)S(1)} %collective-permute-done.3.refs_3_), channel_id=1, source_target_pairs={{0,8},{4,60},{8,16},{12,4},{16,24},{20,12},{24,32},{28,20},{32,40}... | collective-permute-start | bytes 1179656 | tf_op jit(solution)/shard_map/ppermute | solution.py:399
  68.9 10.9 %collective-permute-start = (bf16[384,512]{1,0:T(8,128)(2,1)S(1)}, bf16[384,512]{1,0:T(8,128)(2,1)S(1)}, u32[]{:S(2)}, u32[]{:S(2)}) collective-permute-start(bf16[384,512]{1,0:T(8,128)(2,1)S(1)} %bitcast.5), channel_id=1, source_target_pairs={{0,4},{4,0},{8,12},{12,8},{16,20},{20,16},{24,28},{28,24},{32,36},... | collective-permute-start | bytes 1179656 | tf_op jit(solution)/shard_map/ppermute | solution.py:469
  70.8 11.5 %copy-start.4 = (bf16[256,768]{1,0:T(8,128)(2,1)S(1)}, bf16[256,768]{1,0:T(8,128)(2,1)}, u32[]{:S(2)}) copy-start(bf16[256,768]{1,0:T(8,128)(2,1)} %copy-done.3) | copy-start | bytes 1179652
  70.8 11.5 %copy-start.6 = (bf16[256,768]{1,0:T(8,128)(2,1)S(1)}, bf16[256,768]{1,0:T(8,128)(2,1)}, u32[]{:S(2)}) copy-start(bf16[256,768]{1,0:T(8,128)(2,1)} %copy-done.5) | copy-start | bytes 1179652
  71.9 14.9 %collective-permute-start.8 = (bf16[128,768]{1,0:T(8,128)(2,1)S(1)}, bf16[128,768]{1,0:T(8,128)(2,1)S(1)}, u32[]{:S(2)}, u32[]{:S(2)}) collective-permute-start(bf16[128,768]{1,0:T(8,128)(2,1)S(1)} %constant_dynamic-slice_fusion.1), channel_id=1, source_target_pairs={{0,8},{4,60},{8,16},{12,4},{16,24},{20,12},{24,32},{28,20},{32,40}... | collective-permute-start | bytes 589832 | tf_op jit(solution)/shard_map/ppermute | solution.py:399
  74.5 12.3 %collective-permute-start.9 = (bf16[128,768]{1,0:T(8,128)(2,1)S(1)}, bf16[128,768]{1,0:T(8,128)(2,1)S(1)}, u32[]{:S(2)}, u32[]{:S(2)}) collective-permute-start(bf16[128,768]{1,0:T(8,128)(2,1)S(1)} %constant_dynamic-slice_fusion), channel_id=1, source_target_pairs={{0,8},{4,60},{8,16},{12,4},{16,24},{20,12},{24,32},{28,20},{32,40}... | collective-permute-start | bytes 589832 | tf_op jit(solution)/shard_map/ppermute | solution.py:399
  89.6 3.4 %collective-permute-start.10 = (bf16[256,512]{1,0:T(8,128)(2,1)S(1)}, bf16[256,512]{1,0:T(8,128)(2,1)S(1)}, u32[]{:S(2)}, u32[]{:S(2)}) collective-permute-start(bf16[256,512]{1,0:T(8,128)(2,1)S(1)} %get-tuple-element.35), channel_id=1, source_target_pairs={{0,4},{4,0},{8,12},{12,8},{16,20},{20,16},{24,28},{28,24},{32,36},... | collective-permute-start | bytes 786440 | tf_op jit(solution)/shard_map/ppermute | solution.py:476
  93.8 12.7 %collective-permute-start.11 = (bf16[128,384]{1,0:T(8,128)(2,1)S(1)}, bf16[128,384]{1,0:T(8,128)(2,1)S(1)}, u32[]{:S(2)}, u32[]{:S(2)}) collective-permute-start(bf16[128,384]{1,0:T(8,128)(2,1)S(1)} %shard_map.88), channel_id=1, source_target_pairs={{0,64},{4,68},{8,72},{12,76},{16,80},{20,84},{24,88},{28,92},{32,9... | collective-permute-start | bytes 294920 | tf_op jit(solution)/shard_map/ppermute | solution.py:492

commit v3 on v2

--- a/solution.py
+++ b/solution.py
@@ -14,7 +14,7 @@
 BOUND = 6
 MSG = 24
 CHUNK = 256
-ATTEND_VMEM = 24 * 1024 * 1024
+ATTEND_VMEM = 30 * 1024 * 1024
 SMALL_VMEM = 10 * 1024 * 1024
 
 NN = (((1,), (0,)), ((), ()))
@@ -118,24 +118,23 @@
 
     near, far = half, 1 - half
     order = [me, lax.rem(me + plane, devices)]
-    for h, distance in ((near, 1), (near, 2), (far, 1), (near, 3), (far, 2), (far, 3)):
+    for h, distance in ((near, 1), (far, 1), (near, 2), (far, 2), (near, 3), (far, 3)):
         order += pair(h, distance)
     return order + [pair(near, 4)[0] + core, pair(far, 4)[0] + core]
 
 
 def unpack_kernel(
     devices,
-    early,
+    counts,
     me_ref,
     lengths_ref,
     got_ref,
     other_ref,
     query_ref,
     other_query_ref,
-    clips0_ref,
-    clips1_ref,
-    dead_ref,
+    *refs,
 ):
+    *clip_refs, dead_ref = refs
     each = got_ref.shape[0]
     lines = 2 * each
     rows = HEAD_DIM
@@ -174,10 +173,11 @@
     for j in range(slots):
         member = (ids[j : j + 1, :] == down).astype(jnp.bfloat16)
         clips = dot(unit(rows), member, NT).astype(jnp.bfloat16)
-        if j < early:
-            clips0_ref[j * rows : (j + 1) * rows, :] = clips
-        else:
-            clips1_ref[(j - early) * rows : (j + 1 - early) * rows, :] = clips
+        call = 0
+        while j >= sum(counts[: call + 1]):
+            call += 1
+        at = (j - sum(counts[:call])) * rows
+        clip_refs[call][at : at + rows, :] = clips
 
     bounds = clip_bounds(lengths_ref)
     other = lax.rem(me + plane, devices)
@@ -292,12 +292,14 @@
 
 
 def combine_kernel(
-    devices, mine, me_ref, lengths_ref, own_ref, level_ref, got_ref, gates_ref, out_ref
+    devices, which, me_ref, lengths_ref, own_ref, level_ref, got_ref, gates_ref, out_ref
 ):
     rows, width = own_ref.shape
     me = me_ref[0]
-    half = place_of(me, devices)[0]
-    owner = me if mine else lax.rem(me + devices // 2, devices)
+    half, _, core = place_of(me, devices)
+    owner = lax.rem(me + which * (devices // 2), devices)
+    other = pl.multiple_of((1 - core) * 2 * rows + which * rows, rows)
+    got = got_ref[pl.ds(other, rows), :]
     lane = iota((rows, HEAD_DIM), 1)
     position = iota((rows, HEAD_DIM), 0) + owner * rows
     member = jnp.zeros((rows, HEAD_DIM), jnp.float32)
@@ -306,14 +308,14 @@
         member = jnp.where((lane == c) & inside, 1.0, member)
     gates = jnp.where(half == 0, gates_ref[:, :width], gates_ref[:, width:])
     gate = dot(member[:, : gates.shape[0]].astype(jnp.bfloat16), gates)
-    stat = got_ref[:, width:].astype(jnp.float32)
+    stat = got[:, width:].astype(jnp.float32)
     for h in range(width // HEAD_DIM):
         got_level = (stat[:, h : h + 1] + stat[:, h + 8 : h + 9]) + stat[:, h + 16 : h + 17]
         gap = level_ref[:, h : h + 1] - got_level
         own_share = 1.0 / (1.0 + jnp.exp2(-gap))
         got_share = 1.0 / (1.0 + jnp.exp2(gap))
         at = slice(h * HEAD_DIM, (h + 1) * HEAD_DIM)
-        mixed = own_ref[:, at] * own_share + got_ref[:, at].astype(jnp.float32) * got_share
+        mixed = own_ref[:, at] * own_share + got[:, at].astype(jnp.float32) * got_share
         out_ref[:, at] = (mixed * gate[:, at]).astype(jnp.bfloat16)
 
 
@@ -340,7 +342,30 @@
     return pl.BlockSpec(shape, lambda i: (0,) * len(shape))
 
 
-def attend(dead, queries, blocks, clips, state, last):
+def call(kernel, operands, in_specs, outs, behind=(), scratch=(), vmem=None, token=False):
+    taken, extra = len(operands), len(behind)
+
+    def body(*refs):
+        ins, rest = refs[:taken], list(refs[taken + extra :])
+        if token:
+            done = rest.pop(len(outs))
+            done[...] = jnp.zeros(done.shape, done.dtype)
+        kernel(*ins, *rest)
+
+    results = list(outs) + ([jax.ShapeDtypeStruct((8, HEAD_DIM), jnp.float32)] if token else [])
+    return pl.pallas_call(
+        body,
+        grid=(1,),
+        in_specs=list(in_specs) + [pl.BlockSpec(memory_space=pl.ANY)] * extra,
+        out_specs=[whole(o.shape) for o in results],
+        out_shape=results,
+        scratch_shapes=scratch,
+        compiler_params=pltpu.CompilerParams(vmem_limit_bytes=vmem),
+        cost_estimate=pl.CostEstimate(flops=0, bytes_accessed=0, transcendentals=0),
+    )(*operands, *behind)
+
+
+def attend(dead, queries, blocks, clips, state, last, token=False, behind=()):
     tile, width = queries[0].shape
     heads = width // HEAD_DIM
     sizes = [b.shape[0] for b in blocks]
@@ -349,30 +374,26 @@
     first = state is None
     operands = [dead, *queries, *blocks, clips] + ([] if first else list(state))
     if last:
-        out_shape = [
+        outs = [
             jax.ShapeDtypeStruct((tile, width), jnp.float32),
             jax.ShapeDtypeStruct((tile, HEAD_DIM), jnp.float32),
             jax.ShapeDtypeStruct((tile, width + HEAD_DIM), jnp.bfloat16),
         ]
     else:
-        out_shape = [
+        outs = [
             jax.ShapeDtypeStruct((rows, width), jnp.float32),
             jax.ShapeDtypeStruct((rows, HEAD_DIM), jnp.float32),
         ]
-    return pl.pallas_call(
+    return call(
         functools.partial(attend_kernel, sizes, first, last),
-        grid=(1,),
-        in_specs=[whole(o.shape) for o in operands],
-        out_specs=[whole(o.shape) for o in out_shape],
-        out_shape=out_shape,
-        scratch_shapes=[pltpu.VMEM((2 * heads, tile, keys), jnp.float32)],
-        compiler_params=pltpu.CompilerParams(vmem_limit_bytes=ATTEND_VMEM),
-        cost_estimate=pl.CostEstimate(
-            flops=4 * rows * keys * width,
-            bytes_accessed=4 * keys * width,
-            transcendentals=rows * keys * heads,
-        ),
-    )(*operands)
+        operands,
+        [whole(o.shape) for o in operands],
+        outs,
+        behind,
+        [pltpu.VMEM((2 * heads, tile, keys), jnp.float32)],
+        ATTEND_VMEM,
+        token,
+    )
 
 
 def shards(
@@ -404,98 +425,90 @@
     def core_half(block):
         return lax.dynamic_slice_in_dim(block, core * rows, rows, axis=0)
 
-    def small(kernel, in_specs, outs):
-        return pl.pallas_call(
-            kernel,
-            grid=(1,),
-            in_specs=in_specs,
-            out_specs=[whole(o.shape) for o in outs],
-            out_shape=outs,
-            compiler_params=pltpu.CompilerParams(vmem_limit_bytes=SMALL_VMEM),
-        )
-
     def bf16(*shape):
         return jax.ShapeDtypeStruct(shape, jnp.bfloat16)
 
-    def after(value, *others):
-        return lax.optimization_barrier((value, *others))[0]
-
     mine = me[None]
-    ring_rows = plane * MSG
-    message = pl.pallas_call(
+    sent_rows = plane * MSG
+    sent_width = half_width + HEAD_DIM
+    kept, given = call(
+        functools.partial(split_kernel, devices),
+        [mine, key_rows, value_rows],
+        [SMEM, whole((rows, width)), whole((rows, width))],
+        [bf16(rows, width)] * 2,
+    )
+    taken = lax.ppermute(given, "seq", to_half)
+    near0 = chip_gather(kept)
+    (message,) = call(
         functools.partial(pack_kernel, plane),
-        grid=(1,),
-        in_specs=[SMEM, whole((1, rows)), whole((1, rows)), whole((rows, width))],
-        out_specs=whole((ring_rows, half_width + HEAD_DIM)),
-        out_shape=bf16(ring_rows, half_width + HEAD_DIM),
-    )(clip_lengths, deal_owner[None, :], deal_slot[None, :], query_rows)
+        [clip_lengths, deal_owner[None, :], deal_slot[None, :], query_rows],
+        [SMEM, whole((1, rows)), whole((1, rows)), whole((rows, width))],
+        [bf16(sent_rows, sent_width)],
+        [near0],
+    )
     got = lax.all_to_all(
-        message.reshape(plane, MSG, half_width + HEAD_DIM),
+        message.reshape(plane, MSG, sent_width),
         "seq",
         split_axis=0,
         concat_axis=0,
         axis_index_groups=[list(range(c, devices, 2)) for c in range(2)],
         tiled=True,
-    ).reshape(ring_rows, half_width + HEAD_DIM)
-
-    kept, given = pl.pallas_call(
-        functools.partial(split_kernel, devices),
-        grid=(1,),
-        in_specs=[SMEM, whole((rows, width)), whole((rows, width))],
-        out_specs=[whole((rows, width))] * 2,
-        out_shape=[bf16(rows, width)] * 2,
-    )(mine, after(key_rows, message), value_rows)
-    taken = lax.ppermute(given, "seq", to_half)
-    near0 = chip_gather(kept)
+    ).reshape(sent_rows, sent_width)
+
+    near1 = step(near0)
+    far1 = step(chip_gather(taken))
+    near2 = step(near1)
+    far2 = step(far1)
+    near2, got = lax.optimization_barrier((near2, got))
+    near3 = step(near2)
+    far3 = step(far2)
+    near4 = step(core_half(near3))
     gates = jnp.take(gate_table, clip_steps, axis=0)
-    got, gates = lax.optimization_barrier((got, gates))
-    near1 = step(near0)
-    near2 = step(near1)
-    near3 = step(near2)
-    far0 = chip_gather(after(taken, got))
-    far1 = step(far0)
-    far2 = step(far1)
-    early = 10
-    *queries, clips0, clips1, dead = small(
-        functools.partial(unpack_kernel, devices, early),
-        [SMEM, SMEM] + [whole((ring_rows, half_width + HEAD_DIM))] * 2,
-        [
-            bf16(2 * rows, half_width),
-            bf16(2 * rows, half_width),
-            bf16(early * rows, HEAD_DIM),
-            bf16((plane - early) * rows, HEAD_DIM),
-            bf16(4 * rows, HEAD_DIM),
-        ],
-    )(mine, clip_lengths, got, lax.ppermute(got, "seq", to_core))
-    near4 = step(core_half(near3))
-    far3 = step(far2)
-    far4 = step(core_half(far3))
-
-    state = attend(dead, queries, [kept, taken, near1, near2, far1, near3], clips0, None, False)
-    own, level, sent = attend(dead, queries, [far2, far3, near4, far4], clips1, state, True)
-    received = lax.ppermute(sent, "seq", to_core)
+    counts = (12, 4)
+    *queries, clips0, clips1, dead, unpacked = call(
+        functools.partial(unpack_kernel, devices, counts),
+        [mine, clip_lengths, got, lax.ppermute(got, "seq", to_core)],
+        [SMEM, SMEM] + [whole((sent_rows, sent_width))] * 2,
+        [bf16(2 * rows, half_width)] * 2
+        + [bf16(c * rows, HEAD_DIM) for c in counts]
+        + [bf16(4 * rows, HEAD_DIM)],
+        [gates],
+        vmem=SMALL_VMEM,
+        token=True,
+    )
+    half3, unpacked = lax.optimization_barrier((core_half(far3), unpacked))
+    far4 = step(half3)
+    blocks = [kept, taken, near1, far1, near2, far2, near3]
+    state = attend(dead, queries, blocks, clips0, None, False)
+    own, level, sent = attend(
+        dead, queries, [far3, near4, far4], clips1, state, True, behind=[unpacked]
+    )
+    received = chip_gather(sent)
 
     def combine(which):
-        return small(
-            functools.partial(combine_kernel, devices, which == 0),
+        return call(
+            functools.partial(combine_kernel, devices, which),
+            [mine, clip_lengths, own, level, received, gates],
             [
                 SMEM,
                 SMEM,
                 pl.BlockSpec((rows, half_width), lambda i: (which, 0)),
                 pl.BlockSpec((rows, HEAD_DIM), lambda i: (which, 0)),
-                pl.BlockSpec((rows, half_width + HEAD_DIM), lambda i: (which, 0)),
+                whole((4 * rows, sent_width)),
                 whole(gates.shape),
             ],
             [bf16(rows, half_width)],
-        )(mine, clip_lengths, own, level, received, gates)[0]
+            vmem=SMALL_VMEM,
+        )[0]
 
     back = lax.ppermute(combine(1), "seq", to_half)
-    (out,) = small(
+    return call(
         functools.partial(join_kernel, devices),
+        [mine, combine(0), back],
         [SMEM, whole((rows, half_width)), whole((rows, half_width))],
         [bf16(rows, width)],
-    )(mine, combine(0), back)
-    return out
+        vmem=SMALL_VMEM,
+    )[0]
 
 
 def solution(mesh):

time: 108 us -> 93.6 us (0.87)
  the two profiles are of different devices: /device:TPU:90 before, /device:TPU:1 now
where the time goes in v3:
time: 93.6 us; the launch traced here: 92.1 us
  starting transfers between devices  55.4 us (59%)
  Pallas kernels  17.2 us (18%)
  blocking collectives  9.87 us (11%)
  waiting for transfers between devices  7.05 us (8%)
  local copies, waits for them, and re-layouts  2.13 us (2%)
    ppermute x8, starting transfers between devices, step(): return lax.ppermute(block, 'seq', to_next)  30.1 us
    pallas_call x8, Pallas kernels, call(): pl.pallas_call(body, grid=(1,), in_specs=list(in_specs) + [pl.BlockSpec(m...  17.2 us
    ppermute x1, starting transfers between devices, shards(): taken = lax.ppermute(given, 'seq', to_half)  11.6 us
    all_gather x3, blocking collectives, chip_gather(): return lax.all_gather(block, 'seq', axis_index_groups=chips, tiled=True)  9.87 us
    ppermute x1, starting transfers between devices, shards(): back = lax.ppermute(combine(1), 'seq', to_half)  7 us
    ppermute x8, waiting for transfers between devices, step(): return lax.ppermute(block, 'seq', to_next)  5.08 us
    all_to_all x1, starting transfers between devices, shards(): lax.all_to_all(message.reshape(plane, MSG, sent_width), 'seq', split_axis...  4.15 us
    ppermute x1, starting transfers between devices, shards(): lax.ppermute(got, 'seq', to_core)  2.55 us
  transfers between devices with their start and end apart: 12, of which 3 were waited for; matrix products, arithmetic and copies ran while one was open for 1% of the time, Pallas kernels for 12%

profile of v3, /device:TPU:1, one launch (start us, length us, event | category | flops | bytes accessed | tf_op | source)
XLA Modules:
  0.0 92.1 jit_solution(528436631972575002)
XLA Ops:
  0.0 1.9 %shard_map.82 = (bf16[128,768]{1,0:T(8,128)(2,1)}, bf16[128,768]{1,0:T(8,128)(2,1)}) custom-call(s32[1]{0:T(128)} %bitcast.refs_0_, bf16[128,768]{1,0:T(8,128)(2,1)} %refs_1_.4, bf16[128,768]{1,0:T(8,128)(2,1)} %refs_2_.1), custom_call_target="tpu_custom_call" | custom-call | tf_op jit(solution)/shard_map/pallas_call | solution.py:356
  1.9 11.6 %collective-permute-start.3 = (bf16[128,768]{1,0:T(8,128)(2,1)}, bf16[128,768]{1,0:T(8,128)(2,1)S(1)}, u32[]{:S(2)}, u32[]{:S(2)}) collective-permute-start(bf16[128,768]{1,0:T(8,128)(2,1)} %get-tuple-element.27), channel_id=1, source_target_pairs={{0,64},{4,68},{8,72},{12,76},{16,80},{20,84},{24,88},{28,92},{32,9... | collective-permute-start | bytes 589832 | tf_op jit(solution)/shard_map/ppermute | solution.py:440
  13.5 2.9 %all_gather.9.refs_4_ = bf16[256,768]{1,0:T(8,128)(2,1)S(1)} all-gather(bf16[128,768]{1,0:T(8,128)(2,1)} %get-tuple-element.22.refs_3_), channel_id=1, replica_groups={{0,4},{8,12},{16,20},{24,28},{32,36},{40,44},{48,52},{56,60},{64,68},{7..., dimensions={0}, use_global_device_ids=true | all-gather | bytes 589824 | tf_op jit(solution)/shard_map/all_gather | solution.py:423
  16.4 5.2 %collective-permute-start = (bf16[256,768]{1,0:T(8,128)(2,1)S(1)}, bf16[256,768]{1,0:T(8,128)(2,1)S(1)}, u32[]{:S(2)}, u32[]{:S(2)}) collective-permute-start(bf16[256,768]{1,0:T(8,128)(2,1)S(1)} %all_gather.9.refs_4_), channel_id=1, source_target_pairs={{0,8},{4,60},{8,16},{12,4},{16,24},{20,12},{24,32},{28,20},{32,40}... | collective-permute-start | bytes 1179656 | tf_op jit(solution)/shard_map/ppermute | solution.py:420
  21.6 2.1 %shard_map.83 = bf16[384,512]{1,0:T(8,128)(2,1)} custom-call(s32[8]{0:T(128)} %refs_1_.7, s32[1,128]{1,0:T(1,128)} %bitcast.8, s32[1,128]{1,0:T(1,128)} %bitcast.9, bf16[128,768]{1,0:T(8,128)(2,1)} %refs_3_.1, bf16[256,768]{1,0:T(8,128)(2,1)} %copy-done.7), custom_call_target="tpu_custom_call" | custom-call | tf_op jit(solution)/shard_map/pallas_call | solution.py:356
  23.7 4.1 %all-to-all-start = ((bf16[16,24,512]{2,1,0:T(8,128)(2,1)}), bf16[16,24,512]{2,1,0:T(8,128)(2,1)S(1)}, u32[]{:S(2)}, u32[]{:S(2)}) async-start(bf16[16,24,512]{2,1,0:T(8,128)(2,1)} %bitcast.7), calls=%async_computation | async-start | bytes 786432 | tf_op jit(solution)/shard_map/all_to_all | solution.py:449
  27.9 2.8 %all_gather.10 = bf16[256,768]{1,0:T(8,128)(2,1)S(1)} all-gather(bf16[128,768]{1,0:T(8,128)(2,1)S(1)} %collective-permute-done.3.refs_4_), channel_id=1, replica_groups={{0,4},{8,12},{16,20},{24,28},{32,36},{40,44},{48,52},{56,60},{64,68},{7..., dimensions={0}, use_global_device_ids=true | all-gather | bytes 589824 | tf_op jit(solution)/shard_map/all_gather | solution.py:423
  30.6 4.8 %collective-permute-start.4 = (bf16[256,768]{1,0:T(8,128)(2,1)S(1)}, bf16[256,768]{1,0:T(8,128)(2,1)S(1)}, u32[]{:S(2)}, u32[]{:S(2)}) collective-permute-start(bf16[256,768]{1,0:T(8,128)(2,1)S(1)} %all_gather.10), channel_id=1, source_target_pairs={{0,8},{4,60},{8,16},{12,4},{16,24},{20,12},{24,32},{28,20},{32,40}... | collective-permute-start | bytes 1179656 | tf_op jit(solution)/shard_map/ppermute | solution.py:420
  35.4 3.1 %collective-permute-start.1 = (bf16[256,768]{1,0:T(8,128)(2,1)S(1)}, bf16[256,768]{1,0:T(8,128)(2,1)S(1)}, u32[]{:S(2)}, u32[]{:S(2)}) collective-permute-start(bf16[256,768]{1,0:T(8,128)(2,1)S(1)} %collective-permute-done.refs_5_), channel_id=1, source_target_pairs={{0,8},{4,60},{8,16},{12,4},{16,24},{20,12},{24,32},{28,20},{32,40}... | collective-permute-start | bytes 1179656 | tf_op jit(solution)/shard_map/ppermute | solution.py:420
  38.5 4.8 %collective-permute-done.4.refs_6_ = bf16[256,768]{1,0:T(8,128)(2,1)S(1)} collective-permute-done((bf16[256,768]{1,0:T(8,128)(2,1)S(1)}, bf16[256,768]{1,0:T(8,128)(2,1)S(1)}, u32[]{:S(2)}, u32[]{:S(2)}) %collective-permute-start.4) | collective-permute-done | bytes 393248 | tf_op jit(solution)/shard_map/ppermute | solution.py:420
  43.3 3.2 %collective-permute-start.5 = (bf16[256,768]{1,0:T(8,128)(2,1)S(1)}, bf16[256,768]{1,0:T(8,128)(2,1)}, u32[]{:S(2)}, u32[]{:S(2)}) collective-permute-start(bf16[256,768]{1,0:T(8,128)(2,1)S(1)} %collective-permute-done.4.refs_6_), channel_id=1, source_target_pairs={{0,8},{4,60},{8,16},{12,4},{16,24},{20,12},{24,32},{28,20},{32,40}... | collective-permute-start | bytes 1179656 | tf_op jit(solution)/shard_map/ppermute | solution.py:420
  48.2 2.9 %collective-permute-start.7 = (bf16[256,768]{1,0:T(8,128)(2,1)}, bf16[256,768]{1,0:T(8,128)(2,1)S(1)}, u32[]{:S(2)}, u32[]{:S(2)}) collective-permute-start(bf16[256,768]{1,0:T(8,128)(2,1)} %copy-done.4), channel_id=1, source_target_pairs={{0,8},{4,60},{8,16},{12,4},{16,24},{20,12},{24,32},{28,20},{32,40}... | collective-permute-start | bytes 1179656 | tf_op jit(solution)/shard_map/ppermute | solution.py:420
  51.1 2.6 %collective-permute-start.2 = (bf16[384,512]{1,0:T(8,128)(2,1)S(1)}, bf16[384,512]{1,0:T(8,128)(2,1)}, u32[]{:S(2)}, u32[]{:S(2)}) collective-permute-start(bf16[384,512]{1,0:T(8,128)(2,1)S(1)} %bitcast.5), channel_id=1, source_target_pairs={{0,4},{4,0},{8,12},{12,8},{16,20},{20,16},{24,28},{28,24},{32,36},... | collective-permute-start | bytes 1179656 | tf_op jit(solution)/shard_map/ppermute | solution.py:470
  53.7 4.9 %collective-permute-start.6 = (bf16[256,768]{1,0:T(8,128)(2,1)}, bf16[256,768]{1,0:T(8,128)(2,1)S(1)}, u32[]{:S(2)}, u32[]{:S(2)}) collective-permute-start(bf16[256,768]{1,0:T(8,128)(2,1)} %collective-permute-done.5.refs_8_), channel_id=1, source_target_pairs={{0,8},{4,60},{8,16},{12,4},{16,24},{20,12},{24,32},{28,20},{32,40}... | collective-permute-start | bytes 1179656 | tf_op jit(solution)/shard_map/ppermute | solution.py:420
  59.3 2.3 %collective-permute-start.8 = (bf16[128,768]{1,0:T(8,128)(2,1)S(1)}, bf16[128,768]{1,0:T(8,128)(2,1)S(1)}, u32[]{:S(2)}, u32[]{:S(2)}) collective-permute-start(bf16[128,768]{1,0:T(8,128)(2,1)S(1)} %constant_dynamic-slice_fusion.1), channel_id=1, source_target_pairs={{0,8},{4,60},{8,16},{12,4},{16,24},{20,12},{24,32},{28,20},{32,40}... | collective-permute-start | bytes 589832 | tf_op jit(solution)/shard_map/ppermute | solution.py:420
  61.6 3.0 %shard_map.84 = (bf16[256,384]{1,0:T(8,128)(2,1)S(1)}, bf16[256,384]{1,0:T(8,128)(2,1)S(1)}, bf16[1536,128]{1,0:T(8,128)(2,1)S(1)}, bf16[512,128]{1,0:T(8,128)(2...) custom-call(s32[1]{0:T(128)} %bitcast.refs_0_, s32[8]{0:T(128)S(1)} %copy-done.6, ...), custom_call_target="tpu_custom_call" | custom-call | tf_op jit(solution)/shard_map/pallas_call | solution.py:356
  64.6 3.9 %collective-permute-start.9 = (bf16[128,768]{1,0:T(8,128)(2,1)S(1)}, bf16[128,768]{1,0:T(8,128)(2,1)S(1)}, u32[]{:S(2)}, u32[]{:S(2)}) collective-permute-start(bf16[128,768]{1,0:T(8,128)(2,1)S(1)} %constant_dynamic-slice_fusion), channel_id=1, source_target_pairs={{0,8},{4,60},{8,16},{12,4},{16,24},{20,12},{24,32},{28,20},{32,40}... | collective-permute-start | bytes 589832 | tf_op jit(solution)/shard_map/ppermute | solution.py:420
  68.6 4.7 %shard_map.85 = (f32[512,384]{1,0:T(8,128)S(1)}, f32[512,128]{1,0:T(8,128)S(1)}) custom-call(bf16[512,128]{1,0:T(8,128)(2,1)S(1)} %get-tuple-element.24.refs_0_, bf16[256,384]{1,0:T(8,128)(2,1)S(1)} %get-tuple-element.25.refs_1_, bf16[256,384]{1,0:T(8,128)(2,1)S(1)} %get-tuple-element.26.refs_2_, bf16[128,768]{1,0:T(8,128)(2,1)S(1)} %copy-done.1, ...), custom_call_target="tpu_custom_call" | custom-call | tf_op jit(solution)/shard_map/pallas_call | solution.py:356
  73.3 3.2 %shard_map.86 = (f32[256,384]{1,0:T(8,128)S(1)}, f32[256,128]{1,0:T(8,128)S(1)}, bf16[256,512]{1,0:T(8,128)(2,1)S(1)}) custom-call(bf16[512,128]{1,0:T(8,128)(2,1)S(1)} %get-tuple-element.24.refs_0_, bf16[256,384]{1,0:T(8,128)(2,1)S(1)} %get-tuple-element.25.refs_1_, bf16[256,384]{1,0:T(8,128)(2,1)S(1)} %get-tuple-element.26.refs_2_, ...), custom_call_target="tpu_custom_call" | custom-call | tf_op jit(solution)/shard_map/pallas_call | solution.py:356
  76.5 4.2 %all_gather.11.refs_4_ = bf16[512,512]{1,0:T(8,128)(2,1)S(1)} all-gather(bf16[256,512]{1,0:T(8,128)(2,1)S(1)} %get-tuple-element.38), channel_id=1, replica_groups={{0,4},{8,12},{16,20},{24,28},{32,36},{40,44},{48,52},{56,60},{64,68},{7..., dimensions={0}, use_global_device_ids=true | all-gather | bytes 786432 | tf_op jit(solution)/shard_map/all_gather | solution.py:423
  80.7 0.8 shard_map.88
  81.6 7.0 %collective-permute-start.10 = (bf16[128,384]{1,0:T(8,128)(2,1)S(1)}, bf16[128,384]{1,0:T(8,128)(2,1)S(1)}, u32[]{:S(2)}, u32[]{:S(2)}) collective-permute-start(bf16[128,384]{1,0:T(8,128)(2,1)S(1)} %shard_map.88), channel_id=1, source_target_pairs={{0,64},{4,68},{8,72},{12,76},{16,80},{20,84},{24,88},{28,92},{32,9... | collective-permute-start | bytes 294920 | tf_op jit(solution)/shard_map/ppermute | solution.py:504
  88.6 0.8 shard_map.87.refs_1_
  89.4 2.0 %collective-permute-done.10.refs_2_ = bf16[128,384]{1,0:T(8,128)(2,1)S(1)} collective-permute-done((bf16[128,384]{1,0:T(8,128)(2,1)S(1)}, bf16[128,384]{1,0:T(8,128)(2,1)S(1)}, u32[]{:S(2)}, u32[]{:S(2)}) %collective-permute-start.10) | collective-permute-done | bytes 98336 | tf_op jit(solution)/shard_map/ppermute | solution.py:504
  (36 shorter events, 3.2 us)
Async XLA Ops:
  0.0 58.6 %copy-start = (bf16[1000,768]{1,0:T(8,128)(2,1)S(1)}, bf16[1000,768]{1,0:T(8,128)(2,1)}, u32[]{:S(2)}) copy-start(bf16[1000,768]{1,0:T(8,128)(2,1)} %param.15) | copy-start | bytes 4608004
  1.9 45.3 %copy-start.8 = (s32[8]{0:T(128)S(1)}, s32[8]{0:T(128)}, u32[]{:S(2)}) copy-start(s32[8]{0:T(128)} %param.14) | copy-start | bytes 100
  1.9 25.9 %collective-permute-start.3 = (bf16[128,768]{1,0:T(8,128)(2,1)}, bf16[128,768]{1,0:T(8,128)(2,1)S(1)}, u32[]{:S(2)}, u32[]{:S(2)}) collective-permute-start(bf16[128,768]{1,0:T(8,128)(2,1)} %get-tuple-element.27), channel_id=1, source_target_pairs={{0,64},{4,68},{8,72},{12,76},{16,80},{20,84},{24,88},{28,92},{32,9... | collective-permute-start | bytes 589832 | tf_op jit(solution)/shard_map/ppermute | solution.py:440
  16.4 5.2 %copy-start.7 = (bf16[256,768]{1,0:T(8,128)(2,1)}, bf16[256,768]{1,0:T(8,128)(2,1)S(1)}, u32[]{:S(2)}) copy-start(bf16[256,768]{1,0:T(8,128)(2,1)S(1)} %all_gather.9.refs_4_) | copy-start | bytes 1179652
  16.4 45.2 %copy-start.6 = (s32[8]{0:T(128)S(1)}, s32[8]{0:T(128)}, u32[]{:S(2)}) copy-start(s32[8]{0:T(128)} %refs_1_.7) | copy-start | bytes 100
  16.4 19.0 %collective-permute-start = (bf16[256,768]{1,0:T(8,128)(2,1)S(1)}, bf16[256,768]{1,0:T(8,128)(2,1)S(1)}, u32[]{:S(2)}, u32[]{:S(2)}) collective-permute-start(bf16[256,768]{1,0:T(8,128)(2,1)S(1)} %all_gather.9.refs_4_), channel_id=1, source_target_pairs={{0,8},{4,60},{8,16},{12,4},{16,24},{20,12},{24,32},{28,20},{32,40}... | collective-permute-start | bytes 1179656 | tf_op jit(solution)/shard_map/ppermute | solution.py:420
  23.7 44.8 %copy-start.1 = (bf16[128,768]{1,0:T(8,128)(2,1)S(1)}, bf16[128,768]{1,0:T(8,128)(2,1)}, u32[]{:S(2)}) copy-start(bf16[128,768]{1,0:T(8,128)(2,1)} %get-tuple-element.22.refs_3_) | copy-start | bytes 589828
  23.7 23.6 %all-to-all-start = ((bf16[16,24,512]{2,1,0:T(8,128)(2,1)}), bf16[16,24,512]{2,1,0:T(8,128)(2,1)S(1)}, u32[]{:S(2)}, u32[]{:S(2)}) async-start(bf16[16,24,512]{2,1,0:T(8,128)(2,1)} %bitcast.7), calls=%async_computation | async-start | bytes 786432 | tf_op jit(solution)/shard_map/all_to_all | solution.py:449
  30.6 12.7 %collective-permute-start.4 = (bf16[256,768]{1,0:T(8,128)(2,1)S(1)}, bf16[256,768]{1,0:T(8,128)(2,1)S(1)}, u32[]{:S(2)}, u32[]{:S(2)}) collective-permute-start(bf16[256,768]{1,0:T(8,128)(2,1)S(1)} %all_gather.10), channel_id=1, source_target_pairs={{0,8},{4,60},{8,16},{12,4},{16,24},{20,12},{24,32},{28,20},{32,40}... | collective-permute-start | bytes 1179656 | tf_op jit(solution)/shard_map/ppermute | solution.py:420
  35.4 12.1 %collective-permute-start.1 = (bf16[256,768]{1,0:T(8,128)(2,1)S(1)}, bf16[256,768]{1,0:T(8,128)(2,1)S(1)}, u32[]{:S(2)}, u32[]{:S(2)}) collective-permute-start(bf16[256,768]{1,0:T(8,128)(2,1)S(1)} %collective-permute-done.refs_5_), channel_id=1, source_target_pairs={{0,8},{4,60},{8,16},{12,4},{16,24},{20,12},{24,32},{28,20},{32,40}... | collective-permute-start | bytes 1179656 | tf_op jit(solution)/shard_map/ppermute | solution.py:420
  43.3 10.4 %collective-permute-start.5 = (bf16[256,768]{1,0:T(8,128)(2,1)S(1)}, bf16[256,768]{1,0:T(8,128)(2,1)}, u32[]{:S(2)}, u32[]{:S(2)}) collective-permute-start(bf16[256,768]{1,0:T(8,128)(2,1)S(1)} %collective-permute-done.4.refs_6_), channel_id=1, source_target_pairs={{0,8},{4,60},{8,16},{12,4},{16,24},{20,12},{24,32},{28,20},{32,40}... | collective-permute-start | bytes 1179656 | tf_op jit(solution)/shard_map/ppermute | solution.py:420
  46.5 0.8 copy-start.2
  47.5 0.7 copy-start.4
  48.2 11.0 %collective-permute-start.7 = (bf16[256,768]{1,0:T(8,128)(2,1)}, bf16[256,768]{1,0:T(8,128)(2,1)S(1)}, u32[]{:S(2)}, u32[]{:S(2)}) collective-permute-start(bf16[256,768]{1,0:T(8,128)(2,1)} %copy-done.4), channel_id=1, source_target_pairs={{0,8},{4,60},{8,16},{12,4},{16,24},{20,12},{24,32},{28,20},{32,40}... | collective-permute-start | bytes 1179656 | tf_op jit(solution)/shard_map/ppermute | solution.py:420
  51.1 10.4 %collective-permute-start.2 = (bf16[384,512]{1,0:T(8,128)(2,1)S(1)}, bf16[384,512]{1,0:T(8,128)(2,1)}, u32[]{:S(2)}, u32[]{:S(2)}) collective-permute-start(bf16[384,512]{1,0:T(8,128)(2,1)S(1)} %bitcast.5), channel_id=1, source_target_pairs={{0,4},{4,0},{8,12},{12,8},{16,20},{20,16},{24,28},{28,24},{32,36},... | collective-permute-start | bytes 1179656 | tf_op jit(solution)/shard_map/ppermute | solution.py:470
  53.7 10.9 %collective-permute-start.6 = (bf16[256,768]{1,0:T(8,128)(2,1)}, bf16[256,768]{1,0:T(8,128)(2,1)S(1)}, u32[]{:S(2)}, u32[]{:S(2)}) collective-permute-start(bf16[256,768]{1,0:T(8,128)(2,1)} %collective-permute-done.5.refs_8_), channel_id=1, source_target_pairs={{0,8},{4,60},{8,16},{12,4},{16,24},{20,12},{24,32},{28,20},{32,40}... | collective-permute-start | bytes 1179656 | tf_op jit(solution)/shard_map/ppermute | solution.py:420
  59.2 9.4 %copy-start.3 = (bf16[256,768]{1,0:T(8,128)(2,1)S(1)}, bf16[256,768]{1,0:T(8,128)(2,1)}, u32[]{:S(2)}) copy-start(bf16[256,768]{1,0:T(8,128)(2,1)} %copy-done.2) | copy-start | bytes 1179652
  59.2 9.4 %copy-start.5 = (bf16[256,768]{1,0:T(8,128)(2,1)S(1)}, bf16[256,768]{1,0:T(8,128)(2,1)}, u32[]{:S(2)}) copy-start(bf16[256,768]{1,0:T(8,128)(2,1)} %copy-done.4) | copy-start | bytes 1179652
  59.3 14.0 %collective-permute-start.8 = (bf16[128,768]{1,0:T(8,128)(2,1)S(1)}, bf16[128,768]{1,0:T(8,128)(2,1)S(1)}, u32[]{:S(2)}, u32[]{:S(2)}) collective-permute-start(bf16[128,768]{1,0:T(8,128)(2,1)S(1)} %constant_dynamic-slice_fusion.1), channel_id=1, source_target_pairs={{0,8},{4,60},{8,16},{12,4},{16,24},{20,12},{24,32},{28,20},{32,40}... | collective-permute-start | bytes 589832 | tf_op jit(solution)/shard_map/ppermute | solution.py:420
  64.6 8.7 %collective-permute-start.9 = (bf16[128,768]{1,0:T(8,128)(2,1)S(1)}, bf16[128,768]{1,0:T(8,128)(2,1)S(1)}, u32[]{:S(2)}, u32[]{:S(2)}) collective-permute-start(bf16[128,768]{1,0:T(8,128)(2,1)S(1)} %constant_dynamic-slice_fusion), channel_id=1, source_target_pairs={{0,8},{4,60},{8,16},{12,4},{16,24},{20,12},{24,32},{28,20},{32,40}... | collective-permute-start | bytes 589832 | tf_op jit(solution)/shard_map/ppermute | solution.py:420
  81.6 9.8 %collective-permute-start.10 = (bf16[128,384]{1,0:T(8,128)(2,1)S(1)}, bf16[128,384]{1,0:T(8,128)(2,1)S(1)}, u32[]{:S(2)}, u32[]{:S(2)}) collective-permute-start(bf16[128,384]{1,0:T(8,128)(2,1)S(1)} %shard_map.88), channel_id=1, source_target_pairs={{0,64},{4,68},{8,72},{12,76},{16,80},{20,84},{24,88},{28,92},{32,9... | collective-permute-start | bytes 294920 | tf_op jit(solution)/shard_map/ppermute | solution.py:504

commit v4 on v3

--- a/solution.py
+++ b/solution.py
@@ -130,8 +130,8 @@
     lengths_ref,
     got_ref,
     other_ref,
-    query_ref,
-    other_query_ref,
+    far_query_ref,
+    near_query_ref,
     *refs,
 ):
     *clip_refs, dead_ref = refs
@@ -146,7 +146,7 @@
     kind = lax.rem(iota((lines, 1), 0), MSG)
     from_half = lax.div(kind, 2 * BOUND)
     from_core = lax.rem(lax.div(kind, BOUND), 2)
-    quarter = (from_core != core).astype(jnp.int32) * 2 + (from_half != half).astype(jnp.int32)
+    quarter = (from_half == half).astype(jnp.int32) * 2 + (from_core != core).astype(jnp.int32)
     slot = meta[:, rows - 1 :].astype(jnp.float32)
     target = jnp.where(slot > 0, slot - 1.0 + (quarter * rows).astype(jnp.float32), -1.0)
     target = jnp.broadcast_to(target, (lines, rows))
@@ -155,8 +155,8 @@
     )
     put = (iota((4 * rows, lines), 0).astype(jnp.float32) == target).astype(jnp.bfloat16)
     queries = dot(put, data).astype(jnp.bfloat16)
-    query_ref[...] = queries[: 2 * rows]
-    other_query_ref[...] = queries[2 * rows :]
+    far_query_ref[...] = queries[: 2 * rows]
+    near_query_ref[...] = queries[2 * rows :]
 
     order = key_sources(me, devices)
     slots = len(order)
@@ -183,7 +183,7 @@
     other = lax.rem(me + plane, devices)
     away = 1 - 2 * core
     lane = iota((rows, HEAD_DIM), 1)
-    for q, owner in enumerate((me, other, me + away, other + away)):
+    for q, owner in enumerate((other, other + away, me, me + away)):
         position = iota((rows, HEAD_DIM), 0) + owner * rows
         dead = jnp.zeros((rows, HEAD_DIM), jnp.float32)
         for c, (start, end) in enumerate(bounds):
@@ -219,10 +219,10 @@
     return chunks
 
 
-def attend_kernel(sizes, first, last, *refs):
+def attend_kernel(tiles, sizes, first, last, *refs):
     refs = list(refs)
     dead_ref = refs.pop(0)
-    query_refs = [refs.pop(0), refs.pop(0)]
+    query_refs = [refs.pop(0) for _ in range(tiles)]
     block_refs = [refs.pop(0) for _ in sizes]
     clip_ref = refs.pop(0)
     if not first:
@@ -237,58 +237,72 @@
     lane = iota((tile, HEAD_DIM), 1)
     chunks = pair_up(sizes)
     ones = jnp.ones((CHUNK, HEAD_DIM), jnp.bfloat16)
-    for t in range(2):
+    stats = [jnp.zeros((tile, HEAD_DIM), jnp.float32) for _ in range(tiles)]
+
+    def columns(h):
+        return slice(h * HEAD_DIM, (h + 1) * HEAD_DIM)
+
+    def score(t, h):
         rows = slice(t * tile, (t + 1) * tile)
-        stat = jnp.zeros((tile, HEAD_DIM), jnp.float32)
-        for h in range(heads):
-            key_at = slice(h * HEAD_DIM, (h + 1) * HEAD_DIM)
-            value_at = slice(width + h * HEAD_DIM, width + (h + 1) * HEAD_DIM)
-            query = jnp.concatenate([query_refs[t][:, key_at], dead_ref[rows, :]], axis=1)
-            top = jnp.full((tile, HEAD_DIM), -3e38, jnp.float32)
-            for at, members in chunks:
-                key = jnp.concatenate([block_refs[i][o : o + n, key_at] for i, o, n in members])
-                key = jnp.concatenate([key, clip_ref[at : at + CHUNK, :]], axis=1)
-                s = dot(query, key, NT)
-                scores[t * heads + h, :, at : at + CHUNK] = s
-                for j in range(0, CHUNK, HEAD_DIM):
-                    top = jnp.maximum(top, s[:, j : j + HEAD_DIM])
-            top = jnp.max(top, axis=1, keepdims=True) * SCALE2
-            if first:
-                total = jnp.zeros((tile, 2 * HEAD_DIM), jnp.float32)
-            else:
-                old_top = stat_ref[rows, h : h + 1]
-                top = jnp.maximum(top, old_top)
-                fade = jnp.exp2(old_top - top)
-                weight = stat_ref[rows, h + 8 : h + 9] * fade
-                weight = jnp.broadcast_to(weight, (tile, HEAD_DIM))
-                total = jnp.concatenate([sum_ref[rows, key_at] * fade, weight], axis=1)
-            for at, members in chunks:
-                w = scores[t * heads + h, :, at : at + CHUNK] * SCALE2 - top
-                w = jnp.exp2(w).astype(jnp.bfloat16)
-                value = jnp.concatenate([block_refs[i][o : o + n, value_at] for i, o, n in members])
-                total = total + dot(w, jnp.concatenate([value, ones], axis=1))
-            weight = total[:, HEAD_DIM:]
-            if not last:
-                new_sum_ref[rows, key_at] = total[:, :HEAD_DIM]
-                stat = jnp.where(lane == h, top, stat)
-                stat = jnp.where(lane == h + 8, weight, stat)
-                continue
-            out = total[:, :HEAD_DIM] / weight
-            stat = jnp.where(lane == h, top + jnp.log2(weight), stat)
-            if t == 0:
-                out_ref[:, key_at] = out
-            else:
-                sent_ref[:, key_at] = out.astype(jnp.bfloat16)
+        query = jnp.concatenate([query_refs[t][:, columns(h)], dead_ref[rows, :]], axis=1)
+        top = jnp.full((tile, HEAD_DIM), -3e38, jnp.float32)
+        for at, members in chunks:
+            key = jnp.concatenate([block_refs[i][o : o + n, columns(h)] for i, o, n in members])
+            key = jnp.concatenate([key, clip_ref[at : at + CHUNK, :]], axis=1)
+            s = dot(query, key, NT)
+            scores[t * heads + h, :, at : at + CHUNK] = s
+            for j in range(0, CHUNK, HEAD_DIM):
+                top = jnp.maximum(top, s[:, j : j + HEAD_DIM])
+        return top
+
+    def finish(t, h, top):
+        rows = slice(t * tile, (t + 1) * tile)
+        top = jnp.max(top, axis=1, keepdims=True) * SCALE2
+        if first:
+            total = jnp.zeros((tile, 2 * HEAD_DIM), jnp.float32)
+        else:
+            old_top = stat_ref[rows, h : h + 1]
+            top = jnp.maximum(top, old_top)
+            fade = jnp.exp2(old_top - top)
+            weight = stat_ref[rows, h + 8 : h + 9] * fade
+            weight = jnp.broadcast_to(weight, (tile, HEAD_DIM))
+            total = jnp.concatenate([sum_ref[rows, columns(h)] * fade, weight], axis=1)
+        for at, members in chunks:
+            w = scores[t * heads + h, :, at : at + CHUNK] * SCALE2 - top
+            w = jnp.exp2(w).astype(jnp.bfloat16)
+            value = jnp.concatenate(
+                [block_refs[i][o : o + n, columns(heads + h)] for i, o, n in members]
+            )
+            total = total + dot(w, jnp.concatenate([value, ones], axis=1))
+        weight = total[:, HEAD_DIM:]
         if not last:
-            new_stat_ref[rows, :] = stat
-        elif t == 0:
-            level_ref[...] = stat
-        else:
-            high, mid, low = split3(stat)
-            mid = pltpu.roll(mid.astype(jnp.float32), 8, 1)
-            low = pltpu.roll(low.astype(jnp.float32), 16, 1)
-            packed = jnp.where(lane < 8, high.astype(jnp.float32), jnp.where(lane < 16, mid, low))
-            sent_ref[:, width:] = packed.astype(jnp.bfloat16)
+            new_sum_ref[rows, columns(h)] = total[:, :HEAD_DIM]
+            stats[t] = jnp.where(lane == h, top, stats[t])
+            stats[t] = jnp.where(lane == h + 8, weight, stats[t])
+            return
+        out = total[:, :HEAD_DIM] / weight
+        stats[t] = jnp.where(lane == h, top + jnp.log2(weight), stats[t])
+        out_ref[:, columns(h)] = out[: tile // 2]
+        sent_ref[:, columns(h)] = out[tile // 2 :].astype(jnp.bfloat16)
+
+    jobs = [(t, h) for t in range(tiles) for h in range(heads)]
+    ahead = score(*jobs[0])
+    for n, job in enumerate(jobs):
+        top = ahead
+        if n + 1 < len(jobs):
+            ahead = score(*jobs[n + 1])
+        finish(*job, top)
+    if not last:
+        for t in range(tiles):
+            new_stat_ref[t * tile : (t + 1) * tile, :] = stats[t]
+        return
+    level_ref[...] = stats[0][: tile // 2]
+    lane = lane[tile // 2 :]
+    high, mid, low = split3(stats[0][tile // 2 :])
+    mid = pltpu.roll(mid.astype(jnp.float32), 8, 1)
+    low = pltpu.roll(low.astype(jnp.float32), 16, 1)
+    packed = jnp.where(lane < 8, high.astype(jnp.float32), jnp.where(lane < 16, mid, low))
+    sent_ref[:, width:] = packed.astype(jnp.bfloat16)
 
 
 def combine_kernel(
@@ -297,8 +311,8 @@
     rows, width = own_ref.shape
     me = me_ref[0]
     half, _, core = place_of(me, devices)
-    owner = lax.rem(me + which * (devices // 2), devices)
-    other = pl.multiple_of((1 - core) * 2 * rows + which * rows, rows)
+    owner = lax.rem(me + (1 - which) * (devices // 2), devices)
+    other = pl.multiple_of((1 - core) * rows, rows)
     got = got_ref[pl.ds(other, rows), :]
     lane = iota((rows, HEAD_DIM), 1)
     position = iota((rows, HEAD_DIM), 0) + owner * rows
@@ -342,7 +356,7 @@
     return pl.BlockSpec(shape, lambda i: (0,) * len(shape))
 
 
-def call(kernel, operands, in_specs, outs, behind=(), scratch=(), vmem=None, token=False):
+def call(kernel, operands, in_specs, outs, behind=(), scratch=(), vmem=None, token=False, cost=0):
     taken, extra = len(operands), len(behind)
 
     def body(*refs):
@@ -361,38 +375,52 @@
         out_shape=results,
         scratch_shapes=scratch,
         compiler_params=pltpu.CompilerParams(vmem_limit_bytes=vmem),
-        cost_estimate=pl.CostEstimate(flops=0, bytes_accessed=0, transcendentals=0),
+        cost_estimate=pl.CostEstimate(flops=0, bytes_accessed=cost, transcendentals=0),
     )(*operands, *behind)
 
 
-def attend(dead, queries, blocks, clips, state, last, token=False, behind=()):
+def attend(dead, queries, blocks, clips, behind=()):
     tile, width = queries[0].shape
-    heads = width // HEAD_DIM
     sizes = [b.shape[0] for b in blocks]
-    keys = sum(sizes)
     rows = 2 * tile
-    first = state is None
-    operands = [dead, *queries, *blocks, clips] + ([] if first else list(state))
-    if last:
-        outs = [
-            jax.ShapeDtypeStruct((tile, width), jnp.float32),
-            jax.ShapeDtypeStruct((tile, HEAD_DIM), jnp.float32),
-            jax.ShapeDtypeStruct((tile, width + HEAD_DIM), jnp.bfloat16),
-        ]
-    else:
-        outs = [
+    operands = [dead, *queries, *blocks, clips]
+    return call(
+        functools.partial(attend_kernel, 2, sizes, True, False),
+        operands,
+        [whole(o.shape) for o in operands],
+        [
             jax.ShapeDtypeStruct((rows, width), jnp.float32),
             jax.ShapeDtypeStruct((rows, HEAD_DIM), jnp.float32),
-        ]
+        ],
+        behind,
+        [pltpu.VMEM((2 * width // HEAD_DIM, tile, sum(sizes)), jnp.float32)],
+        ATTEND_VMEM,
+    )
+
+
+def attend_last(which, dead, queries, blocks, clips, state, behind=()):
+    query = queries[which]
+    tile, width = query.shape
+    sizes = [b.shape[0] for b in blocks]
+
+    def part(array):
+        return pl.BlockSpec((tile, array.shape[1]), lambda i: (which, 0))
+
     return call(
-        functools.partial(attend_kernel, sizes, first, last),
-        operands,
-        [whole(o.shape) for o in operands],
-        outs,
+        functools.partial(attend_kernel, 1, sizes, False, True),
+        [dead, query, *blocks, clips, *state],
+        [part(dead), whole(query.shape)]
+        + [whole(b.shape) for b in blocks]
+        + [whole(clips.shape)]
+        + [part(s) for s in state],
+        [
+            jax.ShapeDtypeStruct((tile // 2, width), jnp.float32),
+            jax.ShapeDtypeStruct((tile // 2, HEAD_DIM), jnp.float32),
+            jax.ShapeDtypeStruct((tile // 2, width + HEAD_DIM), jnp.bfloat16),
+        ],
         behind,
-        [pltpu.VMEM((2 * heads, tile, keys), jnp.float32)],
+        [pltpu.VMEM((width // HEAD_DIM, tile, sum(sizes)), jnp.float32)],
         ATTEND_VMEM,
-        token,
     )
 
 
@@ -414,6 +442,7 @@
     to_half = [(index(h, y, c), index(1 - h, y, c)) for h, y, c in everyone]
     to_core = [(index(h, y, c), index(h, y, 1 - c)) for h, y, c in everyone]
     to_next = [(index(h, y, c), index(h, y + 1 - 2 * c, c)) for h, y, c in everyone]
+    to_second = [(index(h, y, c), index(h, y + 2 - 4 * c, c)) for h, y, c in everyone]
     chips = [[2 * i, 2 * i + 1] for i in range(plane)]
 
     def step(block):
@@ -438,14 +467,16 @@
         [bf16(rows, width)] * 2,
     )
     taken = lax.ppermute(given, "seq", to_half)
-    near0 = chip_gather(kept)
     (message,) = call(
         functools.partial(pack_kernel, plane),
         [clip_lengths, deal_owner[None, :], deal_slot[None, :], query_rows],
         [SMEM, whole((1, rows)), whole((1, rows)), whole((rows, width))],
         [bf16(sent_rows, sent_width)],
-        [near0],
-    )
+        [given],
+        cost=8 * 1024 * 1024,
+    )
+    kept, message = lax.optimization_barrier((kept, message))
+    near0 = chip_gather(kept)
     got = lax.all_to_all(
         message.reshape(plane, MSG, sent_width),
         "seq",
@@ -465,7 +496,7 @@
     near4 = step(core_half(near3))
     gates = jnp.take(gate_table, clip_steps, axis=0)
     counts = (12, 4)
-    *queries, clips0, clips1, dead, unpacked = call(
+    *queries, clips0, clips1, dead = call(
         functools.partial(unpack_kernel, devices, counts),
         [mine, clip_lengths, got, lax.ppermute(got, "seq", to_core)],
         [SMEM, SMEM] + [whole((sent_rows, sent_width))] * 2,
@@ -474,37 +505,30 @@
         + [bf16(4 * rows, HEAD_DIM)],
         [gates],
         vmem=SMALL_VMEM,
-        token=True,
-    )
-    half3, unpacked = lax.optimization_barrier((core_half(far3), unpacked))
-    far4 = step(half3)
+    )
+    far4 = lax.ppermute(core_half(far2), "seq", to_second)
     blocks = [kept, taken, near1, far1, near2, far2, near3]
-    state = attend(dead, queries, blocks, clips0, None, False)
-    own, level, sent = attend(
-        dead, queries, [far3, near4, far4], clips1, state, True, behind=[unpacked]
-    )
-    received = chip_gather(sent)
-
-    def combine(which):
+    state = attend(dead, queries, blocks, clips0)
+
+    def finish(which, behind):
+        own, level, sent = attend_last(
+            which, dead, queries, [far3, near4, far4], clips1, state, behind
+        )
+        operands = [mine, clip_lengths, own, level, chip_gather(sent), gates]
         return call(
             functools.partial(combine_kernel, devices, which),
-            [mine, clip_lengths, own, level, received, gates],
-            [
-                SMEM,
-                SMEM,
-                pl.BlockSpec((rows, half_width), lambda i: (which, 0)),
-                pl.BlockSpec((rows, HEAD_DIM), lambda i: (which, 0)),
-                whole((4 * rows, sent_width)),
-                whole(gates.shape),
-            ],
+            operands,
+            [SMEM, SMEM] + [whole(o.shape) for o in operands[2:]],
             [bf16(rows, half_width)],
             vmem=SMALL_VMEM,
         )[0]
 
-    back = lax.ppermute(combine(1), "seq", to_half)
+    theirs = finish(0, [])
+    back = lax.ppermute(theirs, "seq", to_half)
+    ours = finish(1, [theirs])
     return call(
         functools.partial(join_kernel, devices),
-        [mine, combine(0), back],
+        [mine, ours, back],
         [SMEM, whole((rows, half_width)), whole((rows, half_width))],
         [bf16(rows, width)],
         vmem=SMALL_VMEM,

time: 93.6 us -> 91.5 us (0.978)
  blocking collectives: 9.87 us -> 11 us
  waiting for transfers between devices: 7.05 us -> 5.94 us
    ppermute x8 -> x7, starting transfers between devices: 30.1 us -> 27.1 us  [step(): return lax.ppermute(block, 'seq', to_next)]
    ppermute x1 -> x2, starting transfers between devices: 7 us -> 9.77 us  [the longest x1 7 us: shards(): back = lax.ppermute(theirs, 'seq', to_half)]
    ppermute x1 -> x2, waiting for transfers between devices: 1.96 us -> 0.01 us  [the longest x1 0.01 us: shards(): back = lax.ppermute(theirs, 'seq', to_half)]
    all_gather x3 -> x4, blocking collectives: 9.87 us -> 11 us  [chip_gather(): return lax.all_gather(block, 'seq', axis_index_groups=chips, tiled=True)]
    ppermute x8 -> x7, waiting for transfers between devices: 5.08 us -> 5.93 us  [step(): return lax.ppermute(block, 'seq', to_next)]
    pallas_call x8 -> x9, Pallas kernels: 17.2 us -> 17 us  [call(): pl.pallas_call(body, grid=(1,), in_specs=list(in_specs) + [pl.BlockSpec(m...]
  transfers between devices with their start and end apart: 12 -> 12, of which waited for: 3 -> 2; matrix products, arithmetic and copies ran while one was open for 1% -> 1% of each run, Pallas kernels for 12% -> 13%
where the time goes in v4:
time: 91.5 us; the launch traced here: 90.9 us
  starting transfers between devices  55.1 us (60%)
  Pallas kernels  17 us (19%)
  blocking collectives  11 us (12%)
  waiting for transfers between devices  5.94 us (6%)
  local copies, waits for them, and re-layouts  1.38 us (2%)
    ppermute x7, starting transfers between devices, step(): return lax.ppermute(block, 'seq', to_next)  27.1 us
    pallas_call x9, Pallas kernels, call(): pl.pallas_call(body, grid=(1,), in_specs=list(in_specs) + [pl.BlockSpec(m...  17 us
    ppermute x1, starting transfers between devices, shards(): taken = lax.ppermute(given, 'seq', to_half)  11.5 us
    all_gather x4, blocking collectives, chip_gather(): return lax.all_gather(block, 'seq', axis_index_groups=chips, tiled=True)  11 us
    ppermute x1, starting transfers between devices, shards(): back = lax.ppermute(theirs, 'seq', to_half)  7 us
    ppermute x7, waiting for transfers between devices, step(): return lax.ppermute(block, 'seq', to_next)  5.93 us
    all_to_all x1, starting transfers between devices, shards(): lax.all_to_all(message.reshape(plane, MSG, sent_width), 'seq', split_axis...  4.16 us
    ppermute x1, starting transfers between devices, shards(): far4 = lax.ppermute(core_half(far2), 'seq', to_second)  2.78 us
  transfers between devices with their start and end apart: 12, of which 2 were waited for; matrix products, arithmetic and copies ran while one was open for 1% of the time, Pallas kernels for 13%

profile of v4, /device:TPU:1, one launch (start us, length us, event | category | flops | bytes accessed | tf_op | source)
XLA Modules:
  0.0 90.9 jit_solution(15126102539331097731)
XLA Ops:
  0.0 1.9 %shard_map.82 = (bf16[128,768]{1,0:T(8,128)(2,1)}, bf16[128,768]{1,0:T(8,128)(2,1)}) custom-call(s32[1]{0:T(128)} %bitcast.refs_0_, bf16[128,768]{1,0:T(8,128)(2,1)} %refs_1_.4, bf16[128,768]{1,0:T(8,128)(2,1)} %refs_2_.1), custom_call_target="tpu_custom_call" | custom-call | tf_op jit(solution)/shard_map/pallas_call | solution.py:370
  1.9 11.5 %collective-permute-start.3 = (bf16[128,768]{1,0:T(8,128)(2,1)}, bf16[128,768]{1,0:T(8,128)(2,1)S(1)}, u32[]{:S(2)}, u32[]{:S(2)}) collective-permute-start(bf16[128,768]{1,0:T(8,128)(2,1)} %get-tuple-element.25.refs_4_), channel_id=1, source_target_pairs={{0,64},{4,68},{8,72},{12,76},{16,80},{20,84},{24,88},{28,92},{32,9... | collective-permute-start | bytes 589832 | tf_op jit(solution)/shard_map/ppermute | solution.py:469
  13.4 2.1 %shard_map.83 = bf16[384,512]{1,0:T(8,128)(2,1)} custom-call(s32[8]{0:T(128)} %refs_1_.7, s32[1,128]{1,0:T(1,128)} %bitcast.8, s32[1,128]{1,0:T(1,128)} %bitcast.9, bf16[128,768]{1,0:T(8,128)(2,1)} %refs_3_.1, bf16[128,768]{1,0:T(8,128)(2,1)} %get-tuple-element.25.refs_4_), custom_call_target="tpu_custom_call" | custom-call | bytes 8388608 | tf_op jit(solution)/shard_map/pallas_call | solution.py:370
  15.4 3.0 %all_gather.12 = bf16[256,768]{1,0:T(8,128)(2,1)S(1)} all-gather(bf16[128,768]{1,0:T(8,128)(2,1)} %get-tuple-element.26.refs_3_), channel_id=1, replica_groups={{0,4},{8,12},{16,20},{24,28},{32,36},{40,44},{48,52},{56,60},{64,68},{7..., dimensions={0}, use_global_device_ids=true | all-gather | bytes 589824 | tf_op jit(solution)/shard_map/all_gather | solution.py:452
  18.4 5.1 %collective-permute-start = (bf16[256,768]{1,0:T(8,128)(2,1)S(1)}, bf16[256,768]{1,0:T(8,128)(2,1)S(1)}, u32[]{:S(2)}, u32[]{:S(2)}) collective-permute-start(bf16[256,768]{1,0:T(8,128)(2,1)S(1)} %all_gather.12), channel_id=1, source_target_pairs={{0,8},{4,60},{8,16},{12,4},{16,24},{20,12},{24,32},{28,20},{32,40}... | collective-permute-start | bytes 1179656 | tf_op jit(solution)/shard_map/ppermute | solution.py:449
  23.6 4.2 %all-to-all-start = ((bf16[16,24,512]{2,1,0:T(8,128)(2,1)}), bf16[16,24,512]{2,1,0:T(8,128)(2,1)S(1)}, u32[]{:S(2)}, u32[]{:S(2)}) async-start(bf16[16,24,512]{2,1,0:T(8,128)(2,1)} %bitcast.7), calls=%async_computation | async-start | bytes 786432 | tf_op jit(solution)/shard_map/all_to_all | solution.py:480
  27.7 2.8 %all_gather.13 = bf16[256,768]{1,0:T(8,128)(2,1)S(1)} all-gather(bf16[128,768]{1,0:T(8,128)(2,1)S(1)} %collective-permute-done.3.refs_4_), channel_id=1, replica_groups={{0,4},{8,12},{16,20},{24,28},{32,36},{40,44},{48,52},{56,60},{64,68},{7..., dimensions={0}, use_global_device_ids=true | all-gather | bytes 589824 | tf_op jit(solution)/shard_map/all_gather | solution.py:452
  30.5 4.8 %collective-permute-start.4 = (bf16[256,768]{1,0:T(8,128)(2,1)S(1)}, bf16[256,768]{1,0:T(8,128)(2,1)}, u32[]{:S(2)}, u32[]{:S(2)}) collective-permute-start(bf16[256,768]{1,0:T(8,128)(2,1)S(1)} %all_gather.13), channel_id=1, source_target_pairs={{0,8},{4,60},{8,16},{12,4},{16,24},{20,12},{24,32},{28,20},{32,40}... | collective-permute-start | bytes 1179656 | tf_op jit(solution)/shard_map/ppermute | solution.py:449
  35.3 3.1 %collective-permute-start.1 = (bf16[256,768]{1,0:T(8,128)(2,1)S(1)}, bf16[256,768]{1,0:T(8,128)(2,1)S(1)}, u32[]{:S(2)}, u32[]{:S(2)}) collective-permute-start(bf16[256,768]{1,0:T(8,128)(2,1)S(1)} %collective-permute-done.refs_5_), channel_id=1, source_target_pairs={{0,8},{4,60},{8,16},{12,4},{16,24},{20,12},{24,32},{28,20},{32,40}... | collective-permute-start | bytes 1179656 | tf_op jit(solution)/shard_map/ppermute | solution.py:449
  38.4 4.9 %collective-permute-done.4.refs_6_ = bf16[256,768]{1,0:T(8,128)(2,1)} collective-permute-done((bf16[256,768]{1,0:T(8,128)(2,1)S(1)}, bf16[256,768]{1,0:T(8,128)(2,1)}, u32[]{:S(2)}, u32[]{:S(2)}) %collective-permute-start.4) | collective-permute-done | bytes 393248 | tf_op jit(solution)/shard_map/ppermute | solution.py:449
  43.3 3.1 %collective-permute-start.5 = (bf16[256,768]{1,0:T(8,128)(2,1)}, bf16[256,768]{1,0:T(8,128)(2,1)S(1)}, u32[]{:S(2)}, u32[]{:S(2)}) collective-permute-start(bf16[256,768]{1,0:T(8,128)(2,1)} %collective-permute-done.4.refs_6_), channel_id=1, source_target_pairs={{0,8},{4,60},{8,16},{12,4},{16,24},{20,12},{24,32},{28,20},{32,40}... | collective-permute-start | bytes 1179656 | tf_op jit(solution)/shard_map/ppermute | solution.py:449
  46.4 1.0 %collective-permute-done.1.refs_7_ = bf16[256,768]{1,0:T(8,128)(2,1)S(1)} collective-permute-done((bf16[256,768]{1,0:T(8,128)(2,1)S(1)}, bf16[256,768]{1,0:T(8,128)(2,1)S(1)}, u32[]{:S(2)}, u32[]{:S(2)}) %collective-permute-start.1) | collective-permute-done | bytes 393248 | tf_op jit(solution)/shard_map/ppermute | solution.py:449
  48.1 2.9 %collective-permute-start.7 = (bf16[256,768]{1,0:T(8,128)(2,1)}, bf16[256,768]{1,0:T(8,128)(2,1)S(1)}, u32[]{:S(2)}, u32[]{:S(2)}) collective-permute-start(bf16[256,768]{1,0:T(8,128)(2,1)} %copy-done.2), channel_id=1, source_target_pairs={{0,8},{4,60},{8,16},{12,4},{16,24},{20,12},{24,32},{28,20},{32,40}... | collective-permute-start | bytes 1179656 | tf_op jit(solution)/shard_map/ppermute | solution.py:449
  51.7 2.7 %collective-permute-start.2 = (bf16[384,512]{1,0:T(8,128)(2,1)S(1)}, bf16[384,512]{1,0:T(8,128)(2,1)S(1)}, u32[]{:S(2)}, u32[]{:S(2)}) collective-permute-start(bf16[384,512]{1,0:T(8,128)(2,1)S(1)} %bitcast.5), channel_id=1, source_target_pairs={{0,4},{4,0},{8,12},{12,8},{16,20},{20,16},{24,28},{28,24},{32,36},... | collective-permute-start | bytes 1179656 | tf_op jit(solution)/shard_map/ppermute | solution.py:501
  54.4 4.9 %collective-permute-start.6 = (bf16[256,768]{1,0:T(8,128)(2,1)S(1)}, bf16[256,768]{1,0:T(8,128)(2,1)S(1)}, u32[]{:S(2)}, u32[]{:S(2)}) collective-permute-start(bf16[256,768]{1,0:T(8,128)(2,1)S(1)} %collective-permute-done.5.refs_8_), channel_id=1, source_target_pairs={{0,8},{4,60},{8,16},{12,4},{16,24},{20,12},{24,32},{28,20},{32,40}... | collective-permute-start | bytes 1179656 | tf_op jit(solution)/shard_map/ppermute | solution.py:449
  59.3 2.8 %collective-permute-start.9 = (bf16[128,768]{1,0:T(8,128)(2,1)S(1)}, bf16[128,768]{1,0:T(8,128)(2,1)S(1)}, u32[]{:S(2)}, u32[]{:S(2)}) collective-permute-start(bf16[128,768]{1,0:T(8,128)(2,1)S(1)} %constant_dynamic-slice_fusion), channel_id=1, source_target_pairs={{0,16},{4,52},{8,24},{12,60},{16,32},{20,4},{24,40},{28,12},{32,48... | collective-permute-start | bytes 589832 | tf_op jit(solution)/shard_map/ppermute | solution.py:509
  62.1 3.3 %collective-permute-start.8 = (bf16[128,768]{1,0:T(8,128)(2,1)S(1)}, bf16[128,768]{1,0:T(8,128)(2,1)S(1)}, u32[]{:S(2)}, u32[]{:S(2)}) collective-permute-start(bf16[128,768]{1,0:T(8,128)(2,1)S(1)} %constant_dynamic-slice_fusion.1), channel_id=1, source_target_pairs={{0,8},{4,60},{8,16},{12,4},{16,24},{20,12},{24,32},{28,20},{32,40}... | collective-permute-start | bytes 589832 | tf_op jit(solution)/shard_map/ppermute | solution.py:449
  65.5 2.5 %shard_map.84 = (bf16[256,384]{1,0:T(8,128)(2,1)S(1)}, bf16[256,384]{1,0:T(8,128)(2,1)S(1)}, bf16[1536,128]{1,0:T(8,128)(2,1)S(1)}, bf16[512,128]{1,0:T(8,128)(2,1)S(1)}, bf16[512,128]{1,0:T(8,128)(2,1)S(1)}) custom-call(s32[1]{0:T(128)} %bitcast.refs_0_, s32[8]{0:T(128)S(1)} %copy-done.4, bf16[384,512]{1,0:T(8,128)(2,1)S(1)} %bitcast.6, ...), custom_call_target="tpu_custom_call" | custom-call | tf_op jit(solution)/shard_map/pallas_call | solution.py:370
  68.1 4.5 %shard_map.85 = (f32[512,384]{1,0:T(8,128)S(1)}, f32[512,128]{1,0:T(8,128)S(1)}) custom-call(bf16[512,128]{1,0:T(8,128)(2,1)S(1)} %get-tuple-element.29.refs_0_, bf16[256,384]{1,0:T(8,128)(2,1)S(1)} %get-tuple-element.33.refs_1_, bf16[256,384]{1,0:T(8,128)(2,1)S(1)} %get-tuple-element.30.refs_2_.refs_1_, bf16[128,768]{1,0:T(8,128)(2,1)S(1)} %copy-done.1, ...), custom_call_target="tpu_custom_call" | custom-call | tf_op jit(solution)/shard_map/pallas_call | solution.py:370
  72.6 1.8 %shard_map.86 = (f32[128,384]{1,0:T(8,128)S(1)}, f32[128,128]{1,0:T(8,128)S(1)}, bf16[128,512]{1,0:T(8,128)(2,1)S(1)}) custom-call(bf16[512,128]{1,0:T(8,128)(2,1)S(1)} %get-tuple-element.29.refs_0_, bf16[256,384]{1,0:T(8,128)(2,1)S(1)} %get-tuple-element.33.refs_1_, bf16[256,768]{1,0:T(8,128)(2,1)S(1)} %collective-permute-done.6.refs_2_, ...), custom_call_target="tpu_custom_call" | custom-call | tf_op jit(solution)/shard_map/pallas_call | solution.py:370
  74.4 3.0 %all_gather.14.refs_4_ = bf16[256,512]{1,0:T(8,128)(2,1)S(1)} all-gather(bf16[128,512]{1,0:T(8,128)(2,1)S(1)} %get-tuple-element.39), channel_id=1, replica_groups={{0,4},{8,12},{16,20},{24,28},{32,36},{40,44},{48,52},{56,60},{64,68},{7..., dimensions={0}, use_global_device_ids=true | all-gather | bytes 393216 | tf_op jit(solution)/shard_map/all_gather | solution.py:452
  78.2 7.0 %collective-permute-start.10 = (bf16[128,384]{1,0:T(8,128)(2,1)S(1)}, bf16[128,384]{1,0:T(8,128)(2,1)S(1)}, u32[]{:S(2)}, u32[]{:S(2)}) collective-permute-start(bf16[128,384]{1,0:T(8,128)(2,1)S(1)} %shard_map.87.refs_8_), channel_id=1, source_target_pairs={{0,64},{4,68},{8,72},{12,76},{16,80},{20,84},{24,88},{28,92},{32,9... | collective-permute-start | bytes 294920 | tf_op jit(solution)/shard_map/ppermute | solution.py:527
  85.2 1.8 %shard_map.88 = (f32[128,384]{1,0:T(8,128)S(1)}, f32[128,128]{1,0:T(8,128)S(1)}, bf16[128,512]{1,0:T(8,128)(2,1)S(1)}) custom-call(bf16[512,128]{1,0:T(8,128)(2,1)S(1)} %get-tuple-element.29.refs_0_, bf16[256,384]{1,0:T(8,128)(2,1)S(1)} %get-tuple-element.30.refs_2_.refs_1_, bf16[256,768]{1,0:T(8,128)(2,1)S(1)} %collective-permute-done.6.refs_2_, ...), custom_call_target="tpu_custom_call" | custom-call | tf_op jit(solution)/shard_map/pallas_call | solution.py:370
  87.1 2.3 %all_gather.15.refs_4_ = bf16[256,512]{1,0:T(8,128)(2,1)S(1)} all-gather(bf16[128,512]{1,0:T(8,128)(2,1)S(1)} %get-tuple-element.42), channel_id=1, replica_groups={{0,4},{8,12},{16,20},{24,28},{32,36},{40,44},{48,52},{56,60},{64,68},{7..., dimensions={0}, use_global_device_ids=true | all-gather | bytes 393216 | tf_op jit(solution)/shard_map/all_gather | solution.py:452
  (32 shorter events, 3.9 us)
Async XLA Ops:
  0.0 51.0 %copy-start = (bf16[1000,768]{1,0:T(8,128)(2,1)S(1)}, bf16[1000,768]{1,0:T(8,128)(2,1)}, u32[]{:S(2)}) copy-start(bf16[1000,768]{1,0:T(8,128)(2,1)} %param.15) | copy-start | bytes 4608004
  0.0 46.4 %copy-start.5 = (s32[8]{0:T(128)S(1)}, s32[8]{0:T(128)}, u32[]{:S(2)}) copy-start(s32[8]{0:T(128)} %param.14) | copy-start | bytes 100
  1.9 25.8 %collective-permute-start.3 = (bf16[128,768]{1,0:T(8,128)(2,1)}, bf16[128,768]{1,0:T(8,128)(2,1)S(1)}, u32[]{:S(2)}, u32[]{:S(2)}) collective-permute-start(bf16[128,768]{1,0:T(8,128)(2,1)} %get-tuple-element.25.refs_4_), channel_id=1, source_target_pairs={{0,64},{4,68},{8,72},{12,76},{16,80},{20,84},{24,88},{28,92},{32,9... | collective-permute-start | bytes 589832 | tf_op jit(solution)/shard_map/ppermute | solution.py:469
  15.4 50.1 %copy-start.4 = (s32[8]{0:T(128)S(1)}, s32[8]{0:T(128)}, u32[]{:S(2)}) copy-start(s32[8]{0:T(128)} %refs_1_.7) | copy-start | bytes 100
  18.4 16.8 %collective-permute-start = (bf16[256,768]{1,0:T(8,128)(2,1)S(1)}, bf16[256,768]{1,0:T(8,128)(2,1)S(1)}, u32[]{:S(2)}, u32[]{:S(2)}) collective-permute-start(bf16[256,768]{1,0:T(8,128)(2,1)S(1)} %all_gather.12), channel_id=1, source_target_pairs={{0,8},{4,60},{8,16},{12,4},{16,24},{20,12},{24,32},{28,20},{32,40}... | collective-permute-start | bytes 1179656 | tf_op jit(solution)/shard_map/ppermute | solution.py:449
  23.5 44.5 %copy-start.1 = (bf16[128,768]{1,0:T(8,128)(2,1)S(1)}, bf16[128,768]{1,0:T(8,128)(2,1)}, u32[]{:S(2)}) copy-start(bf16[128,768]{1,0:T(8,128)(2,1)} %get-tuple-element.26.refs_3_) | copy-start | bytes 589828
  23.6 22.8 %all-to-all-start = ((bf16[16,24,512]{2,1,0:T(8,128)(2,1)}), bf16[16,24,512]{2,1,0:T(8,128)(2,1)S(1)}, u32[]{:S(2)}, u32[]{:S(2)}) async-start(bf16[16,24,512]{2,1,0:T(8,128)(2,1)} %bitcast.7), calls=%async_computation | async-start | bytes 786432 | tf_op jit(solution)/shard_map/all_to_all | solution.py:480
  30.5 12.8 %collective-permute-start.4 = (bf16[256,768]{1,0:T(8,128)(2,1)S(1)}, bf16[256,768]{1,0:T(8,128)(2,1)}, u32[]{:S(2)}, u32[]{:S(2)}) collective-permute-start(bf16[256,768]{1,0:T(8,128)(2,1)S(1)} %all_gather.13), channel_id=1, source_target_pairs={{0,8},{4,60},{8,16},{12,4},{16,24},{20,12},{24,32},{28,20},{32,40}... | collective-permute-start | bytes 1179656 | tf_op jit(solution)/shard_map/ppermute | solution.py:449
  35.3 12.1 %collective-permute-start.1 = (bf16[256,768]{1,0:T(8,128)(2,1)S(1)}, bf16[256,768]{1,0:T(8,128)(2,1)S(1)}, u32[]{:S(2)}, u32[]{:S(2)}) collective-permute-start(bf16[256,768]{1,0:T(8,128)(2,1)S(1)} %collective-permute-done.refs_5_), channel_id=1, source_target_pairs={{0,8},{4,60},{8,16},{12,4},{16,24},{20,12},{24,32},{28,20},{32,40}... | collective-permute-start | bytes 1179656 | tf_op jit(solution)/shard_map/ppermute | solution.py:449
  43.3 11.1 %collective-permute-start.5 = (bf16[256,768]{1,0:T(8,128)(2,1)}, bf16[256,768]{1,0:T(8,128)(2,1)S(1)}, u32[]{:S(2)}, u32[]{:S(2)}) collective-permute-start(bf16[256,768]{1,0:T(8,128)(2,1)} %collective-permute-done.4.refs_6_), channel_id=1, source_target_pairs={{0,8},{4,60},{8,16},{12,4},{16,24},{20,12},{24,32},{28,20},{32,40}... | collective-permute-start | bytes 1179656 | tf_op jit(solution)/shard_map/ppermute | solution.py:449
  47.4 0.7 copy-start.2
  48.1 13.9 %collective-permute-start.7 = (bf16[256,768]{1,0:T(8,128)(2,1)}, bf16[256,768]{1,0:T(8,128)(2,1)S(1)}, u32[]{:S(2)}, u32[]{:S(2)}) collective-permute-start(bf16[256,768]{1,0:T(8,128)(2,1)} %copy-done.2), channel_id=1, source_target_pairs={{0,8},{4,60},{8,16},{12,4},{16,24},{20,12},{24,32},{28,20},{32,40}... | collective-permute-start | bytes 1179656 | tf_op jit(solution)/shard_map/ppermute | solution.py:449
  51.6 16.4 %copy-start.3 = (bf16[256,768]{1,0:T(8,128)(2,1)S(1)}, bf16[256,768]{1,0:T(8,128)(2,1)}, u32[]{:S(2)}) copy-start(bf16[256,768]{1,0:T(8,128)(2,1)} %copy-done.2) | copy-start | bytes 1179652
  51.7 13.8 %collective-permute-start.2 = (bf16[384,512]{1,0:T(8,128)(2,1)S(1)}, bf16[384,512]{1,0:T(8,128)(2,1)S(1)}, u32[]{:S(2)}, u32[]{:S(2)}) collective-permute-start(bf16[384,512]{1,0:T(8,128)(2,1)S(1)} %bitcast.5), channel_id=1, source_target_pairs={{0,4},{4,0},{8,12},{12,8},{16,20},{20,16},{24,28},{28,24},{32,36},... | collective-permute-start | bytes 1179656 | tf_op jit(solution)/shard_map/ppermute | solution.py:501
  54.4 18.2 %collective-permute-start.6 = (bf16[256,768]{1,0:T(8,128)(2,1)S(1)}, bf16[256,768]{1,0:T(8,128)(2,1)S(1)}, u32[]{:S(2)}, u32[]{:S(2)}) collective-permute-start(bf16[256,768]{1,0:T(8,128)(2,1)S(1)} %collective-permute-done.5.refs_8_), channel_id=1, source_target_pairs={{0,8},{4,60},{8,16},{12,4},{16,24},{20,12},{24,32},{28,20},{32,40}... | collective-permute-start | bytes 1179656 | tf_op jit(solution)/shard_map/ppermute | solution.py:449
  59.3 13.3 %collective-permute-start.9 = (bf16[128,768]{1,0:T(8,128)(2,1)S(1)}, bf16[128,768]{1,0:T(8,128)(2,1)S(1)}, u32[]{:S(2)}, u32[]{:S(2)}) collective-permute-start(bf16[128,768]{1,0:T(8,128)(2,1)S(1)} %constant_dynamic-slice_fusion), channel_id=1, source_target_pairs={{0,16},{4,52},{8,24},{12,60},{16,32},{20,4},{24,40},{28,12},{32,48... | collective-permute-start | bytes 589832 | tf_op jit(solution)/shard_map/ppermute | solution.py:509
  62.1 10.5 %collective-permute-start.8 = (bf16[128,768]{1,0:T(8,128)(2,1)S(1)}, bf16[128,768]{1,0:T(8,128)(2,1)S(1)}, u32[]{:S(2)}, u32[]{:S(2)}) collective-permute-start(bf16[128,768]{1,0:T(8,128)(2,1)S(1)} %constant_dynamic-slice_fusion.1), channel_id=1, source_target_pairs={{0,8},{4,60},{8,16},{12,4},{16,24},{20,12},{24,32},{28,20},{32,40}... | collective-permute-start | bytes 589832 | tf_op jit(solution)/shard_map/ppermute | solution.py:449
  78.2 12.0 %collective-permute-start.10 = (bf16[128,384]{1,0:T(8,128)(2,1)S(1)}, bf16[128,384]{1,0:T(8,128)(2,1)S(1)}, u32[]{:S(2)}, u32[]{:S(2)}) collective-permute-start(bf16[128,384]{1,0:T(8,128)(2,1)S(1)} %shard_map.87.refs_8_), channel_id=1, source_target_pairs={{0,64},{4,68},{8,72},{12,76},{16,80},{20,84},{24,88},{28,92},{32,9... | collective-permute-start | bytes 294920 | tf_op jit(solution)/shard_map/ppermute | solution.py:527

commit v5 on v4

--- a/solution.py
+++ b/solution.py
@@ -379,21 +379,39 @@
     )(*operands, *behind)
 
 
-def attend(dead, queries, blocks, clips, behind=()):
-    tile, width = queries[0].shape
+def unpack_attend_kernel(devices, counts, sizes, *refs):
+    refs = list(refs)
+    head, blocks = [refs.pop(0) for _ in range(4)], [refs.pop(0) for _ in sizes]
+    far_query, near_query, later_clips, dead, sums, stats, clips, scores = refs
+    unpack_kernel(devices, counts, *head, far_query, near_query, clips, later_clips, dead)
+    attend_kernel(
+        2, sizes, True, False, dead, far_query, near_query, *blocks, clips, sums, stats, scores
+    )
+
+
+def unpack_attend(devices, counts, me, lengths, got, other, blocks, behind=()):
+    sent_rows, sent_width = got.shape
+    width = sent_width - HEAD_DIM
     sizes = [b.shape[0] for b in blocks]
-    rows = 2 * tile
-    operands = [dead, *queries, *blocks, clips]
+    tile, rows = 2 * HEAD_DIM, 4 * HEAD_DIM
+    operands = [me, lengths, got, other, *blocks]
+    first, second = (c * HEAD_DIM for c in counts)
     return call(
-        functools.partial(attend_kernel, 2, sizes, True, False),
+        functools.partial(unpack_attend_kernel, devices, counts, sizes),
         operands,
-        [whole(o.shape) for o in operands],
-        [
+        [SMEM, SMEM] + [whole(o.shape) for o in operands[2:]],
+        [jax.ShapeDtypeStruct((tile, width), jnp.bfloat16)] * 2
+        + [
+            jax.ShapeDtypeStruct((second, HEAD_DIM), jnp.bfloat16),
+            jax.ShapeDtypeStruct((rows, HEAD_DIM), jnp.bfloat16),
             jax.ShapeDtypeStruct((rows, width), jnp.float32),
             jax.ShapeDtypeStruct((rows, HEAD_DIM), jnp.float32),
         ],
         behind,
-        [pltpu.VMEM((2 * width // HEAD_DIM, tile, sum(sizes)), jnp.float32)],
+        [
+            pltpu.VMEM((first, HEAD_DIM), jnp.bfloat16),
+            pltpu.VMEM((2 * width // HEAD_DIM, tile, sum(sizes)), jnp.float32),
+        ],
         ATTEND_VMEM,
     )
 
@@ -496,19 +514,18 @@
     near4 = step(core_half(near3))
     gates = jnp.take(gate_table, clip_steps, axis=0)
     counts = (12, 4)
-    *queries, clips0, clips1, dead = call(
-        functools.partial(unpack_kernel, devices, counts),
-        [mine, clip_lengths, got, lax.ppermute(got, "seq", to_core)],
-        [SMEM, SMEM] + [whole((sent_rows, sent_width))] * 2,
-        [bf16(2 * rows, half_width)] * 2
-        + [bf16(c * rows, HEAD_DIM) for c in counts]
-        + [bf16(4 * rows, HEAD_DIM)],
+    far4 = lax.ppermute(core_half(far2), "seq", to_second)
+    *queries, clips1, dead, sums, stats = unpack_attend(
+        devices,
+        counts,
+        mine,
+        clip_lengths,
+        got,
+        lax.ppermute(got, "seq", to_core),
+        [kept, taken, near1, far1, near2, far2, near3],
         [gates],
-        vmem=SMALL_VMEM,
-    )
-    far4 = lax.ppermute(core_half(far2), "seq", to_second)
-    blocks = [kept, taken, near1, far1, near2, far2, near3]
-    state = attend(dead, queries, blocks, clips0)
+    )
+    state = (sums, stats)
 
     def finish(which, behind):
         own, level, sent = attend_last(

time: 91.5 us -> 91.2 us (level)
  Pallas kernels: 17 us -> 15.9 us
  local copies, waits for them, and re-layouts: 1.38 us -> 2.37 us
    pallas_call x9 -> x8, Pallas kernels: 17 us -> 15.9 us  [call(): pl.pallas_call(body, grid=(1,), in_specs=list(in_specs) + [pl.BlockSpec(m...]
    unnamed x12, local copies, waits for them, and re-layouts: 0.77 us -> 1.75 us
  transfers between devices with their start and end apart: 12 -> 12, of which waited for: 2 -> 2; matrix products, arithmetic and copies ran while one was open for 1% -> 1% of each run, Pallas kernels for 13% -> 12%
where the time goes in v5:
time: 91.2 us; the launch traced here: 90.5 us
  starting transfers between devices  54.9 us (60%)
  Pallas kernels  15.9 us (17%)
  blocking collectives  11 us (12%)
  waiting for transfers between devices  5.94 us (7%)
  local copies, waits for them, and re-layouts  2.37 us (3%)
    ppermute x7, starting transfers between devices, step(): return lax.ppermute(block, 'seq', to_next)  27.1 us
    pallas_call x8, Pallas kernels, call(): pl.pallas_call(body, grid=(1,), in_specs=list(in_specs) + [pl.BlockSpec(m...  15.9 us
    ppermute x1, starting transfers between devices, shards(): taken = lax.ppermute(given, 'seq', to_half)  11.5 us
    all_gather x4, blocking collectives, chip_gather(): return lax.all_gather(block, 'seq', axis_index_groups=chips, tiled=True)  11 us
    ppermute x1, starting transfers between devices, shards(): back = lax.ppermute(theirs, 'seq', to_half)  7 us
    ppermute x7, waiting for transfers between devices, step(): return lax.ppermute(block, 'seq', to_next)  5.93 us
    all_to_all x1, starting transfers between devices, shards(): lax.all_to_all(message.reshape(plane, MSG, sent_width), 'seq', split_axis...  4.03 us
    ppermute x1, starting transfers between devices, shards(): far4 = lax.ppermute(core_half(far2), 'seq', to_second)  2.78 us
  transfers between devices with their start and end apart: 12, of which 2 were waited for; matrix products, arithmetic and copies ran while one was open for 1% of the time, Pallas kernels for 12%

profile of v5, /device:TPU:1, one launch (start us, length us, event | category | flops | bytes accessed | tf_op | source)
XLA Modules:
  0.0 90.5 jit_solution(6383581266981509613)
XLA Ops:
  0.0 1.9 %shard_map.82 = (bf16[128,768]{1,0:T(8,128)(2,1)}, bf16[128,768]{1,0:T(8,128)(2,1)}) custom-call(s32[1]{0:T(128)} %bitcast.refs_0_, bf16[128,768]{1,0:T(8,128)(2,1)} %refs_1_.4, bf16[128,768]{1,0:T(8,128)(2,1)} %refs_2_.1), custom_call_target="tpu_custom_call" | custom-call | tf_op jit(solution)/shard_map/pallas_call | solution.py:370
  1.9 11.5 %collective-permute-start.3 = (bf16[128,768]{1,0:T(8,128)(2,1)}, bf16[128,768]{1,0:T(8,128)(2,1)S(1)}, u32[]{:S(2)}, u32[]{:S(2)}) collective-permute-start(bf16[128,768]{1,0:T(8,128)(2,1)} %get-tuple-element.24.refs_4_), channel_id=1, source_target_pairs={{0,64},{4,68},{8,72},{12,76},{16,80},{20,84},{24,88},{28,92},{32,9... | collective-permute-start | bytes 589832 | tf_op jit(solution)/shard_map/ppermute | solution.py:487
  13.4 2.1 %shard_map.83 = bf16[384,512]{1,0:T(8,128)(2,1)} custom-call(s32[8]{0:T(128)} %refs_1_.7, s32[1,128]{1,0:T(1,128)} %bitcast.8, s32[1,128]{1,0:T(1,128)} %bitcast.9, bf16[128,768]{1,0:T(8,128)(2,1)} %refs_3_.1, bf16[128,768]{1,0:T(8,128)(2,1)} %get-tuple-element.24.refs_4_), custom_call_target="tpu_custom_call" | custom-call | bytes 8388608 | tf_op jit(solution)/shard_map/pallas_call | solution.py:370
  15.5 3.0 %all_gather.12 = bf16[256,768]{1,0:T(8,128)(2,1)S(1)} all-gather(bf16[128,768]{1,0:T(8,128)(2,1)} %get-tuple-element.25.refs_4_), channel_id=1, replica_groups={{0,4},{8,12},{16,20},{24,28},{32,36},{40,44},{48,52},{56,60},{64,68},{7..., dimensions={0}, use_global_device_ids=true | all-gather | bytes 589824 | tf_op jit(solution)/shard_map/all_gather | solution.py:470
  18.5 5.1 %collective-permute-start = (bf16[256,768]{1,0:T(8,128)(2,1)S(1)}, bf16[256,768]{1,0:T(8,128)(2,1)S(1)}, u32[]{:S(2)}, u32[]{:S(2)}) collective-permute-start(bf16[256,768]{1,0:T(8,128)(2,1)S(1)} %all_gather.12), channel_id=1, source_target_pairs={{0,8},{4,60},{8,16},{12,4},{16,24},{20,12},{24,32},{28,20},{32,40}... | collective-permute-start | bytes 1179656 | tf_op jit(solution)/shard_map/ppermute | solution.py:467
  23.6 4.0 %all-to-all-start = ((bf16[16,24,512]{2,1,0:T(8,128)(2,1)}), bf16[16,24,512]{2,1,0:T(8,128)(2,1)S(1)}, u32[]{:S(2)}, u32[]{:S(2)}) async-start(bf16[16,24,512]{2,1,0:T(8,128)(2,1)} %bitcast.7), calls=%async_computation | async-start | bytes 786432 | tf_op jit(solution)/shard_map/all_to_all | solution.py:498
  27.6 2.8 %all_gather.13 = bf16[256,768]{1,0:T(8,128)(2,1)S(1)} all-gather(bf16[128,768]{1,0:T(8,128)(2,1)S(1)} %collective-permute-done.3.refs_5_), channel_id=1, replica_groups={{0,4},{8,12},{16,20},{24,28},{32,36},{40,44},{48,52},{56,60},{64,68},{7..., dimensions={0}, use_global_device_ids=true | all-gather | bytes 589824 | tf_op jit(solution)/shard_map/all_gather | solution.py:470
  30.4 4.8 %collective-permute-start.4 = (bf16[256,768]{1,0:T(8,128)(2,1)S(1)}, bf16[256,768]{1,0:T(8,128)(2,1)}, u32[]{:S(2)}, u32[]{:S(2)}) collective-permute-start(bf16[256,768]{1,0:T(8,128)(2,1)S(1)} %all_gather.13), channel_id=1, source_target_pairs={{0,8},{4,60},{8,16},{12,4},{16,24},{20,12},{24,32},{28,20},{32,40}... | collective-permute-start | bytes 1179656 | tf_op jit(solution)/shard_map/ppermute | solution.py:467
  35.1 3.1 %collective-permute-start.1 = (bf16[256,768]{1,0:T(8,128)(2,1)S(1)}, bf16[256,768]{1,0:T(8,128)(2,1)S(1)}, u32[]{:S(2)}, u32[]{:S(2)}) collective-permute-start(bf16[256,768]{1,0:T(8,128)(2,1)S(1)} %collective-permute-done.refs_6_), channel_id=1, source_target_pairs={{0,8},{4,60},{8,16},{12,4},{16,24},{20,12},{24,32},{28,20},{32,40}... | collective-permute-start | bytes 1179656 | tf_op jit(solution)/shard_map/ppermute | solution.py:467
  38.2 4.9 %collective-permute-done.4.refs_7_ = bf16[256,768]{1,0:T(8,128)(2,1)} collective-permute-done((bf16[256,768]{1,0:T(8,128)(2,1)S(1)}, bf16[256,768]{1,0:T(8,128)(2,1)}, u32[]{:S(2)}, u32[]{:S(2)}) %collective-permute-start.4) | collective-permute-done | bytes 393248 | tf_op jit(solution)/shard_map/ppermute | solution.py:467
  43.2 3.1 %collective-permute-start.5 = (bf16[256,768]{1,0:T(8,128)(2,1)}, bf16[256,768]{1,0:T(8,128)(2,1)S(1)}, u32[]{:S(2)}, u32[]{:S(2)}) collective-permute-start(bf16[256,768]{1,0:T(8,128)(2,1)} %collective-permute-done.4.refs_7_), channel_id=1, source_target_pairs={{0,8},{4,60},{8,16},{12,4},{16,24},{20,12},{24,32},{28,20},{32,40}... | collective-permute-start | bytes 1179656 | tf_op jit(solution)/shard_map/ppermute | solution.py:467
  46.3 1.0 %collective-permute-done.1.refs_8_ = bf16[256,768]{1,0:T(8,128)(2,1)S(1)} collective-permute-done((bf16[256,768]{1,0:T(8,128)(2,1)S(1)}, bf16[256,768]{1,0:T(8,128)(2,1)S(1)}, u32[]{:S(2)}, u32[]{:S(2)}) %collective-permute-start.1) | collective-permute-done | bytes 393248 | tf_op jit(solution)/shard_map/ppermute | solution.py:467
  48.0 2.9 %collective-permute-start.6 = (bf16[256,768]{1,0:T(8,128)(2,1)}, bf16[256,768]{1,0:T(8,128)(2,1)S(1)}, u32[]{:S(2)}, u32[]{:S(2)}) collective-permute-start(bf16[256,768]{1,0:T(8,128)(2,1)} %copy-done.2), channel_id=1, source_target_pairs={{0,8},{4,60},{8,16},{12,4},{16,24},{20,12},{24,32},{28,20},{32,40}... | collective-permute-start | bytes 1179656 | tf_op jit(solution)/shard_map/ppermute | solution.py:467
  51.5 2.6 %collective-permute-start.2 = (bf16[384,512]{1,0:T(8,128)(2,1)S(1)}, bf16[384,512]{1,0:T(8,128)(2,1)S(1)}, u32[]{:S(2)}, u32[]{:S(2)}) collective-permute-start(bf16[384,512]{1,0:T(8,128)(2,1)S(1)} %bitcast.5), channel_id=1, source_target_pairs={{0,4},{4,0},{8,12},{12,8},{16,20},{20,16},{24,28},{28,24},{32,36},... | collective-permute-start | bytes 1179656 | tf_op jit(solution)/shard_map/ppermute | solution.py:524
  54.1 4.9 %collective-permute-start.7 = (bf16[256,768]{1,0:T(8,128)(2,1)S(1)}, bf16[256,768]{1,0:T(8,128)(2,1)S(1)}, u32[]{:S(2)}, u32[]{:S(2)}) collective-permute-start(bf16[256,768]{1,0:T(8,128)(2,1)S(1)} %collective-permute-done.5.refs_9_), channel_id=1, source_target_pairs={{0,8},{4,60},{8,16},{12,4},{16,24},{20,12},{24,32},{28,20},{32,40}... | collective-permute-start | bytes 1179656 | tf_op jit(solution)/shard_map/ppermute | solution.py:467
  59.0 2.8 %collective-permute-start.9 = (bf16[128,768]{1,0:T(8,128)(2,1)S(1)}, bf16[128,768]{1,0:T(8,128)(2,1)S(1)}, u32[]{:S(2)}, u32[]{:S(2)}) collective-permute-start(bf16[128,768]{1,0:T(8,128)(2,1)S(1)} %constant_dynamic-slice_fusion), channel_id=1, source_target_pairs={{0,16},{4,52},{8,24},{12,60},{16,32},{20,4},{24,40},{28,12},{32,48... | collective-permute-start | bytes 589832 | tf_op jit(solution)/shard_map/ppermute | solution.py:517
  61.8 3.3 %collective-permute-start.8 = (bf16[128,768]{1,0:T(8,128)(2,1)S(1)}, bf16[128,768]{1,0:T(8,128)(2,1)S(1)}, u32[]{:S(2)}, u32[]{:S(2)}) collective-permute-start(bf16[128,768]{1,0:T(8,128)(2,1)S(1)} %constant_dynamic-slice_fusion.1), channel_id=1, source_target_pairs={{0,8},{4,60},{8,16},{12,4},{16,24},{20,12},{24,32},{28,20},{32,40}... | collective-permute-start | bytes 589832 | tf_op jit(solution)/shard_map/ppermute | solution.py:467
  65.3 1.0 %copy-done.3 = bf16[256,768]{1,0:T(8,128)(2,1)S(1)} copy-done((bf16[256,768]{1,0:T(8,128)(2,1)S(1)}, bf16[256,768]{1,0:T(8,128)(2,1)}, u32[]{:S(2)}) %copy-start.3) | copy-done | bytes 393240
  66.2 5.9 %shard_map.84 = (bf16[256,384]{1,0:T(8,128)(2,1)S(1)}, bf16[256,384]{1,0:T(8,128)(2,1)S(1)}, bf16[512,128]{1,0:T(8,128)(2,1)S(1)}, bf16[512,128]{1,0:T(8,128)(2,...) custom-call(s32[1]{0:T(128)} %bitcast.refs_0_, s32[8]{0:T(128)S(1)} %copy-done.4, bf16[384,512]{1,0:T(8,128)(2,1)S(1)} %bitcast.6, ...), custom_call_target="tpu_custom_call" | custom-call | tf_op jit(solution)/shard_map/pallas_call | solution.py:370
  72.2 1.9 %shard_map.85 = (f32[128,384]{1,0:T(8,128)S(1)}, f32[128,128]{1,0:T(8,128)S(1)}, bf16[128,512]{1,0:T(8,128)(2,1)S(1)}) custom-call(bf16[512,128]{1,0:T(8,128)(2,1)S(1)} %get-tuple-element.29.refs_0_, bf16[256,384]{1,0:T(8,128)(2,1)S(1)} %get-tuple-element.34.refs_1_, bf16[256,768]{1,0:T(8,128)(2,1)S(1)} %collective-permute-done.7.refs_2_, ...), custom_call_target="tpu_custom_call" | custom-call | tf_op jit(solution)/shard_map/pallas_call | solution.py:370
  74.0 3.0 %all_gather.14.refs_4_ = bf16[256,512]{1,0:T(8,128)(2,1)S(1)} all-gather(bf16[128,512]{1,0:T(8,128)(2,1)S(1)} %get-tuple-element.37), channel_id=1, replica_groups={{0,4},{8,12},{16,20},{24,28},{32,36},{40,44},{48,52},{56,60},{64,68},{7..., dimensions={0}, use_global_device_ids=true | all-gather | bytes 393216 | tf_op jit(solution)/shard_map/all_gather | solution.py:470
  77.8 7.0 %collective-permute-start.10 = (bf16[128,384]{1,0:T(8,128)(2,1)S(1)}, bf16[128,384]{1,0:T(8,128)(2,1)S(1)}, u32[]{:S(2)}, u32[]{:S(2)}) collective-permute-start(bf16[128,384]{1,0:T(8,128)(2,1)S(1)} %shard_map.86.refs_8_), channel_id=1, source_target_pairs={{0,64},{4,68},{8,72},{12,76},{16,80},{20,84},{24,88},{28,92},{32,9... | collective-permute-start | bytes 294920 | tf_op jit(solution)/shard_map/ppermute | solution.py:544
  84.9 1.8 %shard_map.87 = (f32[128,384]{1,0:T(8,128)S(1)}, f32[128,128]{1,0:T(8,128)S(1)}, bf16[128,512]{1,0:T(8,128)(2,1)S(1)}) custom-call(bf16[512,128]{1,0:T(8,128)(2,1)S(1)} %get-tuple-element.29.refs_0_, bf16[256,384]{1,0:T(8,128)(2,1)S(1)} %get-tuple-element.30.refs_1_, bf16[256,768]{1,0:T(8,128)(2,1)S(1)} %collective-permute-done.7.refs_2_, ...), custom_call_target="tpu_custom_call" | custom-call | tf_op jit(solution)/shard_map/pallas_call | solution.py:370
  86.7 2.3 %all_gather.15.refs_4_ = bf16[256,512]{1,0:T(8,128)(2,1)S(1)} all-gather(bf16[128,512]{1,0:T(8,128)(2,1)S(1)} %get-tuple-element.40), channel_id=1, replica_groups={{0,4},{8,12},{16,20},{24,28},{32,36},{40,44},{48,52},{56,60},{64,68},{7..., dimensions={0}, use_global_device_ids=true | all-gather | bytes 393216 | tf_op jit(solution)/shard_map/all_gather | solution.py:470
  (31 shorter events, 3.9 us)
Async XLA Ops:
  0.0 50.9 %copy-start = (bf16[1000,768]{1,0:T(8,128)(2,1)S(1)}, bf16[1000,768]{1,0:T(8,128)(2,1)}, u32[]{:S(2)}) copy-start(bf16[1000,768]{1,0:T(8,128)(2,1)} %param.15) | copy-start | bytes 4608004
  0.0 46.2 %copy-start.5 = (s32[8]{0:T(128)S(1)}, s32[8]{0:T(128)}, u32[]{:S(2)}) copy-start(s32[8]{0:T(128)} %param.14) | copy-start | bytes 100
  1.9 25.7 %collective-permute-start.3 = (bf16[128,768]{1,0:T(8,128)(2,1)}, bf16[128,768]{1,0:T(8,128)(2,1)S(1)}, u32[]{:S(2)}, u32[]{:S(2)}) collective-permute-start(bf16[128,768]{1,0:T(8,128)(2,1)} %get-tuple-element.24.refs_4_), channel_id=1, source_target_pairs={{0,64},{4,68},{8,72},{12,76},{16,80},{20,84},{24,88},{28,92},{32,9... | collective-permute-start | bytes 589832 | tf_op jit(solution)/shard_map/ppermute | solution.py:487
  15.5 49.8 %copy-start.1 = (bf16[128,768]{1,0:T(8,128)(2,1)S(1)}, bf16[128,768]{1,0:T(8,128)(2,1)}, u32[]{:S(2)}) copy-start(bf16[128,768]{1,0:T(8,128)(2,1)} %get-tuple-element.25.refs_4_) | copy-start | bytes 589828
  15.5 49.8 %copy-start.4 = (s32[8]{0:T(128)S(1)}, s32[8]{0:T(128)}, u32[]{:S(2)}) copy-start(s32[8]{0:T(128)} %refs_1_.7) | copy-start | bytes 100
  18.5 16.7 %collective-permute-start = (bf16[256,768]{1,0:T(8,128)(2,1)S(1)}, bf16[256,768]{1,0:T(8,128)(2,1)S(1)}, u32[]{:S(2)}, u32[]{:S(2)}) collective-permute-start(bf16[256,768]{1,0:T(8,128)(2,1)S(1)} %all_gather.12), channel_id=1, source_target_pairs={{0,8},{4,60},{8,16},{12,4},{16,24},{20,12},{24,32},{28,20},{32,40}... | collective-permute-start | bytes 1179656 | tf_op jit(solution)/shard_map/ppermute | solution.py:467
  23.6 22.7 %all-to-all-start = ((bf16[16,24,512]{2,1,0:T(8,128)(2,1)}), bf16[16,24,512]{2,1,0:T(8,128)(2,1)S(1)}, u32[]{:S(2)}, u32[]{:S(2)}) async-start(bf16[16,24,512]{2,1,0:T(8,128)(2,1)} %bitcast.7), calls=%async_computation | async-start | bytes 786432 | tf_op jit(solution)/shard_map/all_to_all | solution.py:498
  30.4 12.8 %collective-permute-start.4 = (bf16[256,768]{1,0:T(8,128)(2,1)S(1)}, bf16[256,768]{1,0:T(8,128)(2,1)}, u32[]{:S(2)}, u32[]{:S(2)}) collective-permute-start(bf16[256,768]{1,0:T(8,128)(2,1)S(1)} %all_gather.13), channel_id=1, source_target_pairs={{0,8},{4,60},{8,16},{12,4},{16,24},{20,12},{24,32},{28,20},{32,40}... | collective-permute-start | bytes 1179656 | tf_op jit(solution)/shard_map/ppermute | solution.py:467
  35.1 12.1 %collective-permute-start.1 = (bf16[256,768]{1,0:T(8,128)(2,1)S(1)}, bf16[256,768]{1,0:T(8,128)(2,1)S(1)}, u32[]{:S(2)}, u32[]{:S(2)}) collective-permute-start(bf16[256,768]{1,0:T(8,128)(2,1)S(1)} %collective-permute-done.refs_6_), channel_id=1, source_target_pairs={{0,8},{4,60},{8,16},{12,4},{16,24},{20,12},{24,32},{28,20},{32,40}... | collective-permute-start | bytes 1179656 | tf_op jit(solution)/shard_map/ppermute | solution.py:467
  43.2 10.9 %collective-permute-start.5 = (bf16[256,768]{1,0:T(8,128)(2,1)}, bf16[256,768]{1,0:T(8,128)(2,1)S(1)}, u32[]{:S(2)}, u32[]{:S(2)}) collective-permute-start(bf16[256,768]{1,0:T(8,128)(2,1)} %collective-permute-done.4.refs_7_), channel_id=1, source_target_pairs={{0,8},{4,60},{8,16},{12,4},{16,24},{20,12},{24,32},{28,20},{32,40}... | collective-permute-start | bytes 1179656 | tf_op jit(solution)/shard_map/ppermute | solution.py:467
  47.3 0.8 copy-start.2
  48.0 13.8 %collective-permute-start.6 = (bf16[256,768]{1,0:T(8,128)(2,1)}, bf16[256,768]{1,0:T(8,128)(2,1)S(1)}, u32[]{:S(2)}, u32[]{:S(2)}) collective-permute-start(bf16[256,768]{1,0:T(8,128)(2,1)} %copy-done.2), channel_id=1, source_target_pairs={{0,8},{4,60},{8,16},{12,4},{16,24},{20,12},{24,32},{28,20},{32,40}... | collective-permute-start | bytes 1179656 | tf_op jit(solution)/shard_map/ppermute | solution.py:467
  51.5 13.7 %collective-permute-start.2 = (bf16[384,512]{1,0:T(8,128)(2,1)S(1)}, bf16[384,512]{1,0:T(8,128)(2,1)S(1)}, u32[]{:S(2)}, u32[]{:S(2)}) collective-permute-start(bf16[384,512]{1,0:T(8,128)(2,1)S(1)} %bitcast.5), channel_id=1, source_target_pairs={{0,4},{4,0},{8,12},{12,8},{16,20},{20,16},{24,28},{28,24},{32,36},... | collective-permute-start | bytes 1179656 | tf_op jit(solution)/shard_map/ppermute | solution.py:524
  54.1 18.1 %collective-permute-start.7 = (bf16[256,768]{1,0:T(8,128)(2,1)S(1)}, bf16[256,768]{1,0:T(8,128)(2,1)S(1)}, u32[]{:S(2)}, u32[]{:S(2)}) collective-permute-start(bf16[256,768]{1,0:T(8,128)(2,1)S(1)} %collective-permute-done.5.refs_9_), channel_id=1, source_target_pairs={{0,8},{4,60},{8,16},{12,4},{16,24},{20,12},{24,32},{28,20},{32,40}... | collective-permute-start | bytes 1179656 | tf_op jit(solution)/shard_map/ppermute | solution.py:467
  59.0 13.2 %collective-permute-start.9 = (bf16[128,768]{1,0:T(8,128)(2,1)S(1)}, bf16[128,768]{1,0:T(8,128)(2,1)S(1)}, u32[]{:S(2)}, u32[]{:S(2)}) collective-permute-start(bf16[128,768]{1,0:T(8,128)(2,1)S(1)} %constant_dynamic-slice_fusion), channel_id=1, source_target_pairs={{0,16},{4,52},{8,24},{12,60},{16,32},{20,4},{24,40},{28,12},{32,48... | collective-permute-start | bytes 589832 | tf_op jit(solution)/shard_map/ppermute | solution.py:517
  61.8 10.4 %collective-permute-start.8 = (bf16[128,768]{1,0:T(8,128)(2,1)S(1)}, bf16[128,768]{1,0:T(8,128)(2,1)S(1)}, u32[]{:S(2)}, u32[]{:S(2)}) collective-permute-start(bf16[128,768]{1,0:T(8,128)(2,1)S(1)} %constant_dynamic-slice_fusion.1), channel_id=1, source_target_pairs={{0,8},{4,60},{8,16},{12,4},{16,24},{20,12},{24,32},{28,20},{32,40}... | collective-permute-start | bytes 589832 | tf_op jit(solution)/shard_map/ppermute | solution.py:467
  65.3 1.0 %copy-start.3 = (bf16[256,768]{1,0:T(8,128)(2,1)S(1)}, bf16[256,768]{1,0:T(8,128)(2,1)}, u32[]{:S(2)}) copy-start(bf16[256,768]{1,0:T(8,128)(2,1)} %copy-done.2) | copy-start | bytes 1179652
  77.8 12.0 %collective-permute-start.10 = (bf16[128,384]{1,0:T(8,128)(2,1)S(1)}, bf16[128,384]{1,0:T(8,128)(2,1)S(1)}, u32[]{:S(2)}, u32[]{:S(2)}) collective-permute-start(bf16[128,384]{1,0:T(8,128)(2,1)S(1)} %shard_map.86.refs_8_), channel_id=1, source_target_pairs={{0,64},{4,68},{8,72},{12,76},{16,80},{20,84},{24,88},{28,92},{32,9... | collective-permute-start | bytes 294920 | tf_op jit(solution)/shard_map/ppermute | solution.py:544

commit v6 on v5

--- a/solution.py
+++ b/solution.py
@@ -508,11 +508,11 @@
     far1 = step(chip_gather(taken))
     near2 = step(near1)
     far2 = step(far1)
-    near2, got = lax.optimization_barrier((near2, got))
+    gates = jnp.take(gate_table, clip_steps, axis=0)
+    near2, got, gates = lax.optimization_barrier((near2, got, gates))
     near3 = step(near2)
     far3 = step(far2)
     near4 = step(core_half(near3))
-    gates = jnp.take(gate_table, clip_steps, axis=0)
     counts = (12, 4)
     far4 = lax.ppermute(core_half(far2), "seq", to_second)
     *queries, clips1, dead, sums, stats = unpack_attend(

time: 91.2 us -> 90.7 us (level)
  waiting for transfers between devices: 5.94 us -> 4.84 us
    ppermute x7, waiting for transfers between devices: 5.93 us -> 4.83 us  [step(): return lax.ppermute(block, 'seq', to_next)]
where the time goes in v6:
time: 90.7 us; the launch traced here: 90.1 us
  starting transfers between devices  54.9 us (61%)
  Pallas kernels  16 us (18%)
  blocking collectives  11.5 us (13%)
  waiting for transfers between devices  4.84 us (5%)
  local copies, waits for them, and re-layouts  2.37 us (3%)
    ppermute x7, starting transfers between devices, step(): return lax.ppermute(block, 'seq', to_next)  27.6 us
    pallas_call x8, Pallas kernels, call(): pl.pallas_call(body, grid=(1,), in_specs=list(in_specs) + [pl.BlockSpec(m...  16 us
    all_gather x4, blocking collectives, chip_gather(): return lax.all_gather(block, 'seq', axis_index_groups=chips, tiled=True)  11.5 us
    ppermute x1, starting transfers between devices, shards(): taken = lax.ppermute(given, 'seq', to_half)  11.5 us
    ppermute x1, starting transfers between devices, shards(): back = lax.ppermute(theirs, 'seq', to_half)  6.74 us
    ppermute x7, waiting for transfers between devices, step(): return lax.ppermute(block, 'seq', to_next)  4.83 us
    all_to_all x1, starting transfers between devices, shards(): lax.all_to_all(message.reshape(plane, MSG, sent_width), 'seq', split_axis...  4.03 us
    ppermute x1, starting transfers between devices, shards(): far4 = lax.ppermute(core_half(far2), 'seq', to_second)  2.78 us
  transfers between devices with their start and end apart: 12, of which 2 were waited for; matrix products, arithmetic and copies ran while one was open for 1% of the time, Pallas kernels for 12%

profile of v6, /device:TPU:1, one launch (start us, length us, event | category | flops | bytes accessed | tf_op | source)
XLA Modules:
  0.0 90.1 jit_solution(17555970034849669925)
XLA Ops:
  0.0 1.9 %shard_map.82 = (bf16[128,768]{1,0:T(8,128)(2,1)}, bf16[128,768]{1,0:T(8,128)(2,1)}) custom-call(s32[1]{0:T(128)} %bitcast.refs_0_, bf16[128,768]{1,0:T(8,128)(2,1)} %refs_1_.4, bf16[128,768]{1,0:T(8,128)(2,1)} %refs_2_.1), custom_call_target="tpu_custom_call" | custom-call | tf_op jit(solution)/shard_map/pallas_call | solution.py:370
  1.9 11.5 %collective-permute-start.3 = (bf16[128,768]{1,0:T(8,128)(2,1)}, bf16[128,768]{1,0:T(8,128)(2,1)S(1)}, u32[]{:S(2)}, u32[]{:S(2)}) collective-permute-start(bf16[128,768]{1,0:T(8,128)(2,1)} %get-tuple-element.25.refs_4_), channel_id=1, source_target_pairs={{0,64},{4,68},{8,72},{12,76},{16,80},{20,84},{24,88},{28,92},{32,9... | collective-permute-start | bytes 589832 | tf_op jit(solution)/shard_map/ppermute | solution.py:487
  13.4 2.1 %shard_map.83 = bf16[384,512]{1,0:T(8,128)(2,1)} custom-call(s32[8]{0:T(128)} %refs_1_.7, s32[1,128]{1,0:T(1,128)} %bitcast.8, s32[1,128]{1,0:T(1,128)} %bitcast.9, bf16[128,768]{1,0:T(8,128)(2,1)} %refs_3_.1, bf16[128,768]{1,0:T(8,128)(2,1)} %get-tuple-element.25.refs_4_), custom_call_target="tpu_custom_call" | custom-call | bytes 8388608 | tf_op jit(solution)/shard_map/pallas_call | solution.py:370
  15.5 3.0 %all_gather.12 = bf16[256,768]{1,0:T(8,128)(2,1)S(1)} all-gather(bf16[128,768]{1,0:T(8,128)(2,1)} %get-tuple-element.26.refs_4_), channel_id=1, replica_groups={{0,4},{8,12},{16,20},{24,28},{32,36},{40,44},{48,52},{56,60},{64,68},{7..., dimensions={0}, use_global_device_ids=true | all-gather | bytes 589824 | tf_op jit(solution)/shard_map/all_gather | solution.py:470
  18.5 5.1 %collective-permute-start = (bf16[256,768]{1,0:T(8,128)(2,1)S(1)}, bf16[256,768]{1,0:T(8,128)(2,1)S(1)}, u32[]{:S(2)}, u32[]{:S(2)}) collective-permute-start(bf16[256,768]{1,0:T(8,128)(2,1)S(1)} %all_gather.12), channel_id=1, source_target_pairs={{0,8},{4,60},{8,16},{12,4},{16,24},{20,12},{24,32},{28,20},{32,40}... | collective-permute-start | bytes 1179656 | tf_op jit(solution)/shard_map/ppermute | solution.py:467
  23.6 4.0 %all-to-all-start = ((bf16[16,24,512]{2,1,0:T(8,128)(2,1)}), bf16[16,24,512]{2,1,0:T(8,128)(2,1)S(1)}, u32[]{:S(2)}, u32[]{:S(2)}) async-start(bf16[16,24,512]{2,1,0:T(8,128)(2,1)} %bitcast.7), calls=%async_computation | async-start | bytes 786432 | tf_op jit(solution)/shard_map/all_to_all | solution.py:498
  27.6 2.9 %all_gather.13 = bf16[256,768]{1,0:T(8,128)(2,1)} all-gather(bf16[128,768]{1,0:T(8,128)(2,1)S(1)} %collective-permute-done.3.refs_5_), channel_id=1, replica_groups={{0,4},{8,12},{16,20},{24,28},{32,36},{40,44},{48,52},{56,60},{64,68},{7..., dimensions={0}, use_global_device_ids=true | all-gather | bytes 589824 | tf_op jit(solution)/shard_map/all_gather | solution.py:470
  30.5 4.8 %collective-permute-start.4 = (bf16[256,768]{1,0:T(8,128)(2,1)}, bf16[256,768]{1,0:T(8,128)(2,1)}, u32[]{:S(2)}, u32[]{:S(2)}) collective-permute-start(bf16[256,768]{1,0:T(8,128)(2,1)} %all_gather.13), channel_id=1, source_target_pairs={{0,8},{4,60},{8,16},{12,4},{16,24},{20,12},{24,32},{28,20},{32,40}... | collective-permute-start | bytes 1179656 | tf_op jit(solution)/shard_map/ppermute | solution.py:467
  35.9 3.1 %collective-permute-start.1 = (bf16[256,768]{1,0:T(8,128)(2,1)S(1)}, bf16[256,768]{1,0:T(8,128)(2,1)S(1)}, u32[]{:S(2)}, u32[]{:S(2)}) collective-permute-start(bf16[256,768]{1,0:T(8,128)(2,1)S(1)} %collective-permute-done.refs_6_), channel_id=1, source_target_pairs={{0,8},{4,60},{8,16},{12,4},{16,24},{20,12},{24,32},{28,20},{32,40}... | collective-permute-start | bytes 1179656 | tf_op jit(solution)/shard_map/ppermute | solution.py:467
  39.0 4.1 %collective-permute-done.4.refs_7_ = bf16[256,768]{1,0:T(8,128)(2,1)} collective-permute-done((bf16[256,768]{1,0:T(8,128)(2,1)}, bf16[256,768]{1,0:T(8,128)(2,1)}, u32[]{:S(2)}, u32[]{:S(2)}) %collective-permute-start.4) | collective-permute-done | bytes 393248 | tf_op jit(solution)/shard_map/ppermute | solution.py:467
  43.2 3.4 %collective-permute-start.5 = (bf16[256,768]{1,0:T(8,128)(2,1)}, bf16[256,768]{1,0:T(8,128)(2,1)S(1)}, u32[]{:S(2)}, u32[]{:S(2)}) collective-permute-start(bf16[256,768]{1,0:T(8,128)(2,1)} %collective-permute-done.4.refs_7_), channel_id=1, source_target_pairs={{0,8},{4,60},{8,16},{12,4},{16,24},{20,12},{24,32},{28,20},{32,40}... | collective-permute-start | bytes 1179656 | tf_op jit(solution)/shard_map/ppermute | solution.py:467
  48.0 3.2 %collective-permute-start.6 = (bf16[256,768]{1,0:T(8,128)(2,1)}, bf16[256,768]{1,0:T(8,128)(2,1)S(1)}, u32[]{:S(2)}, u32[]{:S(2)}) collective-permute-start(bf16[256,768]{1,0:T(8,128)(2,1)} %copy-done.2), channel_id=1, source_target_pairs={{0,8},{4,60},{8,16},{12,4},{16,24},{20,12},{24,32},{28,20},{32,40}... | collective-permute-start | bytes 1179656 | tf_op jit(solution)/shard_map/ppermute | solution.py:467
  51.2 2.3 %collective-permute-start.2 = (bf16[384,512]{1,0:T(8,128)(2,1)S(1)}, bf16[384,512]{1,0:T(8,128)(2,1)S(1)}, u32[]{:S(2)}, u32[]{:S(2)}) collective-permute-start(bf16[384,512]{1,0:T(8,128)(2,1)S(1)} %bitcast.5), channel_id=1, source_target_pairs={{0,4},{4,0},{8,12},{12,8},{16,20},{20,16},{24,28},{28,24},{32,36},... | collective-permute-start | bytes 1179656 | tf_op jit(solution)/shard_map/ppermute | solution.py:524
  53.5 4.9 %collective-permute-start.7 = (bf16[256,768]{1,0:T(8,128)(2,1)S(1)}, bf16[256,768]{1,0:T(8,128)(2,1)S(1)}, u32[]{:S(2)}, u32[]{:S(2)}) collective-permute-start(bf16[256,768]{1,0:T(8,128)(2,1)S(1)} %collective-permute-done.5.refs_9_), channel_id=1, source_target_pairs={{0,8},{4,60},{8,16},{12,4},{16,24},{20,12},{24,32},{28,20},{32,40}... | collective-permute-start | bytes 1179656 | tf_op jit(solution)/shard_map/ppermute | solution.py:467
  58.4 2.8 %collective-permute-start.9 = (bf16[128,768]{1,0:T(8,128)(2,1)S(1)}, bf16[128,768]{1,0:T(8,128)(2,1)S(1)}, u32[]{:S(2)}, u32[]{:S(2)}) collective-permute-start(bf16[128,768]{1,0:T(8,128)(2,1)S(1)} %constant_dynamic-slice_fusion), channel_id=1, source_target_pairs={{0,16},{4,52},{8,24},{12,60},{16,32},{20,4},{24,40},{28,12},{32,48... | collective-permute-start | bytes 589832 | tf_op jit(solution)/shard_map/ppermute | solution.py:517
  61.2 3.3 %collective-permute-start.8 = (bf16[128,768]{1,0:T(8,128)(2,1)S(1)}, bf16[128,768]{1,0:T(8,128)(2,1)S(1)}, u32[]{:S(2)}, u32[]{:S(2)}) collective-permute-start(bf16[128,768]{1,0:T(8,128)(2,1)S(1)} %constant_dynamic-slice_fusion.1), channel_id=1, source_target_pairs={{0,8},{4,60},{8,16},{12,4},{16,24},{20,12},{24,32},{28,20},{32,40}... | collective-permute-start | bytes 589832 | tf_op jit(solution)/shard_map/ppermute | solution.py:467
  64.6 1.0 %copy-done.3 = bf16[256,768]{1,0:T(8,128)(2,1)S(1)} copy-done((bf16[256,768]{1,0:T(8,128)(2,1)S(1)}, bf16[256,768]{1,0:T(8,128)(2,1)}, u32[]{:S(2)}) %copy-start.3) | copy-done | bytes 393240
  65.6 6.0 %shard_map.84 = (bf16[256,384]{1,0:T(8,128)(2,1)S(1)}, bf16[256,384]{1,0:T(8,128)(2,1)S(1)}, bf16[512,128]{1,0:T(8,128)(2,1)S(1)}, bf16[512,128]{1,0:T(8,128)(2,...) custom-call(s32[1]{0:T(128)} %bitcast.refs_0_, s32[8]{0:T(128)S(1)} %copy-done.4, bf16[384,512]{1,0:T(8,128)(2,1)S(1)} %bitcast.6, ...), custom_call_target="tpu_custom_call" | custom-call | tf_op jit(solution)/shard_map/pallas_call | solution.py:370
  71.6 1.8 %shard_map.85 = (f32[128,384]{1,0:T(8,128)S(1)}, f32[128,128]{1,0:T(8,128)S(1)}, bf16[128,512]{1,0:T(8,128)(2,1)S(1)}) custom-call(bf16[512,128]{1,0:T(8,128)(2,1)S(1)} %get-tuple-element.31.refs_0_, bf16[256,384]{1,0:T(8,128)(2,1)S(1)} %get-tuple-element.36.refs_1_, bf16[256,768]{1,0:T(8,128)(2,1)S(1)} %collective-permute-done.7.refs_2_, ...), custom_call_target="tpu_custom_call" | custom-call | tf_op jit(solution)/shard_map/pallas_call | solution.py:370
  73.5 3.4 %all_gather.14.refs_4_ = bf16[256,512]{1,0:T(8,128)(2,1)S(1)} all-gather(bf16[128,512]{1,0:T(8,128)(2,1)S(1)} %get-tuple-element.39), channel_id=1, replica_groups={{0,4},{8,12},{16,20},{24,28},{32,36},{40,44},{48,52},{56,60},{64,68},{7..., dimensions={0}, use_global_device_ids=true | all-gather | bytes 393216 | tf_op jit(solution)/shard_map/all_gather | solution.py:470
  77.7 6.7 %collective-permute-start.10 = (bf16[128,384]{1,0:T(8,128)(2,1)S(1)}, bf16[128,384]{1,0:T(8,128)(2,1)S(1)}, u32[]{:S(2)}, u32[]{:S(2)}) collective-permute-start(bf16[128,384]{1,0:T(8,128)(2,1)S(1)} %shard_map.86.refs_8_), channel_id=1, source_target_pairs={{0,64},{4,68},{8,72},{12,76},{16,80},{20,84},{24,88},{28,92},{32,9... | collective-permute-start | bytes 294920 | tf_op jit(solution)/shard_map/ppermute | solution.py:544
  84.4 1.8 %shard_map.87 = (f32[128,384]{1,0:T(8,128)S(1)}, f32[128,128]{1,0:T(8,128)S(1)}, bf16[128,512]{1,0:T(8,128)(2,1)S(1)}) custom-call(bf16[512,128]{1,0:T(8,128)(2,1)S(1)} %get-tuple-element.31.refs_0_, bf16[256,384]{1,0:T(8,128)(2,1)S(1)} %get-tuple-element.32.refs_1_, bf16[256,768]{1,0:T(8,128)(2,1)S(1)} %collective-permute-done.7.refs_2_, ...), custom_call_target="tpu_custom_call" | custom-call | tf_op jit(solution)/shard_map/pallas_call | solution.py:370
  86.3 2.3 %all_gather.15.refs_4_ = bf16[256,512]{1,0:T(8,128)(2,1)S(1)} all-gather(bf16[128,512]{1,0:T(8,128)(2,1)S(1)} %get-tuple-element.42), channel_id=1, replica_groups={{0,4},{8,12},{16,20},{24,28},{32,36},{40,44},{48,52},{56,60},{64,68},{7..., dimensions={0}, use_global_device_ids=true | all-gather | bytes 393216 | tf_op jit(solution)/shard_map/all_gather | solution.py:470
  88.5 0.8 shard_map.88.refs_1_
  (31 shorter events, 3.7 us)
Async XLA Ops:
  0.0 35.3 %copy-start = (bf16[1000,768]{1,0:T(8,128)(2,1)S(1)}, bf16[1000,768]{1,0:T(8,128)(2,1)}, u32[]{:S(2)}) copy-start(bf16[1000,768]{1,0:T(8,128)(2,1)} %param.15) | copy-start | bytes 4608004
  0.0 35.3 %copy-start.5 = (s32[8]{0:T(128)S(1)}, s32[8]{0:T(128)}, u32[]{:S(2)}) copy-start(s32[8]{0:T(128)} %param.14) | copy-start | bytes 100
  1.9 25.7 %collective-permute-start.3 = (bf16[128,768]{1,0:T(8,128)(2,1)}, bf16[128,768]{1,0:T(8,128)(2,1)S(1)}, u32[]{:S(2)}, u32[]{:S(2)}) collective-permute-start(bf16[128,768]{1,0:T(8,128)(2,1)} %get-tuple-element.25.refs_4_), channel_id=1, source_target_pairs={{0,64},{4,68},{8,72},{12,76},{16,80},{20,84},{24,88},{28,92},{32,9... | collective-permute-start | bytes 589832 | tf_op jit(solution)/shard_map/ppermute | solution.py:487
  15.5 49.1 %copy-start.1 = (bf16[128,768]{1,0:T(8,128)(2,1)S(1)}, bf16[128,768]{1,0:T(8,128)(2,1)}, u32[]{:S(2)}) copy-start(bf16[128,768]{1,0:T(8,128)(2,1)} %get-tuple-element.26.refs_4_) | copy-start | bytes 589828
  15.5 49.1 %copy-start.4 = (s32[8]{0:T(128)S(1)}, s32[8]{0:T(128)}, u32[]{:S(2)}) copy-start(s32[8]{0:T(128)} %refs_1_.7) | copy-start | bytes 100
  18.5 17.4 %collective-permute-start = (bf16[256,768]{1,0:T(8,128)(2,1)S(1)}, bf16[256,768]{1,0:T(8,128)(2,1)S(1)}, u32[]{:S(2)}, u32[]{:S(2)}) collective-permute-start(bf16[256,768]{1,0:T(8,128)(2,1)S(1)} %all_gather.12), channel_id=1, source_target_pairs={{0,8},{4,60},{8,16},{12,4},{16,24},{20,12},{24,32},{28,20},{32,40}... | collective-permute-start | bytes 1179656 | tf_op jit(solution)/shard_map/ppermute | solution.py:467
  23.6 23.0 %all-to-all-start = ((bf16[16,24,512]{2,1,0:T(8,128)(2,1)}), bf16[16,24,512]{2,1,0:T(8,128)(2,1)S(1)}, u32[]{:S(2)}, u32[]{:S(2)}) async-start(bf16[16,24,512]{2,1,0:T(8,128)(2,1)} %bitcast.7), calls=%async_computation | async-start | bytes 786432 | tf_op jit(solution)/shard_map/all_to_all | solution.py:498
  30.5 12.7 %collective-permute-start.4 = (bf16[256,768]{1,0:T(8,128)(2,1)}, bf16[256,768]{1,0:T(8,128)(2,1)}, u32[]{:S(2)}, u32[]{:S(2)}) collective-permute-start(bf16[256,768]{1,0:T(8,128)(2,1)} %all_gather.13), channel_id=1, source_target_pairs={{0,8},{4,60},{8,16},{12,4},{16,24},{20,12},{24,32},{28,20},{32,40}... | collective-permute-start | bytes 1179656 | tf_op jit(solution)/shard_map/ppermute | solution.py:467
  35.9 11.4 %collective-permute-start.1 = (bf16[256,768]{1,0:T(8,128)(2,1)S(1)}, bf16[256,768]{1,0:T(8,128)(2,1)S(1)}, u32[]{:S(2)}, u32[]{:S(2)}) collective-permute-start(bf16[256,768]{1,0:T(8,128)(2,1)S(1)} %collective-permute-done.refs_6_), channel_id=1, source_target_pairs={{0,8},{4,60},{8,16},{12,4},{16,24},{20,12},{24,32},{28,20},{32,40}... | collective-permute-start | bytes 1179656 | tf_op jit(solution)/shard_map/ppermute | solution.py:467
  43.2 10.3 %collective-permute-start.5 = (bf16[256,768]{1,0:T(8,128)(2,1)}, bf16[256,768]{1,0:T(8,128)(2,1)S(1)}, u32[]{:S(2)}, u32[]{:S(2)}) collective-permute-start(bf16[256,768]{1,0:T(8,128)(2,1)} %collective-permute-done.4.refs_7_), channel_id=1, source_target_pairs={{0,8},{4,60},{8,16},{12,4},{16,24},{20,12},{24,32},{28,20},{32,40}... | collective-permute-start | bytes 1179656 | tf_op jit(solution)/shard_map/ppermute | solution.py:467
  47.3 0.8 copy-start.2
  48.0 13.1 %collective-permute-start.6 = (bf16[256,768]{1,0:T(8,128)(2,1)}, bf16[256,768]{1,0:T(8,128)(2,1)S(1)}, u32[]{:S(2)}, u32[]{:S(2)}) collective-permute-start(bf16[256,768]{1,0:T(8,128)(2,1)} %copy-done.2), channel_id=1, source_target_pairs={{0,8},{4,60},{8,16},{12,4},{16,24},{20,12},{24,32},{28,20},{32,40}... | collective-permute-start | bytes 1179656 | tf_op jit(solution)/shard_map/ppermute | solution.py:467
  51.2 13.4 %collective-permute-start.2 = (bf16[384,512]{1,0:T(8,128)(2,1)S(1)}, bf16[384,512]{1,0:T(8,128)(2,1)S(1)}, u32[]{:S(2)}, u32[]{:S(2)}) collective-permute-start(bf16[384,512]{1,0:T(8,128)(2,1)S(1)} %bitcast.5), channel_id=1, source_target_pairs={{0,4},{4,0},{8,12},{12,8},{16,20},{20,16},{24,28},{28,24},{32,36},... | collective-permute-start | bytes 1179656 | tf_op jit(solution)/shard_map/ppermute | solution.py:524
  53.5 18.1 %collective-permute-start.7 = (bf16[256,768]{1,0:T(8,128)(2,1)S(1)}, bf16[256,768]{1,0:T(8,128)(2,1)S(1)}, u32[]{:S(2)}, u32[]{:S(2)}) collective-permute-start(bf16[256,768]{1,0:T(8,128)(2,1)S(1)} %collective-permute-done.5.refs_9_), channel_id=1, source_target_pairs={{0,8},{4,60},{8,16},{12,4},{16,24},{20,12},{24,32},{28,20},{32,40}... | collective-permute-start | bytes 1179656 | tf_op jit(solution)/shard_map/ppermute | solution.py:467
  58.4 13.2 %collective-permute-start.9 = (bf16[128,768]{1,0:T(8,128)(2,1)S(1)}, bf16[128,768]{1,0:T(8,128)(2,1)S(1)}, u32[]{:S(2)}, u32[]{:S(2)}) collective-permute-start(bf16[128,768]{1,0:T(8,128)(2,1)S(1)} %constant_dynamic-slice_fusion), channel_id=1, source_target_pairs={{0,16},{4,52},{8,24},{12,60},{16,32},{20,4},{24,40},{28,12},{32,48... | collective-permute-start | bytes 589832 | tf_op jit(solution)/shard_map/ppermute | solution.py:517
  61.2 10.4 %collective-permute-start.8 = (bf16[128,768]{1,0:T(8,128)(2,1)S(1)}, bf16[128,768]{1,0:T(8,128)(2,1)S(1)}, u32[]{:S(2)}, u32[]{:S(2)}) collective-permute-start(bf16[128,768]{1,0:T(8,128)(2,1)S(1)} %constant_dynamic-slice_fusion.1), channel_id=1, source_target_pairs={{0,8},{4,60},{8,16},{12,4},{16,24},{20,12},{24,32},{28,20},{32,40}... | collective-permute-start | bytes 589832 | tf_op jit(solution)/shard_map/ppermute | solution.py:467
  64.6 1.0 %copy-start.3 = (bf16[256,768]{1,0:T(8,128)(2,1)S(1)}, bf16[256,768]{1,0:T(8,128)(2,1)}, u32[]{:S(2)}) copy-start(bf16[256,768]{1,0:T(8,128)(2,1)} %copy-done.2) | copy-start | bytes 1179652
  77.7 11.7 %collective-permute-start.10 = (bf16[128,384]{1,0:T(8,128)(2,1)S(1)}, bf16[128,384]{1,0:T(8,128)(2,1)S(1)}, u32[]{:S(2)}, u32[]{:S(2)}) collective-permute-start(bf16[128,384]{1,0:T(8,128)(2,1)S(1)} %shard_map.86.refs_8_), channel_id=1, source_target_pairs={{0,64},{4,68},{8,72},{12,76},{16,80},{20,84},{24,88},{28,92},{32,9... | collective-permute-start | bytes 294920 | tf_op jit(solution)/shard_map/ppermute | solution.py:544
